TPU v7x, 32 devices: a whole 2x2x4 slice. The times are simulated.
32 devices in a mesh: gx: 2 (over x), gy: 4 (over y, core), gz: 4 (over z).
Axes of the slice: x: 2, y: 2, z: 4, core: 2. Of those that a mesh axis runs over, the one named last changes fastest.
Arguments:
- start_block: float32 [16, 8, 64, 512], P(None, 'gx', 'gy', 'gz')
- basis: bfloat16 [256, 8, 64, 512], P(None, 'gx', 'gy', 'gz')
- trans_x: float32 [8, 64, 512], P('gx', 'gy', 'gz'), may hold values from 0.05 to 1
- trans_y: float32 [8, 64, 512], P('gx', 'gy', 'gz'), may hold values from 0.05 to 1
- trans_z: float32 [8, 64, 512], P('gx', 'gy', 'gz'), may hold values from 0.05 to 1
- pore_volume: float32 [8, 64, 512], P('gx', 'gy', 'gz'), may hold values from 0.5 to 2
- shift_table: float32 [16], replicated, may hold values from 0.5 to 4
- shift_index: int32 [1], replicated, may hold values from 0 to 15
- fault_send: int32 [32, 32, 32], P(('gx', 'gy', 'gz')), may hold values from 0 to 8191
- fault_recv: int32 [32, 32, 32], P(('gx', 'gy', 'gz')), may hold values from 0 to 8191
- fault_trans: float32 [32, 32, 32], P(('gx', 'gy', 'gz')), may hold values from 0.05 to 0.5
- well_cells: int32 [64], replicated, may hold values from 0 to 262143
Outputs:
- new_block: float32 [16, 8, 64, 512], P(None, 'gx', 'gy', 'gz')
- first_coeffs: float32 [256, 16], replicated
- coeffs: float32 [256, 16], replicated
- well_resp: float32 [64, 16], replicated
Inputs may be any that keep to these rules, and one draw needn't show every extreme that they name: fault_send[d, p, s] is a local cell number on device d; the value of that cell feeds a connection into device p. fault_recv[d, p, s] is a local cell number on device d. `well_cells`: flat cell index, last dimension fastest.
All inputs are finite; a program needn't handle non-finite values.
Results may differ from a plain program's by a relative error of at most 0.0065.
Values sent between devices are 32-bit elements; how exact they have to be, the bound alone decides.
No kernel may reach another device: no remote copies, remote signals or barrier semaphores. Data moves between devices by JAX's collectives and lax.ppermute only.
A program may use at most 128 MiB of HBM per device.

v0:
```python
import functools
import math

import jax
import jax.numpy as jnp
from jax import lax
from jax.experimental import pallas as pl
from jax.experimental.pallas import tpu as pltpu
from jax.sharding import PartitionSpec as P

TERMS = 8
AXES = ("gx", "gy", "gz")
LANES = 128
BF16 = jnp.bfloat16
F32 = jnp.float32


def swap_pairs(size, odd):
    pairs = []
    for low in range(1 if odd else 0, size - 1, 2):
        pairs += [(low, low + 1), (low + 1, low)]
    return pairs


def swap(value, axis, odd):
    pairs = swap_pairs(lax.axis_size(axis), odd)
    return lax.ppermute(value, axis, pairs) if pairs else value


def swap_rest(value, first, axis):
    size = lax.axis_size(axis)
    if size == 4:
        return [first, lax.ppermute(first, axis, [(i, i ^ 2) for i in range(size)])]
    return [first, swap(value, axis, True)] if size > 2 else [first]


def from_behind(value, axis):
    size = lax.axis_size(axis)
    return lax.ppermute(value, axis, [(i, i + 1) for i in range(size - 1)])


def exchange(value):
    return lax.all_to_all(value, AXES, split_axis=0, concat_axis=0, tiled=True)


def regroup(tile, rows, slots):
    groups = LANES // slots
    columns = tile.shape[0]
    row_group = lax.broadcasted_iota(jnp.int32, tile.shape, 0) // rows
    lane_group = lax.broadcasted_iota(jnp.int32, tile.shape, 1) // slots
    ahead = lax.rem(lane_group - row_group + groups, groups)
    result = tile
    for k in range(1, groups):
        moved = pltpu.roll(tile, k * slots, 1)
        moved = pltpu.roll(moved, columns - k * rows, 0)
        result = jnp.where(ahead == k, moved, result)
    return result


def split_two(value):
    high = value.astype(BF16)
    low = (value - high.astype(F32)).astype(BF16)
    return high, low


def nt_dot(left, right):
    return lax.dot_general(left, right, (((1,), (1,)), ((), ())), preferred_element_type=F32)


def emit_faces(direction_ref, par_ref, faces_out, dims):
    columns, size_x, size_y, size_z, slots = dims
    lines = size_x * size_y
    x_a, x_b, y_ab, z_ab = faces_out
    even = [par_ref[i] == 0 for i in range(3)]
    field = direction_ref[...]
    first_x, last_x = field[:, :size_y, :], field[:, lines - size_y :, :]
    x_a[...] = jnp.where(even[0], last_x, first_x)
    if x_b is not None:
        x_b[...] = jnp.where(even[0], first_x, last_x)
    for i in range(size_x):
        first_y = direction_ref[:, i * size_y, :]
        last_y = direction_ref[:, (i + 1) * size_y - 1, :]
        y_ab[i] = jnp.where(even[1], last_y, first_y)
        y_ab[size_x + i] = jnp.where(even[1], first_y, last_y)
    both = jnp.concatenate(split_two(field.reshape(columns * lines, size_z)), axis=1)
    row = lax.broadcasted_iota(jnp.int32, (8, size_z), 0)
    lane = lax.broadcasted_iota(jnp.int32, (8, size_z), 1)
    pick = ((row == 0) & (lane == size_z - 1)) | ((row == 1) & (lane == 0))
    pick = jnp.where(pick, 1.0, 0.0).astype(BF16)
    ends = nt_dot(jnp.concatenate([pick, pick], axis=1), both)
    last_z, first_z = ends[0:1, :], ends[1:2, :]
    z_ab[0:1, :] = jnp.where(even[2], last_z, first_z)
    z_ab[1:2, :] = jnp.where(even[2], first_z, last_z)


def gather_kernel(dims, early, *refs):
    extra, goes = early
    direction_ref, send_ref = refs[:2]
    faults_out = refs[-1]
    columns, size_x, size_y, size_z, slots = dims
    lines = size_x * size_y
    rows = columns * slots // LANES
    field = direction_ref[...]
    both = jnp.concatenate(split_two(field.reshape(columns * lines, size_z)), axis=1)
    if goes:
        for i in range(send_ref.shape[1] // slots):
            at = i * (rows + extra) + rows
            source = refs[2][...] if goes == "sums" else refs[2][i * extra : (i + 1) * extra, :]
            faults_out[at : at + extra, :] = source
    total = send_ref.shape[1]
    width = min(256, total)
    for start in range(0, total, width):
        cell = send_ref[:, start : start + width]
        lane_of = jnp.broadcast_to(cell % size_z, (size_z, width))
        hot = lane_of == lax.broadcasted_iota(jnp.int32, (size_z, width), 0)
        hot = jnp.where(hot, 1.0, 0.0).astype(BF16)
        found = jnp.dot(both, jnp.concatenate([hot, hot], axis=0), preferred_element_type=F32)
        line_of = jnp.broadcast_to(cell // size_z, (lines, width))
        mask = line_of == lax.broadcasted_iota(jnp.int32, (lines, width), 0)
        found = jnp.where(mask[None], found.reshape(columns, lines, width), 0.0)
        values = jnp.sum(found, axis=1)
        for j in range(0, width, LANES):
            tile = regroup(values[:, j : j + LANES], rows, slots)
            device = (start + j) // slots
            if not goes:
                faults_out[device * rows : device * rows + columns, :] = tile
                continue
            for i in range(LANES // slots):
                at = (device + i) * (rows + extra)
                faults_out[at : at + rows, :] = tile[i * rows : (i + 1) * rows]


def start_copies(pairs, sem):
    copies = [pltpu.make_async_copy(source, target, sem.at[i]) for i, (source, target) in enumerate(pairs)]
    for copy in copies:
        copy.start()
    return copies


def edges_kernel(dims, *refs):
    columns, size_x, size_y, size_z, slots = dims
    ex_out, ey_out, ez_out = refs[6:9]
    tables_out, held, sem = refs[9:12], refs[12:18], refs[18]
    copies = start_copies(zip(refs[:6], held), sem)
    for copy in copies:
        copy.wait()
    tx, ty, tz = held[:3]
    lines = size_x * size_y
    ex_out[...] = tx[lines - size_y :, :]
    for i in range(size_x):
        ey_out[i : i + 1, :] = ty[(i + 1) * size_y - 1 : (i + 1) * size_y, :]
    ez_out[...] = tz[...].T[size_z - 1 : size_z, :]
    for table, out in zip(held[3:], tables_out):
        value = table[0]
        out[...] = jnp.concatenate([value[i : i + 1, :] for i in range(value.shape[0])], axis=1)


def setup_kernel(dims, has_b, *refs):
    (par_ref, shifts_ref, which_ref, ex_ref, ey_ref, ez_ref, recv_ref, weight_ref) = refs[:8]
    sources = refs[8:13]
    ops_ref, residual_ref, direction_ref = refs[13:16]
    faces_out = unpack_faces(refs[16 : 19 + has_b[0]], has_b)
    held, sem = refs[19 + has_b[0] : -1], refs[-1]
    tx_ref, ty_ref, tz_ref, pore_ref = held
    copies = start_copies(zip(sources, held + (residual_ref,)), sem)
    columns, size_x, size_y, size_z, slots = dims
    lines = size_x * size_y
    line = lax.broadcasted_iota(jnp.int32, (lines, size_z), 0)
    lane = lax.broadcasted_iota(jnp.int32, (lines, size_z), 1)
    last = [par_ref[3 + i] == 1 for i in range(3)]
    in_y = line % size_y
    for copy in copies[:4]:
        copy.wait()
    upper_x = jnp.where((line >= lines - size_y) & last[0], 0.0, tx_ref[...])
    upper_y = jnp.where((in_y == size_y - 1) & last[1], 0.0, ty_ref[...])
    upper_z = jnp.where((lane == size_z - 1) & last[2], 0.0, tz_ref[...])
    lower_x = jnp.concatenate([ex_ref[...], upper_x[: lines - size_y]], axis=0)
    edge_y = jnp.concatenate(
        [jnp.broadcast_to(ey_ref[i : i + 1, :], (size_y, size_z)) for i in range(size_x)], axis=0
    )
    lower_y = jnp.where(in_y == 0, edge_y, pltpu.roll(upper_y, 1, 0))
    lower_z = jnp.where(lane == 0, jnp.broadcast_to(ez_ref[...], (8, lines)).T[:, 0:1], pltpu.roll(upper_z, 1, 1))
    total = recv_ref.shape[1]
    cell = recv_ref[...]
    hot_line = jnp.broadcast_to(cell // size_z, (lines, total)) == lax.broadcasted_iota(
        jnp.int32, (lines, total), 0
    )
    hot_lane = jnp.broadcast_to(cell % size_z, (size_z, total)) == lax.broadcasted_iota(
        jnp.int32, (size_z, total), 0
    )
    weight = weight_ref[...]
    high = weight.astype(BF16).astype(F32)
    middle = (weight - high).astype(BF16).astype(F32)
    low = weight - high - middle
    parts = [jnp.where(hot_line, part, 0.0).astype(BF16) for part in (high, middle, low)]
    summed = nt_dot(jnp.concatenate(parts, axis=0), jnp.where(hot_lane, 1.0, 0.0).astype(BF16))
    fault_diag = summed[:lines] + summed[lines : 2 * lines] + summed[2 * lines :]
    shift = shifts_ref[which_ref[0]]
    diagonal = (
        upper_x + lower_x + upper_y + lower_y + upper_z + lower_z + shift * pore_ref[...] + fault_diag
    )
    inverse = 1.0 / diagonal
    for i, value in enumerate((upper_x, lower_x, upper_y, lower_y, upper_z, lower_z, diagonal, inverse)):
        ops_ref[i] = value
    copies[4].wait()
    for c in range(columns):
        direction_ref[c] = residual_ref[c] * inverse
    emit_faces(direction_ref, par_ref, faces_out, dims)


def unpack_faces(refs, has_b):
    refs = list(refs)
    x_a = refs.pop(0)
    x_b = refs.pop(0) if has_b[0] else None
    return x_a, x_b, refs.pop(0), refs.pop(0)


def stencil_kernel(dims, has_b, *refs):
    refs = list(refs)
    columns, size_x, size_y, size_z, slots = dims
    par_ref, ops_ref, residual_ref, direction_ref = refs[:4]
    refs = refs[4:]
    xa_ref = refs.pop(0)
    xb_ref = refs.pop(0) if has_b[0] else xa_ref
    ya_ref = refs.pop(0)
    yb_ref = refs.pop(0) if has_b[1] else ya_ref
    y_b_at = size_x if has_b[1] else 0
    za_ref = refs.pop(0)
    zb_ref = refs.pop(0) if has_b[2] else za_ref
    (residual_out,) = refs
    lines = size_x * size_y
    even = [par_ref[i] == 0 for i in range(3)]
    z_a, z_b = za_ref[0:1, :], zb_ref[1:2, :] if has_b[2] else za_ref[0:1, :]
    z_rows = jnp.concatenate(
        [jnp.where(even[2], z_b, z_a), jnp.where(even[2], z_a, z_b), jnp.zeros((6, columns * lines), F32)],
        axis=0,
    )
    z_cols = z_rows.T
    in_y = lax.broadcasted_iota(jnp.int32, (lines, size_z), 0) % size_y
    lane = lax.broadcasted_iota(jnp.int32, (lines, size_z), 1)

    def rows_of(ref, at, c):
        return jnp.concatenate(
            [jnp.broadcast_to(ref[at + i, c : c + 1, :], (size_y, size_z)) for i in range(size_x)], axis=0
        )

    for c in range(columns):
        value = direction_ref[c]
        x_low = jnp.where(even[0], xb_ref[c], xa_ref[c])
        x_high = jnp.where(even[0], xa_ref[c], xb_ref[c])
        y_a, y_b = rows_of(ya_ref, 0, c), rows_of(yb_ref, y_b_at, c)
        y_low = jnp.where(even[1], y_b, y_a)
        y_high = jnp.where(even[1], y_a, y_b)
        z_low = z_cols[c * lines : (c + 1) * lines, 0:1]
        z_high = z_cols[c * lines : (c + 1) * lines, 1:2]
        beside = ops_ref[0] * jnp.concatenate([value[size_y:], x_high], axis=0)
        beside += ops_ref[1] * jnp.concatenate([x_low, value[: lines - size_y]], axis=0)
        beside += ops_ref[2] * jnp.where(in_y == size_y - 1, y_high, pltpu.roll(value, lines - 1, 0))
        beside += ops_ref[3] * jnp.where(in_y == 0, y_low, pltpu.roll(value, 1, 0))
        beside += ops_ref[4] * jnp.where(lane == size_z - 1, z_high, pltpu.roll(value, size_z - 1, 1))
        beside += ops_ref[5] * jnp.where(lane == 0, z_low, pltpu.roll(value, 1, 1))
        residual_out[c] = residual_ref[c] - (ops_ref[6] * value - beside)


def update_kernel(dims, has_b, keep, gain, first_round, last_round, early, *refs):
    refs = list(refs)
    columns, size_x, size_y, size_z, slots = dims
    extra, comes = early
    par_ref, ops_ref, residual_ref, direction_ref, recv_ref, weight_ref, arrived_ref = refs[:7]
    refs = refs[7:]
    solution_ref = direction_ref if first_round else refs.pop(0)
    if last_round:
        well_ref, basis_source, sums_out, flat_out, landed_ref, solution_out, basis_ref, sem = refs
        (basis_copy,) = start_copies([(basis_source, basis_ref)], sem)
    else:
        landed_ref = refs.pop()
        solution_out = refs.pop(0)
    table_out = refs.pop(0) if comes else None
    if not last_round:
        residual_out, direction_out = refs[:2]
        faces_out = unpack_faces(refs[2:], has_b)
    lines = size_x * size_y
    rows = columns * slots // LANES
    total = recv_ref.shape[1]
    cell = recv_ref[...]
    hot_line = jnp.broadcast_to(cell // size_z, (lines, total)) == lax.broadcasted_iota(
        jnp.int32, (lines, total), 0
    )
    hot_lane = jnp.broadcast_to(cell % size_z, (size_z, total)) == lax.broadcasted_iota(
        jnp.int32, (size_z, total), 0
    )
    hot_line = jnp.where(hot_line, 1.0, 0.0).astype(BF16)
    hot_lane = jnp.where(hot_lane, 1.0, 0.0).astype(BF16)
    tiles = []
    devices = total // slots
    if comes:
        per_device = rows + extra
        for i in range(devices):
            landed_ref[i * rows : (i + 1) * rows, :] = arrived_ref[i * per_device : i * per_device + rows, :]
        source_ref = landed_ref
    else:
        source_ref = arrived_ref
    for j in range(total // LANES):
        tiles.append(regroup(source_ref[j * columns : (j + 1) * columns, :], rows, slots))
    if comes == "parts":
        added = arrived_ref[rows : rows + extra, :]
        for i in range(1, devices):
            at = i * per_device + rows
            added = added + arrived_ref[at : at + extra, :]
        table_out[...] = added
    if comes == "sums":
        for i in range(devices):
            at = i * per_device + rows
            table_out[i * extra : (i + 1) * extra, :] = arrived_ref[at : at + extra, :]
    weighted = (jnp.concatenate(tiles, axis=1) * weight_ref[...]).astype(BF16)
    spread = weighted[:, None, :] * hot_line[None, :, :]
    landed_ref[...] = nt_dot(spread.reshape(columns * lines, total), hot_lane)
    for c in range(columns):
        left = residual_ref[c] + landed_ref[c * lines : (c + 1) * lines, :]
        after = keep * direction_ref[c] + gain * (left * ops_ref[7])
        solution_out[c] = solution_ref[c] + after
        if not last_round:
            residual_out[c] = left
            direction_out[c] = after
    if not last_round:
        emit_faces(direction_out, par_ref, faces_out, dims)
    else:
        basis_copy.wait()
        sums_of(dims, solution_out, basis_ref, well_ref, flat_out, sums_out)


def basis_kernel(dims, well_ref, source_ref, parts_out, flat_target, basis_ref, flat_out, hot_ref, sem, out_sem):
    columns, size_x, size_y, size_z, slots = dims
    lines = size_x * size_y
    count = basis_ref.shape[0]
    wells = well_ref.shape[1]
    side = 16
    groups = [pl.ds(first, side) for first in range(0, count, side)]
    copies = start_copies([(source_ref.at[g], basis_ref.at[g]) for g in groups], sem)
    row = lax.broadcasted_iota(jnp.int32, (side * side, side * side), 0)
    lane = lax.broadcasted_iota(jnp.int32, (side * side, side * side), 1)
    turn = jnp.where((row % side == lane // side) & (row // side == lane % side), 1.0, 0.0).astype(BF16)
    stores = []
    for index, first in enumerate(range(0, count, side)):
        copies[index].wait()
        for begin in range(0, lines, side):
            tile = basis_ref[first : first + side, begin : begin + side, :].reshape(side * side, size_z)
            tile = jnp.dot(turn, tile, preferred_element_type=F32).astype(BF16)
            for i in range(side):
                lanes = slice((begin + i) * size_z, (begin + i + 1) * size_z)
                flat_out[first : first + side, lanes] = tile[i * side : (i + 1) * side, :]
        stores.append(
            pltpu.make_async_copy(
                flat_out.at[groups[index]], flat_target.at[groups[index]], out_sem.at[index]
            )
        )
        stores[-1].start()
    cell = well_ref[...]
    lane_of = jnp.broadcast_to(lax.rem(cell + size_z, size_z), (size_z, wells))
    lane_of = lane_of == lax.broadcasted_iota(jnp.int32, (size_z, wells), 0)
    line_of = jnp.broadcast_to(jnp.where(cell < 0, -1, cell // size_z), (size_z, wells))
    for line in range(lines):
        hot = jnp.where(lane_of & (line_of == line), 1.0, 0.0)
        hot_ref[line * size_z : (line + 1) * size_z, :] = hot.astype(BF16)
    flat = flat_out[...]
    gram = nt_dot(flat, flat)
    at_wells = jnp.dot(flat, hot_ref[...], preferred_element_type=F32)
    parts_out[...] = jnp.zeros(parts_out.shape, F32)
    blocks = count // LANES
    at = 0
    for i in range(blocks):
        for j in range(i, blocks):
            parts_out[at : at + LANES, :] = gram[i * LANES : (i + 1) * LANES, j * LANES : (j + 1) * LANES]
            at += LANES
    beside = LANES // wells
    for i in range(blocks):
        place = at + i // beside * LANES
        lanes = slice(i % beside * wells, (i % beside + 1) * wells)
        parts_out[place : place + LANES, lanes] = at_wells[i * LANES : (i + 1) * LANES, :]
    for store in stores:
        store.wait()


def split_three(value):
    high = value.astype(BF16)
    left = value - high.astype(F32)
    middle = left.astype(BF16)
    return high, middle, (left - middle.astype(F32)).astype(BF16)


def sums_of(dims, solution_ref, basis_ref, well_ref, flat_out, sums_out):
    columns, size_x, size_y, size_z, slots = dims
    lines = size_x * size_y
    count = basis_ref.shape[0]
    wells = well_ref.shape[1]
    for line in range(lines):
        flat_out[:, line * size_z : (line + 1) * size_z] = solution_ref[:, line, :]
    parts = jnp.concatenate(split_three(flat_out[...]), axis=0)
    with_basis = nt_dot(parts, basis_ref[...])
    with_self = nt_dot(parts, parts)
    sums_out[...] = jnp.zeros(sums_out.shape, F32)
    blocks = count // LANES
    first = with_basis[:columns]
    beyond = with_basis[columns : 2 * columns] + with_basis[2 * columns :]
    for i in range(blocks):
        lanes = slice(i * LANES, (i + 1) * LANES)
        sums_out[i * columns : (i + 1) * columns, :] = first[:, lanes]
        sums_out[(blocks + i) * columns : (blocks + i + 1) * columns, :] = beyond[:, lanes]
    rows = with_self[:columns] + with_self[columns : 2 * columns] + with_self[2 * columns :]
    square = rows[:, :columns] + rows[:, columns : 2 * columns] + rows[:, 2 * columns :]
    at = 2 * blocks * columns
    sums_out[at : at + columns, :columns] = square
    both = jnp.concatenate(split_two(solution_ref[...].reshape(columns * lines, size_z)), axis=1)
    cell = well_ref[...]
    lane_of = jnp.broadcast_to(lax.rem(cell + size_z, size_z), (size_z, wells))
    hot = lane_of == lax.broadcasted_iota(jnp.int32, (size_z, wells), 0)
    hot = jnp.where(hot, 1.0, 0.0).astype(BF16)
    found = jnp.dot(both, jnp.concatenate([hot, hot], axis=0), preferred_element_type=F32)
    line_of = jnp.broadcast_to(jnp.where(cell < 0, -1, cell // size_z), (lines, wells))
    mask = line_of == lax.broadcasted_iota(jnp.int32, (lines, wells), 0)
    found = jnp.where(mask[None], found.reshape(columns, lines, wells), 0.0)
    at += columns
    sums_out[at : at + columns, :wells] = jnp.sum(found, axis=1)


def exact_dot(left, right, transposed=False):
    axes = ((1,), (1,)) if transposed else ((1,), (0,))
    return lax.dot_general(
        left, right, (axes, ((), ())), precision=lax.Precision.HIGHEST, preferred_element_type=F32
    )


def finish_kernel(
    dims, scale, wells, sums_ref, table_ref, flat_ref, basis_source,
    block_out, first_out, coeffs_out, wells_out, basis_ref, sem,
):
    (basis_copy,) = start_copies([(basis_source, basis_ref)], sem)
    columns, size_x, size_y, size_z, slots = dims
    lines = size_x * size_y
    count = basis_ref.shape[0]
    blocks = count // LANES
    pieces, at = {}, 0
    for i in range(blocks):
        for j in range(i, blocks):
            pieces[i, j] = table_ref[at : at + LANES, :]
            pieces[j, i] = pieces[i, j] if i == j else pieces[i, j].T
            at += LANES
    basis_gram = jnp.concatenate(
        [jnp.concatenate([pieces[i, j] for j in range(blocks)], axis=1) for i in range(blocks)], axis=0
    )
    beside = LANES // wells
    wells_basis = []
    for i in range(blocks):
        place = at + i // beside * LANES
        wells_basis.append(table_ref[place : place + LANES, i % beside * wells : (i % beside + 1) * wells])
    wells_basis = jnp.concatenate(wells_basis, axis=0)

    def block(i):
        return sums_ref[i * columns : (i + 1) * columns, :]

    first = jnp.concatenate([block(i) for i in range(blocks)], axis=1)
    beyond = jnp.concatenate([block(blocks + i) for i in range(blocks)], axis=1)
    full = first + beyond
    square = block(2 * blocks)[:, :columns]
    at_wells = block(2 * blocks + 1)[:, :wells]
    first_round = first.astype(BF16)
    second = full - exact_dot(first_round.astype(F32), basis_gram)
    second_round = second.astype(BF16)
    taken = first_round.astype(F32) + second_round.astype(F32)
    half = full - 0.5 * exact_dot(taken, basis_gram)
    cross = exact_dot(taken, half, transposed=True)
    gram = square - cross - cross.T
    rest_wells = at_wells - exact_dot(taken, wells_basis)
    first_out[...] = first
    coeffs_out[...] = first + second
    row = lax.broadcasted_iota(jnp.int32, (columns, columns), 0)
    lane = lax.broadcasted_iota(jnp.int32, (columns, columns), 1)
    left = gram
    right = jnp.where(row == lane, 1.0, 0.0)
    below = lax.broadcasted_iota(jnp.int32, (columns, 1), 0)
    for k in range(columns - 1):
        factor = jnp.where(below > k, left[:, k : k + 1] / left[k : k + 1, k : k + 1], 0.0)
        right = right - factor * right[k : k + 1, :]
        left = left - factor * left[k : k + 1, :]
    pivots = jnp.sum(jnp.where(row == lane, left, 0.0), axis=1, keepdims=True)
    inverse = right * (scale / jnp.sqrt(pivots))
    wells_out[...] = exact_dot(inverse, rest_wells)
    high, low = split_two(inverse)
    factors = jnp.concatenate([high, high, low], axis=1)
    basis_copy.wait()
    rounds = jnp.concatenate([first_round, second_round], axis=0)
    step = min(8, lines)
    for begin in range(0, lines, step):
        lanes = slice(begin * size_z, (begin + step) * size_z)
        spans = jnp.dot(rounds, basis_ref[:, lanes], preferred_element_type=F32)
        rest = flat_ref[:, lanes] - spans[:columns] - spans[columns:]
        rest_high, rest_low = split_two(rest)
        stacked = jnp.concatenate([rest_high, rest_low, rest_high], axis=0)
        done = jnp.dot(factors, stacked, preferred_element_type=F32)
        for i in range(step):
            block_out[:, begin + i, :] = done[:, i * size_z : (i + 1) * size_z]


def local(
    start_block,
    basis,
    trans_x,
    trans_y,
    trans_z,
    pore_volume,
    shift_table,
    shift_index,
    fault_send,
    fault_recv,
    fault_trans,
    well_cells,
):
    columns, size_x, size_y, size_z = start_block.shape
    devices, slots = fault_send.shape[1:]
    lines = size_x * size_y
    cells = lines * size_z
    total = devices * slots
    sizes = [lax.axis_size(axis) for axis in AXES]
    index_x, index_y, index_z = (lax.axis_index(axis) for axis in AXES)
    full_x, full_y, full_z = size_x * sizes[0], size_y * sizes[1], size_z * sizes[2]
    has_b = tuple(size > 2 for size in sizes)
    dims = (columns, size_x, size_y, size_z, slots)
    rows = columns * slots // LANES
    index = [index_x, index_y, index_z]
    par = jnp.stack(
        [i % 2 for i in index] + [(i == n - 1).astype(jnp.int32) for i, n in zip(index, sizes)]
    )

    vmem = pl.BlockSpec(memory_space=pltpu.VMEM)
    smem = pl.BlockSpec(memory_space=pltpu.SMEM)
    params = pltpu.CompilerParams(vmem_limit_bytes=8 * 2**20 + 4096 * total)
    wide_params = pltpu.CompilerParams(vmem_limit_bytes=16 * 2**20 + 4096 * total)
    field_type = jax.ShapeDtypeStruct((columns, lines, size_z), F32)
    x_type = jax.ShapeDtypeStruct((columns, size_y, size_z), F32)
    y_type = jax.ShapeDtypeStruct((2 * size_x, columns, size_z), F32)
    face_types = (
        [x_type] * (1 + has_b[0])
        + [y_type]
        + [jax.ShapeDtypeStruct((2, columns * lines), F32)]
    )

    def in_hbm(*values):
        return [pltpu.with_memory_space_constraint(value, pltpu.HBM) for value in values]

    shape2 = (lines, size_z)
    start = start_block.reshape(columns, lines, size_z)
    anywhere = pl.BlockSpec(memory_space=pltpu.HBM)
    trans = [value.reshape(shape2) for value in (trans_x, trans_y, trans_z)]
    row_types = [jax.ShapeDtypeStruct((1, total), kind) for kind in (jnp.int32, jnp.int32, F32)]
    edge_types = [
        jax.ShapeDtypeStruct(shape, F32) for shape in ((size_y, size_z), (size_x, size_z), (1, lines))
    ]
    edge_x, edge_y, edge_z, send, recv, weight = pl.pallas_call(
        functools.partial(edges_kernel, dims),
        out_shape=edge_types + row_types,
        in_specs=[anywhere] * 6,
        out_specs=[vmem] * 6,
        scratch_shapes=[pltpu.VMEM(shape2, F32)] * 3
        + [pltpu.VMEM(fault_send.shape, kind) for kind in (jnp.int32, jnp.int32, F32)]
        + [pltpu.SemaphoreType.DMA((6,))],
        compiler_params=params,
        name="edges",
    )(*in_hbm(*trans, fault_send, fault_recv, fault_trans))
    edge_x, edge_y, edge_z = from_behind(edge_x, "gx"), from_behind(edge_y, "gy"), from_behind(edge_z, "gz")

    def gather(direction, goes="", source=()):
        sent_rows = devices * (rows + (extra if goes else 0))
        return pl.pallas_call(
            functools.partial(gather_kernel, dims, (extra, goes)),
            out_shape=jax.ShapeDtypeStruct((sent_rows, LANES), F32),
            in_specs=[vmem] * (2 + len(source)),
            out_specs=vmem,
            compiler_params=params,
            cost_estimate=pl.CostEstimate(
                flops=4 * columns * cells * total, bytes_accessed=4 * columns * cells, transcendentals=0
            ),
            name="fault_gather",
        )(direction, send, *source)

    def transfers(faults, faces):
        *x_faces, y_ab, z_ab = faces
        y_first, z_first = swap(y_ab, "gy", False), swap(z_ab, "gz", False)
        came = [swap(face, "gx", odd) for face, odd in zip(x_faces, (False, True))]
        faults, y_first, z_first = lax.optimization_barrier((faults, y_first, z_first))
        arrived = exchange(faults)
        return arrived, came + swap_rest(y_ab, y_first, "gy") + swap_rest(z_ab, z_first, "gz")

    def stencil(residual, direction, came):
        return pl.pallas_call(
            functools.partial(stencil_kernel, dims, has_b),
            out_shape=field_type,
            in_specs=[smem] + [vmem] * (3 + len(came)),
            out_specs=vmem,
            input_output_aliases={2: 0},
            compiler_params=params,
            cost_estimate=pl.CostEstimate(
                flops=20 * columns * cells, bytes_accessed=12 * columns * cells, transcendentals=0
            ),
            name="stencil",
        )(par, ops, residual, direction, *came)

    ops, residual, direction, *faces = pl.pallas_call(
        functools.partial(setup_kernel, dims, has_b),
        out_shape=[jax.ShapeDtypeStruct((8, lines, size_z), F32), field_type, field_type] + face_types,
        in_specs=[smem] * 3 + [vmem] * 5 + [anywhere] * 5,
        out_specs=[vmem] * (3 + len(face_types)),
        scratch_shapes=[pltpu.VMEM(shape2, F32)] * 4 + [pltpu.SemaphoreType.DMA((5,))],
        compiler_params=params,
        name="setup",
    )(
        par, shift_table, shift_index, edge_x, edge_y, edge_z, recv, weight,
        *in_hbm(*trans, pore_volume.reshape(shape2), start),
    )
    plane = full_y * full_z
    well_x = well_cells // plane
    well_y = well_cells // full_z % full_y
    well_z = well_cells % full_z
    owned = (
        (well_x // size_x == index_x)
        & (well_y // size_y == index_y)
        & (well_z // size_z == index_z)
    )
    local_cell = (well_x % size_x * size_y + well_y % size_y) * size_z + well_z % size_z
    wells = well_cells.shape[0]
    well_local = jnp.where(owned, local_cell, -1).reshape(1, wells)
    count = basis.shape[0]
    blocks = count // LANES
    early_rows = LANES * (blocks * (blocks + 1) // 2 + -(-blocks // (LANES // wells)))
    extra = -(-early_rows // devices)
    flat_basis_type = pltpu.HBM((count, cells), BF16)
    parts, flat_basis = pl.pallas_call(
        functools.partial(basis_kernel, dims),
        out_shape=[jax.ShapeDtypeStruct((devices * extra, LANES), F32), flat_basis_type],
        in_specs=[vmem, anywhere],
        out_specs=[vmem, anywhere],
        scratch_shapes=[
            pltpu.VMEM((count, lines, size_z), BF16),
            pltpu.VMEM((count, cells), BF16),
            pltpu.VMEM((cells, wells), BF16),
            pltpu.SemaphoreType.DMA((count // 16,)),
            pltpu.SemaphoreType.DMA((count // 16,)),
        ],
        compiler_params=wide_params,
        cost_estimate=pl.CostEstimate(
            flops=2 * count * cells * (count + wells), bytes_accessed=4 * count * cells, transcendentals=0
        ),
        name="basis_gram",
    )(well_local, *in_hbm(basis.reshape(count, lines, size_z)))

    needed = columns * (2 * blocks + 2)
    per_device = 1 << (-(-needed // devices) - 1).bit_length()
    sums_type = jax.ShapeDtypeStruct((devices * per_device, LANES), F32)
    flat_type = jax.ShapeDtypeStruct((columns, cells), F32)
    sigma = 1.0 / 0.9
    weight_now = 1.0 / sigma
    solution = None
    for number in range(TERMS - 1):
        goes = {2: "parts", 3: "sums"}.get(number, "")
        faults = gather(direction, goes, [parts] if goes == "parts" else [table] if goes else [])
        arrived, came = transfers(faults, faces)
        residual = stencil(residual, direction, came)
        weight_new = 1.0 / (2.0 * sigma - weight_now)
        last_round = number == TERMS - 2
        body = functools.partial(
            update_kernel, dims, has_b, weight_new * weight_now, 2.0 * weight_new / 0.9,
            number == 0, last_round, (extra, goes),
        )
        weight_now = weight_new
        scratch = [pltpu.VMEM((columns * lines, size_z), F32)]
        out_types = [sums_type, flat_type] if last_round else [field_type]
        if goes:
            table_rows = extra if goes == "parts" else devices * extra
            out_types.append(jax.ShapeDtypeStruct((table_rows, LANES), F32))
        operands = [par, ops, residual, direction, recv, weight, arrived]
        aliases = {}
        if number:
            if not last_round:
                aliases[len(operands)] = 0
            operands.append(solution)
        in_specs = [smem] + [vmem] * (len(operands) - 1)
        if not last_round:
            aliases[2], aliases[3] = len(out_types), len(out_types) + 1
            out_types += [field_type, field_type] + face_types
        else:
            operands += [well_local, *in_hbm(flat_basis)]
            in_specs += [vmem, anywhere]
            scratch += [
                pltpu.VMEM((columns, lines, size_z), F32),
                pltpu.VMEM((count, cells), BF16),
                pltpu.SemaphoreType.DMA((1,)),
            ]
        outs = pl.pallas_call(
            body,
            out_shape=out_types,
            in_specs=in_specs,
            out_specs=[vmem] * len(out_types),
            scratch_shapes=scratch,
            input_output_aliases=aliases,
            compiler_params=wide_params if last_round else params,
            name="update",
        )(*operands)
        if last_round:
            sums, flat = outs
            break
        solution, *outs = outs
        if goes:
            table, *outs = outs
        residual, direction, *faces = outs

    mine = exchange(sums).reshape(devices, per_device, LANES).sum(axis=0)
    sums = exchange(jnp.tile(mine, (devices, 1)))

    scale = math.sqrt(full_x * full_y * full_z)
    new_block, first_coeffs, coeffs, well_resp = pl.pallas_call(
        functools.partial(finish_kernel, dims, scale, wells),
        out_shape=[
            field_type,
            jax.ShapeDtypeStruct((columns, count), F32),
            jax.ShapeDtypeStruct((columns, count), F32),
            jax.ShapeDtypeStruct((columns, wells), F32),
        ],
        in_specs=[vmem] * 3 + [anywhere],
        out_specs=[vmem] * 4,
        scratch_shapes=[pltpu.VMEM((count, cells), BF16), pltpu.SemaphoreType.DMA((1,))],
        compiler_params=wide_params,
        name="finish",
    )(sums, table, flat, *in_hbm(flat_basis))
    return new_block.reshape(start_block.shape), first_coeffs.T, coeffs.T, well_resp.T


def solution(mesh):
    in_specs = (
        P(None, "gx", "gy", "gz"),
        P(None, "gx", "gy", "gz"),
        P("gx", "gy", "gz"),
        P("gx", "gy", "gz"),
        P("gx", "gy", "gz"),
        P("gx", "gy", "gz"),
        P(),
        P(),
        P(("gx", "gy", "gz"), None, None),
        P(("gx", "gy", "gz"), None, None),
        P(("gx", "gy", "gz"), None, None),
        P(),
    )
    out_specs = (P(None, "gx", "gy", "gz"), P(), P(), P())
    return jax.shard_map(local, mesh=mesh, in_specs=in_specs, out_specs=out_specs, check_vma=False)
```

profile of v0, /device:TPU:0, one launch (start us, length us, event | category | flops | bytes accessed | tf_op | source)
XLA Modules:
  0.0 193.2 jit_solution(7525275762907632510)
XLA Ops:
  1.7 4.8 %collective-permute-start = (f32[16,128]{1,0:T(8,128)S(1)}, f32[16,128]{1,0:T(8,128)S(1)}, u32[]{:S(2)}, u32[]{:S(2)}) collective-permute-start(f32[16,128]{1,0:T(8,128)S(1)} %get-tuple-element.83), channel_id=1, source_target_pairs={{0,16},{1,17},{2,18},{3,19},{4,20},{5,21},{6,22},{7,23},{8,24},{9,... | collective-permute-start | bytes 24584 | tf_op jit(solution)/shard_map/ppermute | solution.py:39
  6.5 3.5 %collective-permute-start.2 = (f32[1,64]{1,0:T(1,128)S(1)}, f32[1,64]{1,0:T(1,128)S(1)}, u32[]{:S(2)}, u32[]{:S(2)}) collective-permute-start(f32[1,64]{1,0:T(1,128)S(1)} %get-tuple-element.85), channel_id=1, source_target_pairs={{0,1},{1,2},{2,3},{4,5},{5,6},{6,7},{8,9},{9,10},{10,11},{12,13},{... | collective-permute-start | bytes 776 | tf_op jit(solution)/shard_map/ppermute | solution.py:39
  20.7 5.3 %all-to-all-start = ((f32[32,4,128]{2,1,0:T(4,128)}), f32[32,4,128]{2,1,0:T(4,128)S(1)}, u32[]{:S(2)}, u32[]{:S(2)}) async-start(f32[32,4,128]{2,1,0:T(4,128)} %bitcast.11), calls=%async_computation | async-start | bytes 131072 | tf_op jit(solution)/shard_map/all_to_all | solution.py:43
  27.9 2.4 %collective-permute-start.7 = (f32[2,1024]{1,0:T(2,128)S(1)}, f32[2,1024]{1,0:T(2,128)S(1)}, u32[]{:S(2)}, u32[]{:S(2)}) collective-permute-start(f32[2,1024]{1,0:T(2,128)S(1)} %collective-permute-done.5.refs_7_), channel_id=1, source_target_pairs={{0,2},{1,3},{2,0},{3,1},{4,6},{5,7},{6,4},{7,5},{8,10},{9,11},{10,... | collective-permute-start | bytes 24584 | tf_op jit(solution)/shard_map/ppermute | solution.py:33
  40.2 4.1 %all-to-all-start.1 = ((f32[32,4,128]{2,1,0:T(4,128)}), f32[32,4,128]{2,1,0:T(4,128)S(1)}, u32[]{:S(2)}, u32[]{:S(2)}) async-start(f32[32,4,128]{2,1,0:T(4,128)} %bitcast.13), calls=%async_computation.1 | async-start | bytes 131072 | tf_op jit(solution)/shard_map/all_to_all | solution.py:43
  44.3 2.6 %collective-permute-start.12 = (f32[2,1024]{1,0:T(2,128)S(1)}, f32[2,1024]{1,0:T(2,128)S(1)}, u32[]{:S(2)}, u32[]{:S(2)}) collective-permute-start(f32[2,1024]{1,0:T(2,128)S(1)} %collective-permute-done.10.refs_7_), channel_id=1, source_target_pairs={{0,2},{1,3},{2,0},{3,1},{4,6},{5,7},{6,4},{7,5},{8,10},{9,11},{10,... | collective-permute-start | bytes 24584 | tf_op jit(solution)/shard_map/ppermute | solution.py:33
  54.4 8.1 %basis_gram.1 = (f32[512,128]{1,0:T(8,128)S(1)}, bf16[256,8192]{1,0:T(8,128)(2,1)}) custom-call(s32[1,64]{1,0:T(1,128)S(1)} %fusion.4.well_ref.refs_8_, bf16[256,64,128]{2,1,0:T(8,128)(2,1)} %bitcast.45), custom_call_target="tpu_custom_call" | custom-call | flops 1342177280 | bytes 8388608 | tf_op jit(solution)/shard_map/basis_gram/pallas_call | solution.py:636
  67.1 3.6 %all-to-all-start.2 = ((f32[32,20,128]{2,1,0:T(8,128)}), f32[32,20,128]{2,1,0:T(8,128)S(1)}, u32[]{:S(2)}, u32[]{:S(2)}) async-start(f32[32,20,128]{2,1,0:T(8,128)} %all_to_all.66), calls=%async_computation.2 | async-start | bytes 786432 | tf_op jit(solution)/shard_map/all_to_all | solution.py:43
  74.0 2.4 %collective-permute-start.17 = (f32[2,1024]{1,0:T(2,128)S(1)}, f32[2,1024]{1,0:T(2,128)S(1)}, u32[]{:S(2)}, u32[]{:S(2)}) collective-permute-start(f32[2,1024]{1,0:T(2,128)S(1)} %collective-permute-done.15.refs_7_), channel_id=1, source_target_pairs={{0,2},{1,3},{2,0},{3,1},{4,6},{5,7},{6,4},{7,5},{8,10},{9,11},{10,... | collective-permute-start | bytes 24584 | tf_op jit(solution)/shard_map/ppermute | solution.py:33
  76.4 6.8 %collective-permute-done.17.refs_8_ = f32[2,1024]{1,0:T(2,128)S(1)} collective-permute-done((f32[2,1024]{1,0:T(2,128)S(1)}, f32[2,1024]{1,0:T(2,128)S(1)}, u32[]{:S(2)}, u32[]{:S(2)}) %collective-permute-start.17) | collective-permute-done | bytes 8224 | tf_op jit(solution)/shard_map/ppermute | solution.py:33
  87.7 2.6 %collective-permute-done.20.refs_7_ = f32[2,1024]{1,0:T(2,128)S(1)} collective-permute-done((f32[2,1024]{1,0:T(2,128)S(1)}, f32[2,1024]{1,0:T(2,128)S(1)}, u32[]{:S(2)}, u32[]{:S(2)}) %collective-permute-start.20) | collective-permute-done | bytes 8224 | tf_op jit(solution)/shard_map/ppermute | solution.py:27
  91.1 3.8 %all-to-all-start.3 = ((f32[32,20,128]{2,1,0:T(8,128)}), f32[32,20,128]{2,1,0:T(8,128)S(1)}, u32[]{:S(2)}, u32[]{:S(2)}) async-start(f32[32,20,128]{2,1,0:T(8,128)} %all_to_all.69), calls=%async_computation.3 | async-start | bytes 786432 | tf_op jit(solution)/shard_map/all_to_all | solution.py:43
  98.1 2.4 %collective-permute-start.22 = (f32[2,1024]{1,0:T(2,128)S(1)}, f32[2,1024]{1,0:T(2,128)S(1)}, u32[]{:S(2)}, u32[]{:S(2)}) collective-permute-start(f32[2,1024]{1,0:T(2,128)S(1)} %collective-permute-done.20.refs_7_), channel_id=1, source_target_pairs={{0,2},{1,3},{2,0},{3,1},{4,6},{5,7},{6,4},{7,5},{8,10},{9,11},{10,... | collective-permute-start | bytes 24584 | tf_op jit(solution)/shard_map/ppermute | solution.py:33
  100.5 6.8 %collective-permute-done.22.refs_8_ = f32[2,1024]{1,0:T(2,128)S(1)} collective-permute-done((f32[2,1024]{1,0:T(2,128)S(1)}, f32[2,1024]{1,0:T(2,128)S(1)}, u32[]{:S(2)}, u32[]{:S(2)}) %collective-permute-start.22) | collective-permute-done | bytes 8224 | tf_op jit(solution)/shard_map/ppermute | solution.py:33
  114.5 3.6 %all-to-all-start.4 = ((f32[32,4,128]{2,1,0:T(4,128)}), f32[32,4,128]{2,1,0:T(4,128)S(1)}, u32[]{:S(2)}, u32[]{:S(2)}) async-start(f32[32,4,128]{2,1,0:T(4,128)} %bitcast.17), calls=%async_computation.4 | async-start | bytes 131072 | tf_op jit(solution)/shard_map/all_to_all | solution.py:43
  119.9 2.4 %collective-permute-start.27 = (f32[2,1024]{1,0:T(2,128)S(1)}, f32[2,1024]{1,0:T(2,128)S(1)}, u32[]{:S(2)}, u32[]{:S(2)}) collective-permute-start(f32[2,1024]{1,0:T(2,128)S(1)} %collective-permute-done.25.refs_7_), channel_id=1, source_target_pairs={{0,2},{1,3},{2,0},{3,1},{4,6},{5,7},{6,4},{7,5},{8,10},{9,11},{10,... | collective-permute-start | bytes 24584 | tf_op jit(solution)/shard_map/ppermute | solution.py:33
  132.2 3.9 %all-to-all-start.5 = ((f32[32,4,128]{2,1,0:T(4,128)}), f32[32,4,128]{2,1,0:T(4,128)S(1)}, u32[]{:S(2)}, u32[]{:S(2)}) async-start(f32[32,4,128]{2,1,0:T(4,128)} %bitcast.19), calls=%async_computation.5 | async-start | bytes 131072 | tf_op jit(solution)/shard_map/all_to_all | solution.py:43
  137.9 2.4 %collective-permute-start.32 = (f32[2,1024]{1,0:T(2,128)S(1)}, f32[2,1024]{1,0:T(2,128)S(1)}, u32[]{:S(2)}, u32[]{:S(2)}) collective-permute-start(f32[2,1024]{1,0:T(2,128)S(1)} %collective-permute-done.30.refs_7_), channel_id=1, source_target_pairs={{0,2},{1,3},{2,0},{3,1},{4,6},{5,7},{6,4},{7,5},{8,10},{9,11},{10,... | collective-permute-start | bytes 24584 | tf_op jit(solution)/shard_map/ppermute | solution.py:33
  150.2 4.1 %all-to-all-start.6 = ((f32[32,4,128]{2,1,0:T(4,128)}), f32[32,4,128]{2,1,0:T(4,128)S(1)}, u32[]{:S(2)}, u32[]{:S(2)}) async-start(f32[32,4,128]{2,1,0:T(4,128)} %bitcast.21), calls=%async_computation.6 | async-start | bytes 131072 | tf_op jit(solution)/shard_map/all_to_all | solution.py:43
  155.9 2.4 %collective-permute-start.37 = (f32[2,1024]{1,0:T(2,128)S(1)}, f32[2,1024]{1,0:T(2,128)S(1)}, u32[]{:S(2)}, u32[]{:S(2)}) collective-permute-start(f32[2,1024]{1,0:T(2,128)S(1)} %collective-permute-done.35.refs_7_), channel_id=1, source_target_pairs={{0,2},{1,3},{2,0},{3,1},{4,6},{5,7},{6,4},{7,5},{8,10},{9,11},{10,... | collective-permute-start | bytes 24584 | tf_op jit(solution)/shard_map/ppermute | solution.py:33
  162.0 4.9 %update.13 = (f32[128,128]{1,0:T(8,128)S(1)}, f32[16,8192]{1,0:T(8,128)S(1)}) custom-call(s32[6]{0:T(128)S(1)} %stack.39.refs_0_, f32[8,64,128]{2,1,0:T(8,128)S(1)} %get-tuple-element.88.refs_1_, f32[16,64,128]{2,1,0:T(8,128)S(1)} %stencil.13.refs_2_, f32[16,64,128]{2,1,0:T(8,128)S(1)} %get-tuple-element.146.refs_0_.refs_3_, ...), custom_call_target="tpu_custom_call" | custom-call | tf_op jit(solution)/shard_map/update/pallas_call | solution.py:697
  166.9 12.0 %all_to_all.94 = f32[32,4,128]{2,1,0:T(4,128)S(1)} all-to-all(f32[32,4,128]{2,1,0:T(4,128)S(1)} %bitcast.36), channel_id=1, replica_groups=mesh['gx'=2,'gy'=4,'gz'=4] {'gx','gy','gz'}, dimensions={0} | all-to-all | bytes 131072 | tf_op jit(solution)/shard_map/all_to_all | solution.py:43
  178.9 9.2 %all_to_all.95 = f32[32,4,128]{2,1,0:T(4,128)S(1)} all-to-all(f32[32,4,128]{2,1,0:T(4,128)S(1)} %tile.2), channel_id=1, replica_groups=mesh['gx'=2,'gy'=4,'gz'=4] {'gx','gy','gz'}, dimensions={0} | all-to-all | bytes 131072 | tf_op jit(solution)/shard_map/all_to_all | solution.py:43
  188.1 4.9 %finish.1 = (f32[16,64,128]{2,1,0:T(8,128)}, f32[16,256]{1,0:T(8,128)}, f32[16,256]{1,0:T(8,128)}, f32[16,64]{1,0:T(8,128)}) custom-call(f32[128,128]{1,0:T(8,128)S(1)} %bitcast.31, f32[512,128]{1,0:T(8,128)S(1)} %get-tuple-element.156.table_ref, f32[16,8192]{1,0:T(8,128)S(1)} %get-tuple-element.157.flat_ref, ...), custom_call_target="tpu_custom_call" | custom-call | tf_op jit(solution)/shard_map/finish/pallas_call | solution.py:719
  (105 shorter events, 82.4 us)
Async XLA Ops:
  1.7 10.4 %collective-permute-start = (f32[16,128]{1,0:T(8,128)S(1)}, f32[16,128]{1,0:T(8,128)S(1)}, u32[]{:S(2)}, u32[]{:S(2)}) collective-permute-start(f32[16,128]{1,0:T(8,128)S(1)} %get-tuple-element.83), channel_id=1, source_target_pairs={{0,16},{1,17},{2,18},{3,19},{4,20},{5,21},{6,22},{7,23},{8,24},{9,... | collective-permute-start | bytes 24584 | tf_op jit(solution)/shard_map/ppermute | solution.py:39
  18.7 13.8 %collective-permute-start.3 = (f32[16,16,128]{2,1,0:T(8,128)S(1)}, f32[16,16,128]{2,1,0:T(8,128)S(1)}, u32[]{:S(2)}, u32[]{:S(2)}) collective-permute-start(f32[16,16,128]{2,1,0:T(8,128)S(1)} %get-tuple-element.91), channel_id=1, source_target_pairs={{0,16},{16,0},{1,17},{17,1},{2,18},{18,2},{3,19},{19,3},{4,20},{20... | collective-permute-start | bytes 393224 | tf_op jit(solution)/shard_map/ppermute | solution.py:27
  20.7 13.3 %all-to-all-start = ((f32[32,4,128]{2,1,0:T(4,128)}), f32[32,4,128]{2,1,0:T(4,128)S(1)}, u32[]{:S(2)}, u32[]{:S(2)}) async-start(f32[32,4,128]{2,1,0:T(4,128)} %bitcast.11), calls=%async_computation | async-start | bytes 131072 | tf_op jit(solution)/shard_map/all_to_all | solution.py:43
  26.1 6.4 %collective-permute-start.6 = (f32[8,16,128]{2,1,0:T(8,128)S(1)}, f32[8,16,128]{2,1,0:T(8,128)S(1)}, u32[]{:S(2)}, u32[]{:S(2)}) collective-permute-start(f32[8,16,128]{2,1,0:T(8,128)S(1)} %collective-permute-done.4.refs_5_), channel_id=1, source_target_pairs={{0,8},{4,12},{8,0},{12,4},{1,9},{5,13},{9,1},{13,5},{2,10},{6,14},... | collective-permute-start | bytes 196616 | tf_op jit(solution)/shard_map/ppermute | solution.py:33
  38.7 12.5 %collective-permute-start.8 = (f32[16,16,128]{2,1,0:T(8,128)S(1)}, f32[16,16,128]{2,1,0:T(8,128)S(1)}, u32[]{:S(2)}, u32[]{:S(2)}) collective-permute-start(f32[16,16,128]{2,1,0:T(8,128)S(1)} %get-tuple-element.100), channel_id=1, source_target_pairs={{0,16},{16,0},{1,17},{17,1},{2,18},{18,2},{3,19},{19,3},{4,20},{20... | collective-permute-start | bytes 393224 | tf_op jit(solution)/shard_map/ppermute | solution.py:27
  40.2 12.6 %all-to-all-start.1 = ((f32[32,4,128]{2,1,0:T(4,128)}), f32[32,4,128]{2,1,0:T(4,128)S(1)}, u32[]{:S(2)}, u32[]{:S(2)}) async-start(f32[32,4,128]{2,1,0:T(4,128)} %bitcast.13), calls=%async_computation.1 | async-start | bytes 131072 | tf_op jit(solution)/shard_map/all_to_all | solution.py:43
  54.4 11.9 %collective-permute-start.14 = (f32[8,16,128]{2,1,0:T(8,128)S(1)}, f32[8,16,128]{2,1,0:T(8,128)S(1)}, u32[]{:S(2)}, u32[]{:S(2)}) collective-permute-start(f32[8,16,128]{2,1,0:T(8,128)S(1)} %get-tuple-element.111), channel_id=1, source_target_pairs={{0,4},{4,0},{8,12},{12,8},{1,5},{5,1},{9,13},{13,9},{2,6},{6,2},{1... | collective-permute-start | bytes 196616 | tf_op jit(solution)/shard_map/ppermute | solution.py:27
  67.1 17.7 %all-to-all-start.2 = ((f32[32,20,128]{2,1,0:T(8,128)}), f32[32,20,128]{2,1,0:T(8,128)S(1)}, u32[]{:S(2)}, u32[]{:S(2)}) async-start(f32[32,20,128]{2,1,0:T(8,128)} %all_to_all.66), calls=%async_computation.2 | async-start | bytes 786432 | tf_op jit(solution)/shard_map/all_to_all | solution.py:43
  70.7 12.5 %collective-permute-start.13 = (f32[16,16,128]{2,1,0:T(8,128)S(1)}, f32[16,16,128]{2,1,0:T(8,128)S(1)}, u32[]{:S(2)}, u32[]{:S(2)}) collective-permute-start(f32[16,16,128]{2,1,0:T(8,128)S(1)} %get-tuple-element.109), channel_id=1, source_target_pairs={{0,16},{16,0},{1,17},{17,1},{2,18},{18,2},{3,19},{19,3},{4,20},{20... | collective-permute-start | bytes 393224 | tf_op jit(solution)/shard_map/ppermute | solution.py:27
  72.5 10.7 %collective-permute-start.16 = (f32[8,16,128]{2,1,0:T(8,128)S(1)}, f32[8,16,128]{2,1,0:T(8,128)S(1)}, u32[]{:S(2)}, u32[]{:S(2)}) collective-permute-start(f32[8,16,128]{2,1,0:T(8,128)S(1)} %collective-permute-done.14.refs_5_), channel_id=1, source_target_pairs={{0,8},{4,12},{8,0},{12,4},{1,9},{5,13},{9,1},{13,5},{2,10},{6,14},... | collective-permute-start | bytes 196616 | tf_op jit(solution)/shard_map/ppermute | solution.py:33
  74.0 9.2 %collective-permute-start.17 = (f32[2,1024]{1,0:T(2,128)S(1)}, f32[2,1024]{1,0:T(2,128)S(1)}, u32[]{:S(2)}, u32[]{:S(2)}) collective-permute-start(f32[2,1024]{1,0:T(2,128)S(1)} %collective-permute-done.15.refs_7_), channel_id=1, source_target_pairs={{0,2},{1,3},{2,0},{3,1},{4,6},{5,7},{6,4},{7,5},{8,10},{9,11},{10,... | collective-permute-start | bytes 24584 | tf_op jit(solution)/shard_map/ppermute | solution.py:33
  91.1 17.8 %all-to-all-start.3 = ((f32[32,20,128]{2,1,0:T(8,128)}), f32[32,20,128]{2,1,0:T(8,128)S(1)}, u32[]{:S(2)}, u32[]{:S(2)}) async-start(f32[32,20,128]{2,1,0:T(8,128)} %all_to_all.69), calls=%async_computation.3 | async-start | bytes 786432 | tf_op jit(solution)/shard_map/all_to_all | solution.py:43
  95.0 12.3 %collective-permute-start.18 = (f32[16,16,128]{2,1,0:T(8,128)S(1)}, f32[16,16,128]{2,1,0:T(8,128)S(1)}, u32[]{:S(2)}, u32[]{:S(2)}) collective-permute-start(f32[16,16,128]{2,1,0:T(8,128)S(1)} %get-tuple-element.119), channel_id=1, source_target_pairs={{0,16},{16,0},{1,17},{17,1},{2,18},{18,2},{3,19},{19,3},{4,20},{20... | collective-permute-start | bytes 393224 | tf_op jit(solution)/shard_map/ppermute | solution.py:27
  96.6 10.7 %collective-permute-start.21 = (f32[8,16,128]{2,1,0:T(8,128)S(1)}, f32[8,16,128]{2,1,0:T(8,128)S(1)}, u32[]{:S(2)}, u32[]{:S(2)}) collective-permute-start(f32[8,16,128]{2,1,0:T(8,128)S(1)} %collective-permute-done.19.refs_5_), channel_id=1, source_target_pairs={{0,8},{4,12},{8,0},{12,4},{1,9},{5,13},{9,1},{13,5},{2,10},{6,14},... | collective-permute-start | bytes 196616 | tf_op jit(solution)/shard_map/ppermute | solution.py:33
  98.1 9.2 %collective-permute-start.22 = (f32[2,1024]{1,0:T(2,128)S(1)}, f32[2,1024]{1,0:T(2,128)S(1)}, u32[]{:S(2)}, u32[]{:S(2)}) collective-permute-start(f32[2,1024]{1,0:T(2,128)S(1)} %collective-permute-done.20.refs_7_), channel_id=1, source_target_pairs={{0,2},{1,3},{2,0},{3,1},{4,6},{5,7},{6,4},{7,5},{8,10},{9,11},{10,... | collective-permute-start | bytes 24584 | tf_op jit(solution)/shard_map/ppermute | solution.py:33
  111.0 13.5 %collective-permute-start.23 = (f32[16,16,128]{2,1,0:T(8,128)S(1)}, f32[16,16,128]{2,1,0:T(8,128)S(1)}, u32[]{:S(2)}, u32[]{:S(2)}) collective-permute-start(f32[16,16,128]{2,1,0:T(8,128)S(1)} %get-tuple-element.129), channel_id=1, source_target_pairs={{0,16},{16,0},{1,17},{17,1},{2,18},{18,2},{3,19},{19,3},{4,20},{20... | collective-permute-start | bytes 393224 | tf_op jit(solution)/shard_map/ppermute | solution.py:27
  114.5 11.6 %all-to-all-start.4 = ((f32[32,4,128]{2,1,0:T(4,128)}), f32[32,4,128]{2,1,0:T(4,128)S(1)}, u32[]{:S(2)}, u32[]{:S(2)}) async-start(f32[32,4,128]{2,1,0:T(4,128)} %bitcast.17), calls=%async_computation.4 | async-start | bytes 131072 | tf_op jit(solution)/shard_map/all_to_all | solution.py:43
  118.1 6.4 %collective-permute-start.26 = (f32[8,16,128]{2,1,0:T(8,128)S(1)}, f32[8,16,128]{2,1,0:T(8,128)S(1)}, u32[]{:S(2)}, u32[]{:S(2)}) collective-permute-start(f32[8,16,128]{2,1,0:T(8,128)S(1)} %collective-permute-done.24.refs_5_), channel_id=1, source_target_pairs={{0,8},{4,12},{8,0},{12,4},{1,9},{5,13},{9,1},{13,5},{2,10},{6,14},... | collective-permute-start | bytes 196616 | tf_op jit(solution)/shard_map/ppermute | solution.py:33
  129.2 13.2 %collective-permute-start.28 = (f32[16,16,128]{2,1,0:T(8,128)S(1)}, f32[16,16,128]{2,1,0:T(8,128)S(1)}, u32[]{:S(2)}, u32[]{:S(2)}) collective-permute-start(f32[16,16,128]{2,1,0:T(8,128)S(1)} %get-tuple-element.138), channel_id=1, source_target_pairs={{0,16},{16,0},{1,17},{17,1},{2,18},{18,2},{3,19},{19,3},{4,20},{20... | collective-permute-start | bytes 393224 | tf_op jit(solution)/shard_map/ppermute | solution.py:27
  132.2 11.8 %all-to-all-start.5 = ((f32[32,4,128]{2,1,0:T(4,128)}), f32[32,4,128]{2,1,0:T(4,128)S(1)}, u32[]{:S(2)}, u32[]{:S(2)}) async-start(f32[32,4,128]{2,1,0:T(4,128)} %bitcast.19), calls=%async_computation.5 | async-start | bytes 131072 | tf_op jit(solution)/shard_map/all_to_all | solution.py:43
  136.1 6.4 %collective-permute-start.31 = (f32[8,16,128]{2,1,0:T(8,128)S(1)}, f32[8,16,128]{2,1,0:T(8,128)S(1)}, u32[]{:S(2)}, u32[]{:S(2)}) collective-permute-start(f32[8,16,128]{2,1,0:T(8,128)S(1)} %collective-permute-done.29.refs_5_), channel_id=1, source_target_pairs={{0,8},{4,12},{8,0},{12,4},{1,9},{5,13},{9,1},{13,5},{2,10},{6,14},... | collective-permute-start | bytes 196616 | tf_op jit(solution)/shard_map/ppermute | solution.py:33
  147.2 13.2 %collective-permute-start.33 = (f32[16,16,128]{2,1,0:T(8,128)S(1)}, f32[16,16,128]{2,1,0:T(8,128)S(1)}, u32[]{:S(2)}, u32[]{:S(2)}) collective-permute-start(f32[16,16,128]{2,1,0:T(8,128)S(1)} %get-tuple-element.147), channel_id=1, source_target_pairs={{0,16},{16,0},{1,17},{17,1},{2,18},{18,2},{3,19},{19,3},{4,20},{20... | collective-permute-start | bytes 393224 | tf_op jit(solution)/shard_map/ppermute | solution.py:27
  150.2 11.8 %all-to-all-start.6 = ((f32[32,4,128]{2,1,0:T(4,128)}), f32[32,4,128]{2,1,0:T(4,128)S(1)}, u32[]{:S(2)}, u32[]{:S(2)}) async-start(f32[32,4,128]{2,1,0:T(4,128)} %bitcast.21), calls=%async_computation.6 | async-start | bytes 131072 | tf_op jit(solution)/shard_map/all_to_all | solution.py:43
  154.3 6.1 %collective-permute-start.36 = (f32[8,16,128]{2,1,0:T(8,128)S(1)}, f32[8,16,128]{2,1,0:T(8,128)S(1)}, u32[]{:S(2)}, u32[]{:S(2)}) collective-permute-start(f32[8,16,128]{2,1,0:T(8,128)S(1)} %collective-permute-done.34.refs_5_), channel_id=1, source_target_pairs={{0,8},{4,12},{8,0},{12,4},{1,9},{5,13},{9,1},{13,5},{2,10},{6,14},... | collective-permute-start | bytes 196616 | tf_op jit(solution)/shard_map/ppermute | solution.py:33
  (23 other events, 126.2 us)
where the time goes:
time: 194 us; the launch traced here: 193 us
  starting transfers between devices  86.1 us (44%)
  Pallas kernels  51.3 us (26%)
  waiting for transfers between devices  30.5 us (16%)
  blocking collectives  21.1 us (11%)
  local copies, waits for them, and re-layouts  2.36 us (1%)
    all_to_all x7, starting transfers between devices, exchange(): return lax.all_to_all(value, AXES, split_axis=0, concat_axis=0, tiled=True)  28.5 us
    ppermute x14, starting transfers between devices, swap_rest(): return [first, lax.ppermute(first, axis, [(i, i ^ 2) for i in range(size)])]  28.4 us
    ppermute x14, waiting for transfers between devices, swap_rest(): return [first, lax.ppermute(first, axis, [(i, i ^ 2) for i in range(size)])]  25.2 us
    all_to_all x2, blocking collectives, exchange(): return lax.all_to_all(value, AXES, split_axis=0, concat_axis=0, tiled=True)  21.1 us
    ppermute x21, starting transfers between devices, swap(): return lax.ppermute(value, axis, pairs) if pairs else value  19.6 us
    pallas_call x7, Pallas kernels, local(): pl.pallas_call(body, out_shape=out_types, in_specs=in_specs, out_specs=[v...  15 us
    pallas_call x7, Pallas kernels, stencil(): pl.pallas_call(functools.partial(stencil_kernel, dims, has_b), out_shape=...  11 us
    ppermute x3, starting transfers between devices, from_behind(): return lax.ppermute(value, axis, [(i, i + 1) for i in range(size - 1)])  9.61 us
  transfers between devices with their start and end apart: 45, of which 12 were waited for; matrix products, arithmetic and copies ran while one was open for 0% of the time, Pallas kernels for 15%

commit v1 on v0

--- a/solution.py
+++ b/solution.py
@@ -15,28 +15,30 @@
 F32 = jnp.float32
 
 
-def swap_pairs(size, odd):
+def swap_even(value, axis):
+    size = lax.axis_size(axis)
+    pairs = [(i, i ^ 1) for i in range(size) if i ^ 1 < size]
+    return lax.ppermute(value, axis, pairs)
+
+
+def swap_odd(value, axis):
+    size = lax.axis_size(axis)
+    other = "gy" if axis == "gx" else "gx"
+    across = lax.axis_size(other)
+    names = (axis, other) if axis == "gx" else (other, axis)
+
+    def number(i, o):
+        return i * across + o if axis == "gx" else o * size + i
+
     pairs = []
-    for low in range(1 if odd else 0, size - 1, 2):
-        pairs += [(low, low + 1), (low + 1, low)]
-    return pairs
-
-
-def swap(value, axis, odd):
-    pairs = swap_pairs(lax.axis_size(axis), odd)
-    return lax.ppermute(value, axis, pairs) if pairs else value
-
-
-def swap_rest(value, first, axis):
-    size = lax.axis_size(axis)
-    if size == 4:
-        return [first, lax.ppermute(first, axis, [(i, i ^ 2) for i in range(size)])]
-    return [first, swap(value, axis, True)] if size > 2 else [first]
-
-
-def from_behind(value, axis):
-    size = lax.axis_size(axis)
-    return lax.ppermute(value, axis, [(i, i + 1) for i in range(size - 1)])
+    for o in range(across):
+        for i in range(size):
+            to = (i + 1 if i % 2 else i - 1, o)
+            if not 0 <= to[0] < size:
+                to = (i, o ^ 1)
+            if to[1] < across:
+                pairs.append((number(i, o), number(*to)))
+    return lax.ppermute(value, names, pairs)
 
 
 def exchange(value):
@@ -63,15 +65,30 @@
     return high, low
 
 
+def one_hots(cell, lines, size_z):
+    half = lines // 2
+    total = cell.shape[1]
+    line = cell // size_z
+    key = line // half * size_z + cell % size_z
+    rows = jnp.broadcast_to(line % half, (half, total)) == lax.broadcasted_iota(jnp.int32, (half, total), 0)
+    keys = lax.broadcasted_iota(jnp.int32, (2 * size_z, total), 0)
+    keys = jnp.where(jnp.broadcast_to(key, (2 * size_z, total)) == keys, 1.0, 0.0).astype(BF16)
+    return rows, keys
+
+
 def nt_dot(left, right):
     return lax.dot_general(left, right, (((1,), (1,)), ((), ())), preferred_element_type=F32)
 
 
-def emit_faces(direction_ref, par_ref, faces_out, dims):
-    columns, size_x, size_y, size_z, slots = dims
-    lines = size_x * size_y
-    x_a, x_b, y_ab, z_ab = faces_out
-    even = [par_ref[i] == 0 for i in range(3)]
+def even_places():
+    return [lax.axis_index(axis) % 2 == 0 for axis in AXES]
+
+
+def emit_faces(direction_ref, faces_out, dims):
+    columns, size_x, size_y, size_z, slots = dims
+    lines = size_x * size_y
+    x_a, x_b, y_a, y_b, z_a, z_b = faces_out
+    even = even_places()
     field = direction_ref[...]
     first_x, last_x = field[:, :size_y, :], field[:, lines - size_y :, :]
     x_a[...] = jnp.where(even[0], last_x, first_x)
@@ -80,8 +97,9 @@
     for i in range(size_x):
         first_y = direction_ref[:, i * size_y, :]
         last_y = direction_ref[:, (i + 1) * size_y - 1, :]
-        y_ab[i] = jnp.where(even[1], last_y, first_y)
-        y_ab[size_x + i] = jnp.where(even[1], first_y, last_y)
+        y_a[i] = jnp.where(even[1], last_y, first_y)
+        if y_b is not None:
+            y_b[i] = jnp.where(even[1], first_y, last_y)
     both = jnp.concatenate(split_two(field.reshape(columns * lines, size_z)), axis=1)
     row = lax.broadcasted_iota(jnp.int32, (8, size_z), 0)
     lane = lax.broadcasted_iota(jnp.int32, (8, size_z), 1)
@@ -89,8 +107,9 @@
     pick = jnp.where(pick, 1.0, 0.0).astype(BF16)
     ends = nt_dot(jnp.concatenate([pick, pick], axis=1), both)
     last_z, first_z = ends[0:1, :], ends[1:2, :]
-    z_ab[0:1, :] = jnp.where(even[2], last_z, first_z)
-    z_ab[1:2, :] = jnp.where(even[2], first_z, last_z)
+    z_a[...] = jnp.where(even[2], last_z, first_z)
+    if z_b is not None:
+        z_b[...] = jnp.where(even[2], first_z, last_z)
 
 
 def gather_kernel(dims, early, *refs):
@@ -100,8 +119,9 @@
     columns, size_x, size_y, size_z, slots = dims
     lines = size_x * size_y
     rows = columns * slots // LANES
-    field = direction_ref[...]
-    both = jnp.concatenate(split_two(field.reshape(columns * lines, size_z)), axis=1)
+    half = lines // 2
+    field = direction_ref[...].astype(BF16)
+    field = jnp.concatenate([field[:, :half, :], field[:, half:, :]], axis=2).reshape(columns * half, 2 * size_z)
     if goes:
         for i in range(send_ref.shape[1] // slots):
             at = i * (rows + extra) + rows
@@ -110,14 +130,9 @@
     total = send_ref.shape[1]
     width = min(256, total)
     for start in range(0, total, width):
-        cell = send_ref[:, start : start + width]
-        lane_of = jnp.broadcast_to(cell % size_z, (size_z, width))
-        hot = lane_of == lax.broadcasted_iota(jnp.int32, (size_z, width), 0)
-        hot = jnp.where(hot, 1.0, 0.0).astype(BF16)
-        found = jnp.dot(both, jnp.concatenate([hot, hot], axis=0), preferred_element_type=F32)
-        line_of = jnp.broadcast_to(cell // size_z, (lines, width))
-        mask = line_of == lax.broadcasted_iota(jnp.int32, (lines, width), 0)
-        found = jnp.where(mask[None], found.reshape(columns, lines, width), 0.0)
+        hot_row, hot_key = one_hots(send_ref[:, start : start + width], lines, size_z)
+        found = jnp.dot(field, hot_key, preferred_element_type=F32)
+        found = jnp.where(hot_row[None], found.reshape(columns, half, width), 0.0)
         values = jnp.sum(found, axis=1)
         for j in range(0, width, LANES):
             tile = regroup(values[:, j : j + LANES], rows, slots)
@@ -156,30 +171,39 @@
 
 
 def setup_kernel(dims, has_b, *refs):
-    (par_ref, shifts_ref, which_ref, ex_ref, ey_ref, ez_ref, recv_ref, weight_ref) = refs[:8]
-    sources = refs[8:13]
-    ops_ref, residual_ref, direction_ref = refs[13:16]
-    faces_out = unpack_faces(refs[16 : 19 + has_b[0]], has_b)
-    held, sem = refs[19 + has_b[0] : -1], refs[-1]
+    shifts_ref, which_ref, recv_ref, weight_ref = refs[:4]
+    sources = refs[4:9]
+    faces = 3 + sum(has_b)
+    edges = unpack_faces(refs[9 : 9 + faces], has_b)
+    ops_ref, residual_ref, direction_ref = refs[9 + faces : 12 + faces]
+    faces_out = unpack_faces(refs[12 + faces : 12 + 2 * faces], has_b)
+    held, sem = refs[12 + 2 * faces : -1], refs[-1]
     tx_ref, ty_ref, tz_ref, pore_ref = held
     copies = start_copies(zip(sources, held + (residual_ref,)), sem)
     columns, size_x, size_y, size_z, slots = dims
     lines = size_x * size_y
     line = lax.broadcasted_iota(jnp.int32, (lines, size_z), 0)
     lane = lax.broadcasted_iota(jnp.int32, (lines, size_z), 1)
-    last = [par_ref[3 + i] == 1 for i in range(3)]
+    last = [lax.axis_index(axis) == lax.axis_size(axis) - 1 for axis in AXES]
+    even = even_places()
     in_y = line % size_y
     for copy in copies[:4]:
         copy.wait()
     upper_x = jnp.where((line >= lines - size_y) & last[0], 0.0, tx_ref[...])
     upper_y = jnp.where((in_y == size_y - 1) & last[1], 0.0, ty_ref[...])
     upper_z = jnp.where((lane == size_z - 1) & last[2], 0.0, tz_ref[...])
-    lower_x = jnp.concatenate([ex_ref[...], upper_x[: lines - size_y]], axis=0)
+    behind = []
+    for i in range(3):
+        came = edges[2 * i][...]
+        if edges[2 * i + 1] is not None:
+            came = jnp.where(even[i], edges[2 * i + 1][...], came)
+        behind.append(jnp.where(lax.axis_index(AXES[i]) == 0, 0.0, came))
+    lower_x = jnp.concatenate([behind[0], upper_x[: lines - size_y]], axis=0)
     edge_y = jnp.concatenate(
-        [jnp.broadcast_to(ey_ref[i : i + 1, :], (size_y, size_z)) for i in range(size_x)], axis=0
+        [jnp.broadcast_to(behind[1][i : i + 1, :], (size_y, size_z)) for i in range(size_x)], axis=0
     )
     lower_y = jnp.where(in_y == 0, edge_y, pltpu.roll(upper_y, 1, 0))
-    lower_z = jnp.where(lane == 0, jnp.broadcast_to(ez_ref[...], (8, lines)).T[:, 0:1], pltpu.roll(upper_z, 1, 1))
+    lower_z = jnp.where(lane == 0, jnp.broadcast_to(behind[2], (8, lines)).T[:, 0:1], pltpu.roll(upper_z, 1, 1))
     total = recv_ref.shape[1]
     cell = recv_ref[...]
     hot_line = jnp.broadcast_to(cell // size_z, (lines, total)) == lax.broadcasted_iota(
@@ -205,32 +229,31 @@
     copies[4].wait()
     for c in range(columns):
         direction_ref[c] = residual_ref[c] * inverse
-    emit_faces(direction_ref, par_ref, faces_out, dims)
+    emit_faces(direction_ref, faces_out, dims)
 
 
 def unpack_faces(refs, has_b):
     refs = list(refs)
-    x_a = refs.pop(0)
-    x_b = refs.pop(0) if has_b[0] else None
-    return x_a, x_b, refs.pop(0), refs.pop(0)
-
-
-def stencil_kernel(dims, has_b, *refs):
+    faces = []
+    for more in has_b:
+        faces += [refs.pop(0), refs.pop(0) if more else None]
+    return faces
+
+
+def stencil_kernel(dims, has_b, first_round, *refs):
     refs = list(refs)
     columns, size_x, size_y, size_z, slots = dims
-    par_ref, ops_ref, residual_ref, direction_ref = refs[:4]
-    refs = refs[4:]
-    xa_ref = refs.pop(0)
-    xb_ref = refs.pop(0) if has_b[0] else xa_ref
-    ya_ref = refs.pop(0)
-    yb_ref = refs.pop(0) if has_b[1] else ya_ref
-    y_b_at = size_x if has_b[1] else 0
-    za_ref = refs.pop(0)
-    zb_ref = refs.pop(0) if has_b[2] else za_ref
-    (residual_out,) = refs
-    lines = size_x * size_y
-    even = [par_ref[i] == 0 for i in range(3)]
-    z_a, z_b = za_ref[0:1, :], zb_ref[1:2, :] if has_b[2] else za_ref[0:1, :]
+    ops_ref, residual_ref, direction_ref = refs[:3]
+    refs = refs[3:]
+    solution_out, residual_out = refs.pop(), refs.pop()
+    solution_ref = None if first_round else refs.pop()
+    xa_ref, xb_ref, ya_ref, yb_ref, za_ref, zb_ref = unpack_faces(refs, has_b)
+    xb_ref = xa_ref if xb_ref is None else xb_ref
+    yb_ref = ya_ref if yb_ref is None else yb_ref
+    zb_ref = za_ref if zb_ref is None else zb_ref
+    lines = size_x * size_y
+    even = even_places()
+    z_a, z_b = za_ref[...], zb_ref[...]
     z_rows = jnp.concatenate(
         [jnp.where(even[2], z_b, z_a), jnp.where(even[2], z_a, z_b), jnp.zeros((6, columns * lines), F32)],
         axis=0,
@@ -239,16 +262,16 @@
     in_y = lax.broadcasted_iota(jnp.int32, (lines, size_z), 0) % size_y
     lane = lax.broadcasted_iota(jnp.int32, (lines, size_z), 1)
 
-    def rows_of(ref, at, c):
+    def rows_of(ref, c):
         return jnp.concatenate(
-            [jnp.broadcast_to(ref[at + i, c : c + 1, :], (size_y, size_z)) for i in range(size_x)], axis=0
+            [jnp.broadcast_to(ref[i, c : c + 1, :], (size_y, size_z)) for i in range(size_x)], axis=0
         )
 
     for c in range(columns):
         value = direction_ref[c]
         x_low = jnp.where(even[0], xb_ref[c], xa_ref[c])
         x_high = jnp.where(even[0], xa_ref[c], xb_ref[c])
-        y_a, y_b = rows_of(ya_ref, 0, c), rows_of(yb_ref, y_b_at, c)
+        y_a, y_b = rows_of(ya_ref, c), rows_of(yb_ref, c)
         y_low = jnp.where(even[1], y_b, y_a)
         y_high = jnp.where(even[1], y_a, y_b)
         z_low = z_cols[c * lines : (c + 1) * lines, 0:1]
@@ -260,21 +283,20 @@
         beside += ops_ref[4] * jnp.where(lane == size_z - 1, z_high, pltpu.roll(value, size_z - 1, 1))
         beside += ops_ref[5] * jnp.where(lane == 0, z_low, pltpu.roll(value, 1, 1))
         residual_out[c] = residual_ref[c] - (ops_ref[6] * value - beside)
-
-
-def update_kernel(dims, has_b, keep, gain, first_round, last_round, early, *refs):
+        solution_out[c] = value if first_round else solution_ref[c] + value
+
+
+def update_kernel(dims, has_b, keep, gain, last_round, early, *refs):
     refs = list(refs)
     columns, size_x, size_y, size_z, slots = dims
     extra, comes = early
-    par_ref, ops_ref, residual_ref, direction_ref, recv_ref, weight_ref, arrived_ref = refs[:7]
-    refs = refs[7:]
-    solution_ref = direction_ref if first_round else refs.pop(0)
+    ops_ref, residual_ref, direction_ref, recv_ref, weight_ref, arrived_ref = refs[:6]
+    refs = refs[6:]
     if last_round:
-        well_ref, basis_source, sums_out, flat_out, landed_ref, solution_out, basis_ref, sem = refs
+        solution_ref, well_ref, basis_source, sums_out, flat_out, landed_ref, solution_out, basis_ref, sem = refs
         (basis_copy,) = start_copies([(basis_source, basis_ref)], sem)
     else:
         landed_ref = refs.pop()
-        solution_out = refs.pop(0)
     table_out = refs.pop(0) if comes else None
     if not last_round:
         residual_out, direction_out = refs[:2]
@@ -282,26 +304,20 @@
     lines = size_x * size_y
     rows = columns * slots // LANES
     total = recv_ref.shape[1]
-    cell = recv_ref[...]
-    hot_line = jnp.broadcast_to(cell // size_z, (lines, total)) == lax.broadcasted_iota(
-        jnp.int32, (lines, total), 0
-    )
-    hot_lane = jnp.broadcast_to(cell % size_z, (size_z, total)) == lax.broadcasted_iota(
-        jnp.int32, (size_z, total), 0
-    )
-    hot_line = jnp.where(hot_line, 1.0, 0.0).astype(BF16)
-    hot_lane = jnp.where(hot_lane, 1.0, 0.0).astype(BF16)
+    half = lines // 2
+    hot_row, hot_key = one_hots(recv_ref[...], lines, size_z)
+    hot_row = jnp.where(hot_row, 1.0, 0.0).astype(BF16)
     tiles = []
     devices = total // slots
     if comes:
         per_device = rows + extra
         for i in range(devices):
-            landed_ref[i * rows : (i + 1) * rows, :] = arrived_ref[i * per_device : i * per_device + rows, :]
+            landed_ref[i * rows : (i + 1) * rows, :LANES] = arrived_ref[i * per_device : i * per_device + rows, :]
         source_ref = landed_ref
     else:
         source_ref = arrived_ref
     for j in range(total // LANES):
-        tiles.append(regroup(source_ref[j * columns : (j + 1) * columns, :], rows, slots))
+        tiles.append(regroup(source_ref[j * columns : (j + 1) * columns, :LANES], rows, slots))
     if comes == "parts":
         added = arrived_ref[rows : rows + extra, :]
         for i in range(1, devices):
@@ -313,17 +329,19 @@
             at = i * per_device + rows
             table_out[i * extra : (i + 1) * extra, :] = arrived_ref[at : at + extra, :]
     weighted = (jnp.concatenate(tiles, axis=1) * weight_ref[...]).astype(BF16)
-    spread = weighted[:, None, :] * hot_line[None, :, :]
-    landed_ref[...] = nt_dot(spread.reshape(columns * lines, total), hot_lane)
+    spread = weighted[:, None, :] * hot_row[None, :, :]
+    landed_ref[...] = nt_dot(spread.reshape(columns * half, total), hot_key)
     for c in range(columns):
-        left = residual_ref[c] + landed_ref[c * lines : (c + 1) * lines, :]
+        landed = landed_ref[c * half : (c + 1) * half, :]
+        left = residual_ref[c] + jnp.concatenate([landed[:, :size_z], landed[:, size_z:]], axis=0)
         after = keep * direction_ref[c] + gain * (left * ops_ref[7])
-        solution_out[c] = solution_ref[c] + after
-        if not last_round:
+        if last_round:
+            solution_out[c] = solution_ref[c] + after
+        else:
             residual_out[c] = left
             direction_out[c] = after
     if not last_round:
-        emit_faces(direction_out, par_ref, faces_out, dims)
+        emit_faces(direction_out, faces_out, dims)
     else:
         basis_copy.wait()
         sums_of(dims, solution_out, basis_ref, well_ref, flat_out, sums_out)
@@ -336,25 +354,35 @@
     wells = well_ref.shape[1]
     side = 16
     groups = [pl.ds(first, side) for first in range(0, count, side)]
-    copies = start_copies([(source_ref.at[g], basis_ref.at[g]) for g in groups], sem)
+    copies = [pltpu.make_async_copy(source_ref.at[g], basis_ref.at[g], sem.at[i]) for i, g in enumerate(groups)]
+    ahead = 4
+    for copy in copies[:ahead]:
+        copy.start()
     row = lax.broadcasted_iota(jnp.int32, (side * side, side * side), 0)
     lane = lax.broadcasted_iota(jnp.int32, (side * side, side * side), 1)
     turn = jnp.where((row % side == lane // side) & (row // side == lane % side), 1.0, 0.0).astype(BF16)
     stores = []
-    for index, first in enumerate(range(0, count, side)):
-        copies[index].wait()
+    for index in range(0, len(groups), 2):
+        for i in (index, index + 1):
+            copies[i].wait()
+            if i + ahead < len(copies):
+                copies[i + ahead].start()
+        first = index * side
         for begin in range(0, lines, side):
-            tile = basis_ref[first : first + side, begin : begin + side, :].reshape(side * side, size_z)
-            tile = jnp.dot(turn, tile, preferred_element_type=F32).astype(BF16)
+            tile = [
+                basis_ref[at : at + side, begin : begin + side, :].reshape(side * side, size_z)
+                for at in (first, first + side)
+            ]
+            tile = jnp.dot(turn, jnp.concatenate(tile, axis=1), preferred_element_type=F32).astype(BF16)
             for i in range(side):
                 lanes = slice((begin + i) * size_z, (begin + i + 1) * size_z)
-                flat_out[first : first + side, lanes] = tile[i * side : (i + 1) * side, :]
-        stores.append(
-            pltpu.make_async_copy(
-                flat_out.at[groups[index]], flat_target.at[groups[index]], out_sem.at[index]
+                flat_out[first : first + side, lanes] = tile[i * side : (i + 1) * side, :size_z]
+                flat_out[first + side : first + 2 * side, lanes] = tile[i * side : (i + 1) * side, size_z:]
+        for i in (index, index + 1):
+            stores.append(
+                pltpu.make_async_copy(flat_out.at[groups[i]], flat_target.at[groups[i]], out_sem.at[i])
             )
-        )
-        stores[-1].start()
+            stores[-1].start()
     cell = well_ref[...]
     lane_of = jnp.broadcast_to(lax.rem(cell + size_z, size_z), (size_z, wells))
     lane_of = lane_of == lax.broadcasted_iota(jnp.int32, (size_z, wells), 0)
@@ -526,10 +554,6 @@
     has_b = tuple(size > 2 for size in sizes)
     dims = (columns, size_x, size_y, size_z, slots)
     rows = columns * slots // LANES
-    index = [index_x, index_y, index_z]
-    par = jnp.stack(
-        [i % 2 for i in index] + [(i == n - 1).astype(jnp.int32) for i, n in zip(index, sizes)]
-    )
 
     vmem = pl.BlockSpec(memory_space=pltpu.VMEM)
     smem = pl.BlockSpec(memory_space=pltpu.SMEM)
@@ -537,12 +561,9 @@
     wide_params = pltpu.CompilerParams(vmem_limit_bytes=16 * 2**20 + 4096 * total)
     field_type = jax.ShapeDtypeStruct((columns, lines, size_z), F32)
     x_type = jax.ShapeDtypeStruct((columns, size_y, size_z), F32)
-    y_type = jax.ShapeDtypeStruct((2 * size_x, columns, size_z), F32)
-    face_types = (
-        [x_type] * (1 + has_b[0])
-        + [y_type]
-        + [jax.ShapeDtypeStruct((2, columns * lines), F32)]
-    )
+    y_type = jax.ShapeDtypeStruct((size_x, columns, size_z), F32)
+    z_type = jax.ShapeDtypeStruct((1, columns * lines), F32)
+    face_types = [x_type] * (1 + has_b[0]) + [y_type] * (1 + has_b[1]) + [z_type] * (1 + has_b[2])
 
     def in_hbm(*values):
         return [pltpu.with_memory_space_constraint(value, pltpu.HBM) for value in values]
@@ -566,7 +587,9 @@
         compiler_params=params,
         name="edges",
     )(*in_hbm(*trans, fault_send, fault_recv, fault_trans))
-    edge_x, edge_y, edge_z = from_behind(edge_x, "gx"), from_behind(edge_y, "gy"), from_behind(edge_z, "gz")
+    edges = []
+    for axis, edge, more in zip(AXES, (edge_x, edge_y, edge_z), has_b):
+        edges += [swap_even(edge, axis)] + ([swap_odd(edge, axis)] if more else [])
 
     def gather(direction, goes="", source=()):
         sent_rows = devices * (rows + (extra if goes else 0))
@@ -583,38 +606,44 @@
         )(direction, send, *source)
 
     def transfers(faults, faces):
-        *x_faces, y_ab, z_ab = faces
-        y_first, z_first = swap(y_ab, "gy", False), swap(z_ab, "gz", False)
-        came = [swap(face, "gx", odd) for face, odd in zip(x_faces, (False, True))]
-        faults, y_first, z_first = lax.optimization_barrier((faults, y_first, z_first))
-        arrived = exchange(faults)
-        return arrived, came + swap_rest(y_ab, y_first, "gy") + swap_rest(z_ab, z_first, "gz")
-
-    def stencil(residual, direction, came):
+        faces = list(faces)
+        came = []
+        for axis, more in zip(AXES, has_b):
+            came.append(swap_even(faces.pop(0), axis))
+            if more:
+                came.append(swap_odd(faces.pop(0), axis))
+        first = [1 + has_b[0], 2 + has_b[0] + has_b[1]]
+        faults, came[first[0]], came[first[1]] = lax.optimization_barrier(
+            (faults, came[first[0]], came[first[1]])
+        )
+        return exchange(faults), came
+
+    def stencil(residual, direction, came, solution):
+        more = [] if solution is None else [solution]
         return pl.pallas_call(
-            functools.partial(stencil_kernel, dims, has_b),
-            out_shape=field_type,
-            in_specs=[smem] + [vmem] * (3 + len(came)),
-            out_specs=vmem,
-            input_output_aliases={2: 0},
+            functools.partial(stencil_kernel, dims, has_b, solution is None),
+            out_shape=[field_type, field_type],
+            in_specs=[vmem] * (3 + len(came) + len(more)),
+            out_specs=[vmem] * 2,
+            input_output_aliases={1: 0, 3 + len(came): 1} if more else {1: 0},
             compiler_params=params,
             cost_estimate=pl.CostEstimate(
                 flops=20 * columns * cells, bytes_accessed=12 * columns * cells, transcendentals=0
             ),
             name="stencil",
-        )(par, ops, residual, direction, *came)
+        )(ops, residual, direction, *came, *more)
 
     ops, residual, direction, *faces = pl.pallas_call(
         functools.partial(setup_kernel, dims, has_b),
         out_shape=[jax.ShapeDtypeStruct((8, lines, size_z), F32), field_type, field_type] + face_types,
-        in_specs=[smem] * 3 + [vmem] * 5 + [anywhere] * 5,
+        in_specs=[smem] * 2 + [vmem] * 2 + [anywhere] * 5 + [vmem] * len(edges),
         out_specs=[vmem] * (3 + len(face_types)),
         scratch_shapes=[pltpu.VMEM(shape2, F32)] * 4 + [pltpu.SemaphoreType.DMA((5,))],
         compiler_params=params,
         name="setup",
     )(
-        par, shift_table, shift_index, edge_x, edge_y, edge_z, recv, weight,
-        *in_hbm(*trans, pore_volume.reshape(shape2), start),
+        shift_table, shift_index, recv, weight,
+        *in_hbm(*trans, pore_volume.reshape(shape2), start), *edges,
     )
     plane = full_y * full_z
     well_x = well_cells // plane
@@ -663,28 +692,26 @@
         goes = {2: "parts", 3: "sums"}.get(number, "")
         faults = gather(direction, goes, [parts] if goes == "parts" else [table] if goes else [])
         arrived, came = transfers(faults, faces)
-        residual = stencil(residual, direction, came)
+        residual, solution = stencil(residual, direction, came, solution)
         weight_new = 1.0 / (2.0 * sigma - weight_now)
         last_round = number == TERMS - 2
         body = functools.partial(
             update_kernel, dims, has_b, weight_new * weight_now, 2.0 * weight_new / 0.9,
-            number == 0, last_round, (extra, goes),
+            last_round, (extra, goes),
         )
         weight_now = weight_new
-        scratch = [pltpu.VMEM((columns * lines, size_z), F32)]
-        out_types = [sums_type, flat_type] if last_round else [field_type]
+        scratch = [pltpu.VMEM((columns * lines // 2, 2 * size_z), F32)]
+        out_types = [sums_type, flat_type] if last_round else []
         if goes:
             table_rows = extra if goes == "parts" else devices * extra
             out_types.append(jax.ShapeDtypeStruct((table_rows, LANES), F32))
-        operands = [par, ops, residual, direction, recv, weight, arrived]
+        operands = [ops, residual, direction, recv, weight, arrived]
         aliases = {}
-        if number:
-            if not last_round:
-                aliases[len(operands)] = 0
+        if last_round:
             operands.append(solution)
-        in_specs = [smem] + [vmem] * (len(operands) - 1)
+        in_specs = [vmem] * len(operands)
         if not last_round:
-            aliases[2], aliases[3] = len(out_types), len(out_types) + 1
+            aliases[1], aliases[2] = len(out_types), len(out_types) + 1
             out_types += [field_type, field_type] + face_types
         else:
             operands += [well_local, *in_hbm(flat_basis)]
@@ -707,7 +734,6 @@
         if last_round:
             sums, flat = outs
             break
-        solution, *outs = outs
         if goes:
             table, *outs = outs
         residual, direction, *faces = outs

time: 194 us -> 171 us (0.88)
  starting transfers between devices: 86.1 us -> 66.9 us
  Pallas kernels: 51.3 us -> 41.9 us
  waiting for transfers between devices: 30.5 us -> 37.2 us
    ppermute x38 -> x40, starting transfers between devices: 57.6 us -> 40.7 us  [the longest x24 25.6 us: swap_even(): return lax.ppermute(value, axis, pairs)]
    all_to_all x7, waiting for transfers between devices: 0.02 us -> 6.57 us  [exchange(): return lax.all_to_all(value, AXES, split_axis=0, concat_axis=0, tiled=True)]
    pallas_call x7, Pallas kernels: 15 us -> 11.1 us  [local(): pl.pallas_call(body, out_shape=out_types, in_specs=in_specs, out_specs=[v...]
    pallas_call x7, Pallas kernels: 11 us -> 8.04 us  [stencil(): pl.pallas_call(functools.partial(stencil_kernel, dims, has_b, solution is...]
    all_to_all x7, starting transfers between devices: 28.5 us -> 26.2 us  [exchange(): return lax.all_to_all(value, AXES, split_axis=0, concat_axis=0, tiled=True)]
    pallas_call x7, Pallas kernels: 9.2 us -> 7.21 us  [gather(): pl.pallas_call(functools.partial(gather_kernel, dims, (extra, goes)), out...]
    ppermute x38 -> x40, waiting for transfers between devices: 30.5 us -> 30.6 us  [the longest x16 23.9 us: swap_odd(): return lax.ppermute(value, names, pairs)]
  transfers between devices with their start and end apart: 45 -> 47, of which waited for: 12 -> 18; matrix products, arithmetic and copies ran while one was open for 0% -> 0% of each run, Pallas kernels for 15% -> 13%
where the time goes in v1:
time: 171 us; the launch traced here: 170 us
  starting transfers between devices  66.9 us (39%)
  Pallas kernels  41.9 us (25%)
  waiting for transfers between devices  37.2 us (22%)
  blocking collectives  20 us (12%)
  local copies, waits for them, and re-layouts  2.27 us (1%)
  between operations  1.74 us (1%)
    all_to_all x7, starting transfers between devices, exchange(): return lax.all_to_all(value, AXES, split_axis=0, concat_axis=0, tiled=True)  26.2 us
    ppermute x24, starting transfers between devices, swap_even(): return lax.ppermute(value, axis, pairs)  25.6 us
    ppermute x16, waiting for transfers between devices, swap_odd(): return lax.ppermute(value, names, pairs)  23.9 us
    all_to_all x2, blocking collectives, exchange(): return lax.all_to_all(value, AXES, split_axis=0, concat_axis=0, tiled=True)  20 us
    ppermute x16, starting transfers between devices, swap_odd(): return lax.ppermute(value, names, pairs)  15.1 us
    pallas_call x7, Pallas kernels, local(): pl.pallas_call(body, out_shape=out_types, in_specs=in_specs, out_specs=[v...  11.1 us
    pallas_call x7, Pallas kernels, stencil(): pl.pallas_call(functools.partial(stencil_kernel, dims, has_b, solution is...  8.04 us
    pallas_call x1, Pallas kernels, local(): pl.pallas_call(functools.partial(basis_kernel, dims), out_shape=[jax.Shap...  7.56 us
  transfers between devices with their start and end apart: 47, of which 18 were waited for; matrix products, arithmetic and copies ran while one was open for 0% of the time, Pallas kernels for 13%

profile of v1, /device:TPU:0, one launch (start us, length us, event | category | flops | bytes accessed | tf_op | source)
XLA Modules:
  0.0 170.0 jit_solution(330834169465150288)
XLA Ops:
  1.7 3.0 %collective-permute-start = (f32[16,128]{1,0:T(8,128)S(1)}, f32[16,128]{1,0:T(8,128)S(1)}, u32[]{:S(2)}, u32[]{:S(2)}) collective-permute-start(f32[16,128]{1,0:T(8,128)S(1)} %get-tuple-element.107), channel_id=1, source_target_pairs={{0,16},{16,0},{1,17},{17,1},{2,18},{18,2},{3,19},{19,3},{4,20},{20... | collective-permute-start | bytes 24584 | tf_op jit(solution)/shard_map/ppermute | solution.py:21
  6.9 2.6 %collective-permute-start.3 = (f32[1,64]{1,0:T(1,128)S(1)}, f32[1,64]{1,0:T(1,128)S(1)}, u32[]{:S(2)}, u32[]{:S(2)}) collective-permute-start(f32[1,64]{1,0:T(1,128)S(1)} %get-tuple-element.109), channel_id=1, source_target_pairs={{0,1},{1,0},{2,3},{3,2},{4,5},{5,4},{6,7},{7,6},{8,9},{9,8},{10,11... | collective-permute-start | bytes 776 | tf_op jit(solution)/shard_map/ppermute | solution.py:21
  13.7 2.1 %collective-permute-start.7 = (f32[1,1024]{1,0:T(1,128)S(1)}, f32[1,1024]{1,0:T(1,128)S(1)}, u32[]{:S(2)}, u32[]{:S(2)}) collective-permute-start(f32[1,1024]{1,0:T(1,128)S(1)} %get-tuple-element.116), channel_id=1, source_target_pairs={{0,1},{1,0},{2,3},{3,2},{4,5},{5,4},{6,7},{7,6},{8,9},{9,8},{10,11... | collective-permute-start | bytes 12296 | tf_op jit(solution)/shard_map/ppermute | solution.py:21
  17.5 4.1 %all-to-all-start = ((f32[32,4,128]{2,1,0:T(4,128)}), f32[32,4,128]{2,1,0:T(4,128)S(1)}, u32[]{:S(2)}, u32[]{:S(2)}) async-start(f32[32,4,128]{2,1,0:T(4,128)} %bitcast.5), calls=%async_computation | async-start | bytes 131072 | tf_op jit(solution)/shard_map/all_to_all | solution.py:45
  23.7 3.3 %collective-permute-done.9.refs_7_ = f32[1,1024]{1,0:T(1,128)S(1)} collective-permute-done((f32[1,1024]{1,0:T(1,128)S(1)}, f32[1,1024]{1,0:T(1,128)S(1)}, u32[]{:S(2)}, u32[]{:S(2)}) %collective-permute-start.9) | collective-permute-done | bytes 4128 | tf_op jit(solution)/shard_map/ppermute | solution.py:41
  33.9 3.3 %all-to-all-start.1 = ((f32[32,4,128]{2,1,0:T(4,128)}), f32[32,4,128]{2,1,0:T(4,128)S(1)}, u32[]{:S(2)}, u32[]{:S(2)}) async-start(f32[32,4,128]{2,1,0:T(4,128)} %bitcast.7), calls=%async_computation.1 | async-start | bytes 131072 | tf_op jit(solution)/shard_map/all_to_all | solution.py:45
  39.4 7.6 %basis_gram.1 = (f32[512,128]{1,0:T(8,128)S(1)}, bf16[256,8192]{1,0:T(8,128)(2,1)}) custom-call(s32[1,64]{1,0:T(1,128)S(1)} %fusion.4.well_ref.refs_7_, bf16[256,64,128]{2,1,0:T(8,128)(2,1)} %bitcast.39), custom_call_target="tpu_custom_call" | custom-call | flops 1342177280 | bytes 8388608 | tf_op jit(solution)/shard_map/basis_gram/pallas_call | solution.py:665
  49.4 2.7 %collective-permute-start.17 = (f32[1,1024]{1,0:T(1,128)S(1)}, f32[1,1024]{1,0:T(1,128)S(1)}, u32[]{:S(2)}, u32[]{:S(2)}) collective-permute-start(f32[1,1024]{1,0:T(1,128)S(1)} %get-tuple-element.140), channel_id=1, source_target_pairs={{0,1},{1,0},{2,3},{3,2},{4,5},{5,4},{6,7},{7,6},{8,9},{9,8},{10,11... | collective-permute-start | bytes 12296 | tf_op jit(solution)/shard_map/ppermute | solution.py:21
  54.5 4.2 %all-to-all-start.2 = ((f32[32,20,128]{2,1,0:T(8,128)}), f32[32,20,128]{2,1,0:T(8,128)S(1)}, u32[]{:S(2)}, u32[]{:S(2)}) async-start(f32[32,20,128]{2,1,0:T(8,128)} %all_to_all.66), calls=%async_computation.2 | async-start | bytes 786432 | tf_op jit(solution)/shard_map/all_to_all | solution.py:45
  62.6 5.4 %collective-permute-done.19.refs_7_ = f32[1,1024]{1,0:T(1,128)S(1)} collective-permute-done((f32[1,1024]{1,0:T(1,128)S(1)}, f32[1,1024]{1,0:T(1,128)S(1)}, u32[]{:S(2)}, u32[]{:S(2)}) %collective-permute-start.19) | collective-permute-done | bytes 4128 | tf_op jit(solution)/shard_map/ppermute | solution.py:41
  71.7 2.3 %collective-permute-start.22 = (f32[1,1024]{1,0:T(1,128)S(1)}, f32[1,1024]{1,0:T(1,128)S(1)}, u32[]{:S(2)}, u32[]{:S(2)}) collective-permute-start(f32[1,1024]{1,0:T(1,128)S(1)} %get-tuple-element.153), channel_id=1, source_target_pairs={{0,1},{1,0},{2,3},{3,2},{4,5},{5,4},{6,7},{7,6},{8,9},{9,8},{10,11... | collective-permute-start | bytes 12296 | tf_op jit(solution)/shard_map/ppermute | solution.py:21
  76.3 4.1 %all-to-all-start.3 = ((f32[32,20,128]{2,1,0:T(8,128)}), f32[32,20,128]{2,1,0:T(8,128)S(1)}, u32[]{:S(2)}, u32[]{:S(2)}) async-start(f32[32,20,128]{2,1,0:T(8,128)} %all_to_all.69), calls=%async_computation.3 | async-start | bytes 786432 | tf_op jit(solution)/shard_map/all_to_all | solution.py:45
  84.3 5.4 %collective-permute-done.24.refs_7_ = f32[1,1024]{1,0:T(1,128)S(1)} collective-permute-done((f32[1,1024]{1,0:T(1,128)S(1)}, f32[1,1024]{1,0:T(1,128)S(1)}, u32[]{:S(2)}, u32[]{:S(2)}) %collective-permute-start.24) | collective-permute-done | bytes 4128 | tf_op jit(solution)/shard_map/ppermute | solution.py:41
  93.5 2.3 %collective-permute-start.27 = (f32[1,1024]{1,0:T(1,128)S(1)}, f32[1,1024]{1,0:T(1,128)S(1)}, u32[]{:S(2)}, u32[]{:S(2)}) collective-permute-start(f32[1,1024]{1,0:T(1,128)S(1)} %get-tuple-element.165), channel_id=1, source_target_pairs={{0,1},{1,0},{2,3},{3,2},{4,5},{5,4},{6,7},{7,6},{8,9},{9,8},{10,11... | collective-permute-start | bytes 12296 | tf_op jit(solution)/shard_map/ppermute | solution.py:21
  98.4 3.1 %all-to-all-start.4 = ((f32[32,4,128]{2,1,0:T(4,128)}), f32[32,4,128]{2,1,0:T(4,128)S(1)}, u32[]{:S(2)}, u32[]{:S(2)}) async-start(f32[32,4,128]{2,1,0:T(4,128)} %bitcast.11), calls=%async_computation.4 | async-start | bytes 131072 | tf_op jit(solution)/shard_map/all_to_all | solution.py:45
  103.6 3.3 %collective-permute-done.29.refs_7_ = f32[1,1024]{1,0:T(1,128)S(1)} collective-permute-done((f32[1,1024]{1,0:T(1,128)S(1)}, f32[1,1024]{1,0:T(1,128)S(1)}, u32[]{:S(2)}, u32[]{:S(2)}) %collective-permute-start.29) | collective-permute-done | bytes 4128 | tf_op jit(solution)/shard_map/ppermute | solution.py:41
  113.8 3.7 %all-to-all-start.5 = ((f32[32,4,128]{2,1,0:T(4,128)}), f32[32,4,128]{2,1,0:T(4,128)S(1)}, u32[]{:S(2)}, u32[]{:S(2)}) async-start(f32[32,4,128]{2,1,0:T(4,128)} %bitcast.13), calls=%async_computation.5 | async-start | bytes 131072 | tf_op jit(solution)/shard_map/all_to_all | solution.py:45
  119.6 3.1 %collective-permute-done.34.refs_7_ = f32[1,1024]{1,0:T(1,128)S(1)} collective-permute-done((f32[1,1024]{1,0:T(1,128)S(1)}, f32[1,1024]{1,0:T(1,128)S(1)}, u32[]{:S(2)}, u32[]{:S(2)}) %collective-permute-start.34) | collective-permute-done | bytes 4128 | tf_op jit(solution)/shard_map/ppermute | solution.py:41
  129.5 3.5 %all-to-all-start.6 = ((f32[32,4,128]{2,1,0:T(4,128)}), f32[32,4,128]{2,1,0:T(4,128)S(1)}, u32[]{:S(2)}, u32[]{:S(2)}) async-start(f32[32,4,128]{2,1,0:T(4,128)} %bitcast.15), calls=%async_computation.6 | async-start | bytes 131072 | tf_op jit(solution)/shard_map/all_to_all | solution.py:45
  135.1 3.3 %collective-permute-done.39.refs_7_ = f32[1,1024]{1,0:T(1,128)S(1)} collective-permute-done((f32[1,1024]{1,0:T(1,128)S(1)}, f32[1,1024]{1,0:T(1,128)S(1)}, u32[]{:S(2)}, u32[]{:S(2)}) %collective-permute-start.39) | collective-permute-done | bytes 4128 | tf_op jit(solution)/shard_map/ppermute | solution.py:41
  140.5 4.3 %update.13 = (f32[128,128]{1,0:T(8,128)S(1)}, f32[16,8192]{1,0:T(8,128)S(1)}) custom-call(f32[8,64,128]{2,1,0:T(8,128)S(1)} %get-tuple-element.110.refs_0_, f32[16,64,128]{2,1,0:T(8,128)S(1)} %get-tuple-element.195.refs_1_, f32[16,64,128]{2,1,0:T(8,128)S(1)} %get-tuple-element.186.refs_0_.refs_2_, s32[1,1024]{1,0:T(1,128)S(1)} %get-tuple-element.105.refs_2_.refs_3_, ...), custom_call_target="tpu_custom_call" | custom-call | tf_op jit(solution)/shard_map/update/pallas_call | solution.py:724
  144.9 10.8 %all_to_all.94 = f32[32,4,128]{2,1,0:T(4,128)S(1)} all-to-all(f32[32,4,128]{2,1,0:T(4,128)S(1)} %bitcast.30), channel_id=1, replica_groups=mesh['gx'=2,'gy'=4,'gz'=4] {'gx','gy','gz'}, dimensions={0} | all-to-all | bytes 131072 | tf_op jit(solution)/shard_map/all_to_all | solution.py:45
  155.7 9.2 %all_to_all.95 = f32[32,4,128]{2,1,0:T(4,128)S(1)} all-to-all(f32[32,4,128]{2,1,0:T(4,128)S(1)} %tile.2), channel_id=1, replica_groups=mesh['gx'=2,'gy'=4,'gz'=4] {'gx','gy','gz'}, dimensions={0} | all-to-all | bytes 131072 | tf_op jit(solution)/shard_map/all_to_all | solution.py:45
  164.9 4.9 %finish.1 = (f32[16,64,128]{2,1,0:T(8,128)}, f32[16,256]{1,0:T(8,128)}, f32[16,256]{1,0:T(8,128)}, f32[16,64]{1,0:T(8,128)}) custom-call(f32[128,128]{1,0:T(8,128)S(1)} %bitcast.25, f32[512,128]{1,0:T(8,128)S(1)} %get-tuple-element.200.table_ref, f32[16,8192]{1,0:T(8,128)S(1)} %get-tuple-element.201.flat_ref, ...), custom_call_target="tpu_custom_call" | custom-call | tf_op jit(solution)/shard_map/finish/pallas_call | solution.py:745
  (108 shorter events, 66.5 us)
Async XLA Ops:
  1.7 9.3 %collective-permute-start = (f32[16,128]{1,0:T(8,128)S(1)}, f32[16,128]{1,0:T(8,128)S(1)}, u32[]{:S(2)}, u32[]{:S(2)}) collective-permute-start(f32[16,128]{1,0:T(8,128)S(1)} %get-tuple-element.107), channel_id=1, source_target_pairs={{0,16},{16,0},{1,17},{17,1},{2,18},{18,2},{3,19},{19,3},{4,20},{20... | collective-permute-start | bytes 24584 | tf_op jit(solution)/shard_map/ppermute | solution.py:21
  4.7 6.3 %collective-permute-start.2 = (f32[4,128]{1,0:T(4,128)S(1)}, f32[4,128]{1,0:T(4,128)S(1)}, u32[]{:S(2)}, u32[]{:S(2)}) collective-permute-start(f32[4,128]{1,0:T(4,128)S(1)} %get-tuple-element.108), channel_id=1, source_target_pairs={{0,16},{4,8},{8,4},{12,28},{16,0},{20,24},{24,20},{28,12},{1,17},{... | collective-permute-start | bytes 6152 | tf_op jit(solution)/shard_map/ppermute | solution.py:41
  4.8 6.2 %collective-permute-start.1 = (f32[4,128]{1,0:T(4,128)S(1)}, f32[4,128]{1,0:T(4,128)S(1)}, u32[]{:S(2)}, u32[]{:S(2)}) collective-permute-start(f32[4,128]{1,0:T(4,128)S(1)} %get-tuple-element.108), channel_id=1, source_target_pairs={{0,4},{4,0},{8,12},{12,8},{1,5},{5,1},{9,13},{13,9},{2,6},{6,2},{1... | collective-permute-start | bytes 6152 | tf_op jit(solution)/shard_map/ppermute | solution.py:21
  15.8 11.3 %collective-permute-start.5 = (f32[16,16,128]{2,1,0:T(8,128)S(1)}, f32[16,16,128]{2,1,0:T(8,128)S(1)}, u32[]{:S(2)}, u32[]{:S(2)}) collective-permute-start(f32[16,16,128]{2,1,0:T(8,128)S(1)} %get-tuple-element.113), channel_id=1, source_target_pairs={{0,16},{16,0},{1,17},{17,1},{2,18},{18,2},{3,19},{19,3},{4,20},{20... | collective-permute-start | bytes 393224 | tf_op jit(solution)/shard_map/ppermute | solution.py:21
  17.5 11.6 %all-to-all-start = ((f32[32,4,128]{2,1,0:T(4,128)}), f32[32,4,128]{2,1,0:T(4,128)S(1)}, u32[]{:S(2)}, u32[]{:S(2)}) async-start(f32[32,4,128]{2,1,0:T(4,128)} %bitcast.5), calls=%async_computation | async-start | bytes 131072 | tf_op jit(solution)/shard_map/all_to_all | solution.py:45
  21.7 5.4 %collective-permute-start.8 = (f32[4,16,128]{2,1,0:T(8,128)S(1)}, f32[4,16,128]{2,1,0:T(8,128)S(1)}, u32[]{:S(2)}, u32[]{:S(2)}) collective-permute-start(f32[4,16,128]{2,1,0:T(8,128)S(1)} %get-tuple-element.118), channel_id=1, source_target_pairs={{0,16},{4,8},{8,4},{12,28},{16,0},{20,24},{24,20},{28,12},{1,17},{... | collective-permute-start | bytes 98312 | tf_op jit(solution)/shard_map/ppermute | solution.py:41
  32.0 15.0 %collective-permute-start.10 = (f32[16,16,128]{2,1,0:T(8,128)S(1)}, f32[16,16,128]{2,1,0:T(8,128)S(1)}, u32[]{:S(2)}, u32[]{:S(2)}) collective-permute-start(f32[16,16,128]{2,1,0:T(8,128)S(1)} %get-tuple-element.125), channel_id=1, source_target_pairs={{0,16},{16,0},{1,17},{17,1},{2,18},{18,2},{3,19},{19,3},{4,20},{20... | collective-permute-start | bytes 393224 | tf_op jit(solution)/shard_map/ppermute | solution.py:21
  33.9 14.3 %all-to-all-start.1 = ((f32[32,4,128]{2,1,0:T(4,128)}), f32[32,4,128]{2,1,0:T(4,128)S(1)}, u32[]{:S(2)}, u32[]{:S(2)}) async-start(f32[32,4,128]{2,1,0:T(4,128)} %bitcast.7), calls=%async_computation.1 | async-start | bytes 131072 | tf_op jit(solution)/shard_map/all_to_all | solution.py:45
  37.3 9.7 %collective-permute-start.14 = (f32[1,1024]{1,0:T(1,128)S(1)}, f32[1,1024]{1,0:T(1,128)S(1)}, u32[]{:S(2)}, u32[]{:S(2)}) collective-permute-start(f32[1,1024]{1,0:T(1,128)S(1)} %get-tuple-element.131), channel_id=1, source_target_pairs={{0,16},{1,2},{2,1},{3,19},{16,0},{17,18},{18,17},{19,3},{4,20},{5,... | collective-permute-start | bytes 12296 | tf_op jit(solution)/shard_map/ppermute | solution.py:41
  39.2 7.8 %collective-permute-start.13 = (f32[4,16,128]{2,1,0:T(8,128)S(1)}, f32[4,16,128]{2,1,0:T(8,128)S(1)}, u32[]{:S(2)}, u32[]{:S(2)}) collective-permute-start(f32[4,16,128]{2,1,0:T(8,128)S(1)} %get-tuple-element.129), channel_id=1, source_target_pairs={{0,16},{4,8},{8,4},{12,28},{16,0},{20,24},{24,20},{28,12},{1,17},{... | collective-permute-start | bytes 98312 | tf_op jit(solution)/shard_map/ppermute | solution.py:41
  54.5 16.1 %all-to-all-start.2 = ((f32[32,20,128]{2,1,0:T(8,128)}), f32[32,20,128]{2,1,0:T(8,128)S(1)}, u32[]{:S(2)}, u32[]{:S(2)}) async-start(f32[32,20,128]{2,1,0:T(8,128)} %all_to_all.66), calls=%async_computation.2 | async-start | bytes 786432 | tf_op jit(solution)/shard_map/all_to_all | solution.py:45
  58.7 9.2 %collective-permute-start.15 = (f32[16,16,128]{2,1,0:T(8,128)S(1)}, f32[16,16,128]{2,1,0:T(8,128)S(1)}, u32[]{:S(2)}, u32[]{:S(2)}) collective-permute-start(f32[16,16,128]{2,1,0:T(8,128)S(1)} %get-tuple-element.137), channel_id=1, source_target_pairs={{0,16},{16,0},{1,17},{17,1},{2,18},{18,2},{3,19},{19,3},{4,20},{20... | collective-permute-start | bytes 393224 | tf_op jit(solution)/shard_map/ppermute | solution.py:21
  60.5 7.4 %collective-permute-start.18 = (f32[4,16,128]{2,1,0:T(8,128)S(1)}, f32[4,16,128]{2,1,0:T(8,128)S(1)}, u32[]{:S(2)}, u32[]{:S(2)}) collective-permute-start(f32[4,16,128]{2,1,0:T(8,128)S(1)} %get-tuple-element.142), channel_id=1, source_target_pairs={{0,16},{4,8},{8,4},{12,28},{16,0},{20,24},{24,20},{28,12},{1,17},{... | collective-permute-start | bytes 98312 | tf_op jit(solution)/shard_map/ppermute | solution.py:41
  60.8 7.1 %collective-permute-start.19 = (f32[1,1024]{1,0:T(1,128)S(1)}, f32[1,1024]{1,0:T(1,128)S(1)}, u32[]{:S(2)}, u32[]{:S(2)}) collective-permute-start(f32[1,1024]{1,0:T(1,128)S(1)} %get-tuple-element.144), channel_id=1, source_target_pairs={{0,16},{1,2},{2,1},{3,19},{16,0},{17,18},{18,17},{19,3},{4,20},{5,... | collective-permute-start | bytes 12296 | tf_op jit(solution)/shard_map/ppermute | solution.py:41
  76.3 16.0 %all-to-all-start.3 = ((f32[32,20,128]{2,1,0:T(8,128)}), f32[32,20,128]{2,1,0:T(8,128)S(1)}, u32[]{:S(2)}, u32[]{:S(2)}) async-start(f32[32,20,128]{2,1,0:T(8,128)} %all_to_all.69), calls=%async_computation.3 | async-start | bytes 786432 | tf_op jit(solution)/shard_map/all_to_all | solution.py:45
  80.5 9.2 %collective-permute-start.20 = (f32[16,16,128]{2,1,0:T(8,128)S(1)}, f32[16,16,128]{2,1,0:T(8,128)S(1)}, u32[]{:S(2)}, u32[]{:S(2)}) collective-permute-start(f32[16,16,128]{2,1,0:T(8,128)S(1)} %get-tuple-element.150), channel_id=1, source_target_pairs={{0,16},{16,0},{1,17},{17,1},{2,18},{18,2},{3,19},{19,3},{4,20},{20... | collective-permute-start | bytes 393224 | tf_op jit(solution)/shard_map/ppermute | solution.py:21
  82.3 7.4 %collective-permute-start.23 = (f32[4,16,128]{2,1,0:T(8,128)S(1)}, f32[4,16,128]{2,1,0:T(8,128)S(1)}, u32[]{:S(2)}, u32[]{:S(2)}) collective-permute-start(f32[4,16,128]{2,1,0:T(8,128)S(1)} %get-tuple-element.155), channel_id=1, source_target_pairs={{0,16},{4,8},{8,4},{12,28},{16,0},{20,24},{24,20},{28,12},{1,17},{... | collective-permute-start | bytes 98312 | tf_op jit(solution)/shard_map/ppermute | solution.py:41
  82.6 7.1 %collective-permute-start.24 = (f32[1,1024]{1,0:T(1,128)S(1)}, f32[1,1024]{1,0:T(1,128)S(1)}, u32[]{:S(2)}, u32[]{:S(2)}) collective-permute-start(f32[1,1024]{1,0:T(1,128)S(1)} %get-tuple-element.157), channel_id=1, source_target_pairs={{0,16},{1,2},{2,1},{3,19},{16,0},{17,18},{18,17},{19,3},{4,20},{5,... | collective-permute-start | bytes 12296 | tf_op jit(solution)/shard_map/ppermute | solution.py:41
  95.7 11.2 %collective-permute-start.25 = (f32[16,16,128]{2,1,0:T(8,128)S(1)}, f32[16,16,128]{2,1,0:T(8,128)S(1)}, u32[]{:S(2)}, u32[]{:S(2)}) collective-permute-start(f32[16,16,128]{2,1,0:T(8,128)S(1)} %get-tuple-element.163), channel_id=1, source_target_pairs={{0,16},{16,0},{1,17},{17,1},{2,18},{18,2},{3,19},{19,3},{4,20},{20... | collective-permute-start | bytes 393224 | tf_op jit(solution)/shard_map/ppermute | solution.py:21
  98.4 10.6 %all-to-all-start.4 = ((f32[32,4,128]{2,1,0:T(4,128)}), f32[32,4,128]{2,1,0:T(4,128)S(1)}, u32[]{:S(2)}, u32[]{:S(2)}) async-start(f32[32,4,128]{2,1,0:T(4,128)} %bitcast.11), calls=%async_computation.4 | async-start | bytes 131072 | tf_op jit(solution)/shard_map/all_to_all | solution.py:45
  110.8 12.0 %collective-permute-start.30 = (f32[16,16,128]{2,1,0:T(8,128)S(1)}, f32[16,16,128]{2,1,0:T(8,128)S(1)}, u32[]{:S(2)}, u32[]{:S(2)}) collective-permute-start(f32[16,16,128]{2,1,0:T(8,128)S(1)} %get-tuple-element.175), channel_id=1, source_target_pairs={{0,16},{16,0},{1,17},{17,1},{2,18},{18,2},{3,19},{19,3},{4,20},{20... | collective-permute-start | bytes 393224 | tf_op jit(solution)/shard_map/ppermute | solution.py:21
  113.8 11.0 %all-to-all-start.5 = ((f32[32,4,128]{2,1,0:T(4,128)}), f32[32,4,128]{2,1,0:T(4,128)S(1)}, u32[]{:S(2)}, u32[]{:S(2)}) async-start(f32[32,4,128]{2,1,0:T(4,128)} %bitcast.13), calls=%async_computation.5 | async-start | bytes 131072 | tf_op jit(solution)/shard_map/all_to_all | solution.py:45
  126.6 11.9 %collective-permute-start.35 = (f32[16,16,128]{2,1,0:T(8,128)S(1)}, f32[16,16,128]{2,1,0:T(8,128)S(1)}, u32[]{:S(2)}, u32[]{:S(2)}) collective-permute-start(f32[16,16,128]{2,1,0:T(8,128)S(1)} %get-tuple-element.187), channel_id=1, source_target_pairs={{0,16},{16,0},{1,17},{17,1},{2,18},{18,2},{3,19},{19,3},{4,20},{20... | collective-permute-start | bytes 393224 | tf_op jit(solution)/shard_map/ppermute | solution.py:21
  129.5 11.0 %all-to-all-start.6 = ((f32[32,4,128]{2,1,0:T(4,128)}), f32[32,4,128]{2,1,0:T(4,128)S(1)}, u32[]{:S(2)}, u32[]{:S(2)}) async-start(f32[32,4,128]{2,1,0:T(4,128)} %bitcast.15), calls=%async_computation.6 | async-start | bytes 131072 | tf_op jit(solution)/shard_map/all_to_all | solution.py:45
  (25 other events, 120.2 us)

commit v2 on v1

--- a/solution.py
+++ b/solution.py
@@ -187,7 +187,7 @@
     last = [lax.axis_index(axis) == lax.axis_size(axis) - 1 for axis in AXES]
     even = even_places()
     in_y = line % size_y
-    for copy in copies[:4]:
+    for copy in copies[:-1]:
         copy.wait()
     upper_x = jnp.where((line >= lines - size_y) & last[0], 0.0, tx_ref[...])
     upper_y = jnp.where((in_y == size_y - 1) & last[1], 0.0, ty_ref[...])
@@ -219,14 +219,19 @@
     parts = [jnp.where(hot_line, part, 0.0).astype(BF16) for part in (high, middle, low)]
     summed = nt_dot(jnp.concatenate(parts, axis=0), jnp.where(hot_lane, 1.0, 0.0).astype(BF16))
     fault_diag = summed[:lines] + summed[lines : 2 * lines] + summed[2 * lines :]
-    shift = shifts_ref[which_ref[0]]
+    number = lax.broadcasted_iota(jnp.int32, shifts_ref.shape, 1)
+    shift = jnp.sum(jnp.where(number == which_ref[...], shifts_ref[...], 0.0), axis=1, keepdims=True)
     diagonal = (
         upper_x + lower_x + upper_y + lower_y + upper_z + lower_z + shift * pore_ref[...] + fault_diag
     )
     inverse = 1.0 / diagonal
-    for i, value in enumerate((upper_x, lower_x, upper_y, lower_y, upper_z, lower_z, diagonal, inverse)):
+    inner_y = jnp.where(in_y == size_y - 1, 0.0, upper_y), jnp.where(in_y == 0, 0.0, lower_y)
+    inner_z = jnp.where(lane == size_z - 1, 0.0, upper_z), jnp.where(lane == 0, 0.0, lower_z)
+    face_y = upper_y - inner_y[0] + (lower_y - inner_y[1])
+    face_z = upper_z - inner_z[0] + (lower_z - inner_z[1])
+    for i, value in enumerate((upper_x, lower_x, *inner_y, *inner_z, diagonal, inverse, face_y, face_z)):
         ops_ref[i] = value
-    copies[4].wait()
+    copies[-1].wait()
     for c in range(columns):
         direction_ref[c] = residual_ref[c] * inverse
     emit_faces(direction_ref, faces_out, dims)
@@ -247,41 +252,19 @@
     refs = refs[3:]
     solution_out, residual_out = refs.pop(), refs.pop()
     solution_ref = None if first_round else refs.pop()
-    xa_ref, xb_ref, ya_ref, yb_ref, za_ref, zb_ref = unpack_faces(refs, has_b)
-    xb_ref = xa_ref if xb_ref is None else xb_ref
-    yb_ref = ya_ref if yb_ref is None else yb_ref
-    zb_ref = za_ref if zb_ref is None else zb_ref
-    lines = size_x * size_y
-    even = even_places()
-    z_a, z_b = za_ref[...], zb_ref[...]
-    z_rows = jnp.concatenate(
-        [jnp.where(even[2], z_b, z_a), jnp.where(even[2], z_a, z_b), jnp.zeros((6, columns * lines), F32)],
-        axis=0,
-    )
-    z_cols = z_rows.T
-    in_y = lax.broadcasted_iota(jnp.int32, (lines, size_z), 0) % size_y
-    lane = lax.broadcasted_iota(jnp.int32, (lines, size_z), 1)
-
-    def rows_of(ref, c):
-        return jnp.concatenate(
-            [jnp.broadcast_to(ref[i, c : c + 1, :], (size_y, size_z)) for i in range(size_x)], axis=0
-        )
-
+    xa_ref, xb_ref = refs[0], refs[-1]
+    lines = size_x * size_y
+    even = lax.axis_index(AXES[0]) % 2 == 0
     for c in range(columns):
         value = direction_ref[c]
-        x_low = jnp.where(even[0], xb_ref[c], xa_ref[c])
-        x_high = jnp.where(even[0], xa_ref[c], xb_ref[c])
-        y_a, y_b = rows_of(ya_ref, c), rows_of(yb_ref, c)
-        y_low = jnp.where(even[1], y_b, y_a)
-        y_high = jnp.where(even[1], y_a, y_b)
-        z_low = z_cols[c * lines : (c + 1) * lines, 0:1]
-        z_high = z_cols[c * lines : (c + 1) * lines, 1:2]
+        x_low = jnp.where(even, xb_ref[c], xa_ref[c])
+        x_high = jnp.where(even, xa_ref[c], xb_ref[c])
         beside = ops_ref[0] * jnp.concatenate([value[size_y:], x_high], axis=0)
         beside += ops_ref[1] * jnp.concatenate([x_low, value[: lines - size_y]], axis=0)
-        beside += ops_ref[2] * jnp.where(in_y == size_y - 1, y_high, pltpu.roll(value, lines - 1, 0))
-        beside += ops_ref[3] * jnp.where(in_y == 0, y_low, pltpu.roll(value, 1, 0))
-        beside += ops_ref[4] * jnp.where(lane == size_z - 1, z_high, pltpu.roll(value, size_z - 1, 1))
-        beside += ops_ref[5] * jnp.where(lane == 0, z_low, pltpu.roll(value, 1, 1))
+        beside += ops_ref[2] * pltpu.roll(value, lines - 1, 0)
+        beside += ops_ref[3] * pltpu.roll(value, 1, 0)
+        beside += ops_ref[4] * pltpu.roll(value, size_z - 1, 1)
+        beside += ops_ref[5] * pltpu.roll(value, 1, 1)
         residual_out[c] = residual_ref[c] - (ops_ref[6] * value - beside)
         solution_out[c] = value if first_round else solution_ref[c] + value
 
@@ -292,6 +275,10 @@
     extra, comes = early
     ops_ref, residual_ref, direction_ref, recv_ref, weight_ref, arrived_ref = refs[:6]
     refs = refs[6:]
+    ya_ref, yb_ref, za_ref, zb_ref = unpack_faces(refs[: 2 + has_b[1] + has_b[2]], has_b[1:])
+    refs = refs[2 + has_b[1] + has_b[2] :]
+    yb_ref = ya_ref if yb_ref is None else yb_ref
+    zb_ref = za_ref if zb_ref is None else zb_ref
     if last_round:
         solution_ref, well_ref, basis_source, sums_out, flat_out, landed_ref, solution_out, basis_ref, sem = refs
         (basis_copy,) = start_copies([(basis_source, basis_ref)], sem)
@@ -331,9 +318,24 @@
     weighted = (jnp.concatenate(tiles, axis=1) * weight_ref[...]).astype(BF16)
     spread = weighted[:, None, :] * hot_row[None, :, :]
     landed_ref[...] = nt_dot(spread.reshape(columns * half, total), hot_key)
+    even = even_places()
+    in_slab = lax.broadcasted_iota(jnp.int32, (size_y, size_z), 0)
+    lane = lax.broadcasted_iota(jnp.int32, (lines, size_z), 1)
+    z_a, z_b = za_ref[...], zb_ref[...]
+    z_rows = [jnp.where(even[2], z_b, z_a), jnp.where(even[2], z_a, z_b), jnp.zeros((6, columns * lines), F32)]
+    z_cols = jnp.concatenate(z_rows, axis=0).T
     for c in range(columns):
         landed = landed_ref[c * half : (c + 1) * half, :]
         left = residual_ref[c] + jnp.concatenate([landed[:, :size_z], landed[:, size_z:]], axis=0)
+        beside_y = []
+        for i in range(size_x):
+            y_a, y_b = ya_ref[i, c : c + 1, :], yb_ref[i, c : c + 1, :]
+            y_low, y_high = jnp.where(even[1], y_b, y_a), jnp.where(even[1], y_a, y_b)
+            beside_y.append(jnp.where(in_slab < size_y // 2, y_low, y_high))
+        z_low = z_cols[c * lines : (c + 1) * lines, 0:1]
+        z_high = z_cols[c * lines : (c + 1) * lines, 1:2]
+        left = left + ops_ref[8] * jnp.concatenate(beside_y, axis=0)
+        left = left + ops_ref[9] * jnp.where(lane < size_z // 2, z_low, z_high)
         after = keep * direction_ref[c] + gain * (left * ops_ref[7])
         if last_round:
             solution_out[c] = solution_ref[c] + after
@@ -556,7 +558,6 @@
     rows = columns * slots // LANES
 
     vmem = pl.BlockSpec(memory_space=pltpu.VMEM)
-    smem = pl.BlockSpec(memory_space=pltpu.SMEM)
     params = pltpu.CompilerParams(vmem_limit_bytes=8 * 2**20 + 4096 * total)
     wide_params = pltpu.CompilerParams(vmem_limit_bytes=16 * 2**20 + 4096 * total)
     field_type = jax.ShapeDtypeStruct((columns, lines, size_z), F32)
@@ -607,16 +608,11 @@
 
     def transfers(faults, faces):
         faces = list(faces)
-        came = []
+        came = {}
         for axis, more in zip(AXES, has_b):
-            came.append(swap_even(faces.pop(0), axis))
-            if more:
-                came.append(swap_odd(faces.pop(0), axis))
-        first = [1 + has_b[0], 2 + has_b[0] + has_b[1]]
-        faults, came[first[0]], came[first[1]] = lax.optimization_barrier(
-            (faults, came[first[0]], came[first[1]])
-        )
-        return exchange(faults), came
+            came[axis] = [swap_even(faces.pop(0), axis)] + ([swap_odd(faces.pop(0), axis)] if more else [])
+        faults, came["gy"][0] = lax.optimization_barrier((faults, came["gy"][0]))
+        return exchange(faults), came["gx"], came["gy"] + came["gz"]
 
     def stencil(residual, direction, came, solution):
         more = [] if solution is None else [solution]
@@ -635,14 +631,15 @@
 
     ops, residual, direction, *faces = pl.pallas_call(
         functools.partial(setup_kernel, dims, has_b),
-        out_shape=[jax.ShapeDtypeStruct((8, lines, size_z), F32), field_type, field_type] + face_types,
-        in_specs=[smem] * 2 + [vmem] * 2 + [anywhere] * 5 + [vmem] * len(edges),
+        out_shape=[jax.ShapeDtypeStruct((10, lines, size_z), F32), field_type, field_type] + face_types,
+        in_specs=[vmem] * 4 + [anywhere] * 5 + [vmem] * len(edges),
         out_specs=[vmem] * (3 + len(face_types)),
-        scratch_shapes=[pltpu.VMEM(shape2, F32)] * 4 + [pltpu.SemaphoreType.DMA((5,))],
+        scratch_shapes=[pltpu.VMEM(shape2, F32)] * 4
+        + [pltpu.SemaphoreType.DMA((5,))],
         compiler_params=params,
         name="setup",
     )(
-        shift_table, shift_index, recv, weight,
+        shift_table.reshape(1, -1), shift_index.reshape(1, 1), recv, weight,
         *in_hbm(*trans, pore_volume.reshape(shape2), start), *edges,
     )
     plane = full_y * full_z
@@ -691,7 +688,7 @@
     for number in range(TERMS - 1):
         goes = {2: "parts", 3: "sums"}.get(number, "")
         faults = gather(direction, goes, [parts] if goes == "parts" else [table] if goes else [])
-        arrived, came = transfers(faults, faces)
+        arrived, came, far = transfers(faults, faces)
         residual, solution = stencil(residual, direction, came, solution)
         weight_new = 1.0 / (2.0 * sigma - weight_now)
         last_round = number == TERMS - 2
@@ -705,7 +702,7 @@
         if goes:
             table_rows = extra if goes == "parts" else devices * extra
             out_types.append(jax.ShapeDtypeStruct((table_rows, LANES), F32))
-        operands = [ops, residual, direction, recv, weight, arrived]
+        operands = [ops, residual, direction, recv, weight, arrived, *far]
         aliases = {}
         if last_round:
             operands.append(solution)

time: 171 us -> 156 us (0.912)
  waiting for transfers between devices: 37.2 us -> 25.4 us
  Pallas kernels: 41.9 us -> 38.8 us
    ppermute x16, waiting for transfers between devices: 23.9 us -> 5.72 us  [swap_odd(): return lax.ppermute(value, names, pairs)]
    ppermute x24, waiting for transfers between devices: 6.64 us -> 11.8 us  [swap_even(): return lax.ppermute(value, axis, pairs)]
    ppermute x24, starting transfers between devices: 25.6 us -> 29.6 us  [swap_even(): return lax.ppermute(value, axis, pairs)]
    all_to_all x7, starting transfers between devices: 26.2 us -> 22.3 us  [exchange(): return lax.all_to_all(value, AXES, split_axis=0, concat_axis=0, tiled=True)]
    pallas_call x7, Pallas kernels: 8.04 us -> 4.39 us  [stencil(): pl.pallas_call(functools.partial(stencil_kernel, dims, has_b, solution is...]
  transfers between devices with their start and end apart: 47 -> 47, of which waited for: 18 -> 19; matrix products, arithmetic and copies ran while one was open for 0% -> 0% of each run, Pallas kernels for 13% -> 12%
where the time goes in v2:
time: 156 us; the launch traced here: 155 us
  starting transfers between devices  67.6 us (43%)
  Pallas kernels  38.8 us (25%)
  waiting for transfers between devices  25.4 us (16%)
  blocking collectives  19.3 us (12%)
  local copies, waits for them, and re-layouts  2.26 us (1%)
  between operations  1.82 us (1%)
    ppermute x24, starting transfers between devices, swap_even(): return lax.ppermute(value, axis, pairs)  29.6 us
    all_to_all x7, starting transfers between devices, exchange(): return lax.all_to_all(value, AXES, split_axis=0, concat_axis=0, tiled=True)  22.3 us
    all_to_all x2, blocking collectives, exchange(): return lax.all_to_all(value, AXES, split_axis=0, concat_axis=0, tiled=True)  19.3 us
    ppermute x16, starting transfers between devices, swap_odd(): return lax.ppermute(value, names, pairs)  15.6 us
    pallas_call x7, Pallas kernels, local(): pl.pallas_call(body, out_shape=out_types, in_specs=in_specs, out_specs=[v...  12.2 us
    ppermute x24, waiting for transfers between devices, swap_even(): return lax.ppermute(value, axis, pairs)  11.8 us
    all_to_all x7, waiting for transfers between devices, exchange(): return lax.all_to_all(value, AXES, split_axis=0, concat_axis=0, tiled=True)  7.94 us
    pallas_call x1, Pallas kernels, local(): pl.pallas_call(functools.partial(basis_kernel, dims), out_shape=[jax.Shap...  7.58 us
  transfers between devices with their start and end apart: 47, of which 19 were waited for; matrix products, arithmetic and copies ran while one was open for 0% of the time, Pallas kernels for 12%

profile of v2, /device:TPU:0, one launch (start us, length us, event | category | flops | bytes accessed | tf_op | source)
XLA Modules:
  0.0 155.3 jit_solution(3626292651782726514)
XLA Ops:
  1.7 3.0 %collective-permute-start = (f32[16,128]{1,0:T(8,128)S(1)}, f32[16,128]{1,0:T(8,128)S(1)}, u32[]{:S(2)}, u32[]{:S(2)}) collective-permute-start(f32[16,128]{1,0:T(8,128)S(1)} %get-tuple-element.100), channel_id=1, source_target_pairs={{0,16},{16,0},{1,17},{17,1},{2,18},{18,2},{3,19},{19,3},{4,20},{20... | collective-permute-start | bytes 24584 | tf_op jit(solution)/shard_map/ppermute | solution.py:21
  6.9 2.6 %collective-permute-start.3 = (f32[1,64]{1,0:T(1,128)S(1)}, f32[1,64]{1,0:T(1,128)S(1)}, u32[]{:S(2)}, u32[]{:S(2)}) collective-permute-start(f32[1,64]{1,0:T(1,128)S(1)} %get-tuple-element.102), channel_id=1, source_target_pairs={{0,1},{1,0},{2,3},{3,2},{4,5},{5,4},{6,7},{7,6},{8,9},{9,8},{10,11... | collective-permute-start | bytes 776 | tf_op jit(solution)/shard_map/ppermute | solution.py:21
  15.4 4.0 %all-to-all-start = ((f32[32,4,128]{2,1,0:T(4,128)}), f32[32,4,128]{2,1,0:T(4,128)S(1)}, u32[]{:S(2)}, u32[]{:S(2)}) async-start(f32[32,4,128]{2,1,0:T(4,128)} %bitcast.7), calls=%async_computation | async-start | bytes 131072 | tf_op jit(solution)/shard_map/all_to_all | solution.py:45
  19.4 1.8 %collective-permute-start.7 = (f32[4,16,128]{2,1,0:T(8,128)S(1)}, f32[4,16,128]{2,1,0:T(8,128)S(1)}, u32[]{:S(2)}, u32[]{:S(2)}) collective-permute-start(f32[4,16,128]{2,1,0:T(8,128)S(1)} %get-tuple-element.112), channel_id=1, source_target_pairs={{0,16},{4,8},{8,4},{12,28},{16,0},{20,24},{24,20},{28,12},{1,17},{... | collective-permute-start | bytes 98312 | tf_op jit(solution)/shard_map/ppermute | solution.py:41
  30.2 3.0 %all-to-all-start.1 = ((f32[32,4,128]{2,1,0:T(4,128)}), f32[32,4,128]{2,1,0:T(4,128)S(1)}, u32[]{:S(2)}, u32[]{:S(2)}) async-start(f32[32,4,128]{2,1,0:T(4,128)} %bitcast.9), calls=%async_computation.1 | async-start | bytes 131072 | tf_op jit(solution)/shard_map/all_to_all | solution.py:45
  33.3 1.8 %collective-permute-start.13 = (f32[1,1024]{1,0:T(1,128)S(1)}, f32[1,1024]{1,0:T(1,128)S(1)}, u32[]{:S(2)}, u32[]{:S(2)}) collective-permute-start(f32[1,1024]{1,0:T(1,128)S(1)} %get-tuple-element.124), channel_id=1, source_target_pairs={{0,1},{1,0},{2,3},{3,2},{4,5},{5,4},{6,7},{7,6},{8,9},{9,8},{10,11... | collective-permute-start | bytes 12296 | tf_op jit(solution)/shard_map/ppermute | solution.py:21
  37.1 7.6 %basis_gram.1 = (f32[512,128]{1,0:T(8,128)S(1)}, bf16[256,8192]{1,0:T(8,128)(2,1)}) custom-call(s32[1,64]{1,0:T(1,128)S(1)} %fusion.4.well_ref.refs_11_, bf16[256,64,128]{2,1,0:T(8,128)(2,1)} %bitcast.43), custom_call_target="tpu_custom_call" | custom-call | flops 1342177280 | bytes 8388608 | tf_op jit(solution)/shard_map/basis_gram/pallas_call | solution.py:662
  49.4 3.1 %all-to-all-start.2 = ((f32[32,20,128]{2,1,0:T(8,128)}), f32[32,20,128]{2,1,0:T(8,128)S(1)}, u32[]{:S(2)}, u32[]{:S(2)}) async-start(f32[32,20,128]{2,1,0:T(8,128)} %all_to_all.66), calls=%async_computation.2 | async-start | bytes 786432 | tf_op jit(solution)/shard_map/all_to_all | solution.py:45
  57.7 3.2 %collective-permute-done.15.refs_3_ = f32[16,16,128]{2,1,0:T(8,128)S(1)} collective-permute-done((f32[16,16,128]{2,1,0:T(8,128)S(1)}, f32[16,16,128]{2,1,0:T(8,128)S(1)}, u32[]{:S(2)}, u32[]{:S(2)}) %collective-permute-start.15) | collective-permute-done | bytes 131104 | tf_op jit(solution)/shard_map/ppermute | solution.py:21
  61.5 2.7 %all-to-all-done.2 = f32[32,20,128]{2,1,0:T(8,128)S(1)} async-done(((f32[32,20,128]{2,1,0:T(8,128)}), f32[32,20,128]{2,1,0:T(8,128)S(1)}, u32[]{:S(2)}, u32[]{:S(2)}) %all-to-all-start.2) | async-done | bytes 327712 | tf_op jit(solution)/shard_map/all_to_all | solution.py:45
  68.4 3.1 %all-to-all-start.3 = ((f32[32,20,128]{2,1,0:T(8,128)}), f32[32,20,128]{2,1,0:T(8,128)S(1)}, u32[]{:S(2)}, u32[]{:S(2)}) async-start(f32[32,20,128]{2,1,0:T(8,128)} %all_to_all.69), calls=%async_computation.3 | async-start | bytes 786432 | tf_op jit(solution)/shard_map/all_to_all | solution.py:45
  71.5 1.8 %collective-permute-start.20 = (f32[16,16,128]{2,1,0:T(8,128)S(1)}, f32[16,16,128]{2,1,0:T(8,128)S(1)}, u32[]{:S(2)}, u32[]{:S(2)}) collective-permute-start(f32[16,16,128]{2,1,0:T(8,128)S(1)} %get-tuple-element.140), channel_id=1, source_target_pairs={{0,16},{16,0},{1,17},{17,1},{2,18},{18,2},{3,19},{19,3},{4,20},{20... | collective-permute-start | bytes 393224 | tf_op jit(solution)/shard_map/ppermute | solution.py:21
  73.6 1.8 %collective-permute-start.23 = (f32[1,1024]{1,0:T(1,128)S(1)}, f32[1,1024]{1,0:T(1,128)S(1)}, u32[]{:S(2)}, u32[]{:S(2)}) collective-permute-start(f32[1,1024]{1,0:T(1,128)S(1)} %get-tuple-element.148), channel_id=1, source_target_pairs={{0,1},{1,0},{2,3},{3,2},{4,5},{5,4},{6,7},{7,6},{8,9},{9,8},{10,11... | collective-permute-start | bytes 12296 | tf_op jit(solution)/shard_map/ppermute | solution.py:21
  76.8 3.2 %collective-permute-done.20.refs_3_ = f32[16,16,128]{2,1,0:T(8,128)S(1)} collective-permute-done((f32[16,16,128]{2,1,0:T(8,128)S(1)}, f32[16,16,128]{2,1,0:T(8,128)S(1)}, u32[]{:S(2)}, u32[]{:S(2)}) %collective-permute-start.20) | collective-permute-done | bytes 131104 | tf_op jit(solution)/shard_map/ppermute | solution.py:21
  80.6 2.7 %all-to-all-done.3 = f32[32,20,128]{2,1,0:T(8,128)S(1)} async-done(((f32[32,20,128]{2,1,0:T(8,128)}), f32[32,20,128]{2,1,0:T(8,128)S(1)}, u32[]{:S(2)}, u32[]{:S(2)}) %all-to-all-start.3) | async-done | bytes 327712 | tf_op jit(solution)/shard_map/all_to_all | solution.py:45
  88.5 2.9 %all-to-all-start.4 = ((f32[32,4,128]{2,1,0:T(4,128)}), f32[32,4,128]{2,1,0:T(4,128)S(1)}, u32[]{:S(2)}, u32[]{:S(2)}) async-start(f32[32,4,128]{2,1,0:T(4,128)} %bitcast.13), calls=%async_computation.4 | async-start | bytes 131072 | tf_op jit(solution)/shard_map/all_to_all | solution.py:45
  91.4 1.8 %collective-permute-start.27 = (f32[4,16,128]{2,1,0:T(8,128)S(1)}, f32[4,16,128]{2,1,0:T(8,128)S(1)}, u32[]{:S(2)}, u32[]{:S(2)}) collective-permute-start(f32[4,16,128]{2,1,0:T(8,128)S(1)} %get-tuple-element.158), channel_id=1, source_target_pairs={{0,16},{4,8},{8,4},{12,28},{16,0},{20,24},{24,20},{28,12},{1,17},{... | collective-permute-start | bytes 98312 | tf_op jit(solution)/shard_map/ppermute | solution.py:41
  102.2 3.0 %all-to-all-start.5 = ((f32[32,4,128]{2,1,0:T(4,128)}), f32[32,4,128]{2,1,0:T(4,128)S(1)}, u32[]{:S(2)}, u32[]{:S(2)}) async-start(f32[32,4,128]{2,1,0:T(4,128)} %bitcast.15), calls=%async_computation.5 | async-start | bytes 131072 | tf_op jit(solution)/shard_map/all_to_all | solution.py:45
  105.2 1.8 %collective-permute-start.32 = (f32[4,16,128]{2,1,0:T(8,128)S(1)}, f32[4,16,128]{2,1,0:T(8,128)S(1)}, u32[]{:S(2)}, u32[]{:S(2)}) collective-permute-start(f32[4,16,128]{2,1,0:T(8,128)S(1)} %get-tuple-element.169), channel_id=1, source_target_pairs={{0,16},{4,8},{8,4},{12,28},{16,0},{20,24},{24,20},{28,12},{1,17},{... | collective-permute-start | bytes 98312 | tf_op jit(solution)/shard_map/ppermute | solution.py:41
  116.0 3.2 %all-to-all-start.6 = ((f32[32,4,128]{2,1,0:T(4,128)}), f32[32,4,128]{2,1,0:T(4,128)S(1)}, u32[]{:S(2)}, u32[]{:S(2)}) async-start(f32[32,4,128]{2,1,0:T(4,128)} %bitcast.17), calls=%async_computation.6 | async-start | bytes 131072 | tf_op jit(solution)/shard_map/all_to_all | solution.py:45
  126.5 4.3 %update.13 = (f32[128,128]{1,0:T(8,128)S(1)}, f32[16,8192]{1,0:T(8,128)S(1)}) custom-call(f32[10,64,128]{2,1,0:T(8,128)S(1)} %get-tuple-element.103.refs_0_, f32[16,64,128]{2,1,0:T(8,128)S(1)} %get-tuple-element.176.refs_1_, f32[16,64,128]{2,1,0:T(8,128)S(1)} %get-tuple-element.173.refs_2_.refs_0_, s32[1,1024]{1,0:T(1,128)S(1)} %get-tuple-element.98.refs_2_.refs_3_, ...), custom_call_target="tpu_custom_call" | custom-call | tf_op jit(solution)/shard_map/update/pallas_call | solution.py:721
  130.8 10.1 %all_to_all.94 = f32[32,4,128]{2,1,0:T(4,128)S(1)} all-to-all(f32[32,4,128]{2,1,0:T(4,128)S(1)} %bitcast.33), channel_id=1, replica_groups=mesh['gx'=2,'gy'=4,'gz'=4] {'gx','gy','gz'}, dimensions={0} | all-to-all | bytes 131072 | tf_op jit(solution)/shard_map/all_to_all | solution.py:45
  141.0 9.2 %all_to_all.95 = f32[32,4,128]{2,1,0:T(4,128)S(1)} all-to-all(f32[32,4,128]{2,1,0:T(4,128)S(1)} %tile.2), channel_id=1, replica_groups=mesh['gx'=2,'gy'=4,'gz'=4] {'gx','gy','gz'}, dimensions={0} | all-to-all | bytes 131072 | tf_op jit(solution)/shard_map/all_to_all | solution.py:45
  150.2 4.9 %finish.1 = (f32[16,64,128]{2,1,0:T(8,128)}, f32[16,256]{1,0:T(8,128)}, f32[16,256]{1,0:T(8,128)}, f32[16,64]{1,0:T(8,128)}) custom-call(f32[128,128]{1,0:T(8,128)S(1)} %bitcast.28, f32[512,128]{1,0:T(8,128)S(1)} %get-tuple-element.186.table_ref, f32[16,8192]{1,0:T(8,128)S(1)} %get-tuple-element.187.flat_ref, ...), custom_call_target="tpu_custom_call" | custom-call | tf_op jit(solution)/shard_map/finish/pallas_call | solution.py:742
  (108 shorter events, 66.6 us)
Async XLA Ops:
  1.7 9.3 %collective-permute-start = (f32[16,128]{1,0:T(8,128)S(1)}, f32[16,128]{1,0:T(8,128)S(1)}, u32[]{:S(2)}, u32[]{:S(2)}) collective-permute-start(f32[16,128]{1,0:T(8,128)S(1)} %get-tuple-element.100), channel_id=1, source_target_pairs={{0,16},{16,0},{1,17},{17,1},{2,18},{18,2},{3,19},{19,3},{4,20},{20... | collective-permute-start | bytes 24584 | tf_op jit(solution)/shard_map/ppermute | solution.py:21
  13.2 10.1 %collective-permute-start.5 = (f32[16,16,128]{2,1,0:T(8,128)S(1)}, f32[16,16,128]{2,1,0:T(8,128)S(1)}, u32[]{:S(2)}, u32[]{:S(2)}) collective-permute-start(f32[16,16,128]{2,1,0:T(8,128)S(1)} %get-tuple-element.106), channel_id=1, source_target_pairs={{0,16},{16,0},{1,17},{17,1},{2,18},{18,2},{3,19},{19,3},{4,20},{20... | collective-permute-start | bytes 393224 | tf_op jit(solution)/shard_map/ppermute | solution.py:21
  15.4 11.6 %all-to-all-start = ((f32[32,4,128]{2,1,0:T(4,128)}), f32[32,4,128]{2,1,0:T(4,128)S(1)}, u32[]{:S(2)}, u32[]{:S(2)}) async-start(f32[32,4,128]{2,1,0:T(4,128)} %bitcast.7), calls=%async_computation | async-start | bytes 131072 | tf_op jit(solution)/shard_map/all_to_all | solution.py:45
  28.3 16.4 %collective-permute-start.10 = (f32[16,16,128]{2,1,0:T(8,128)S(1)}, f32[16,16,128]{2,1,0:T(8,128)S(1)}, u32[]{:S(2)}, u32[]{:S(2)}) collective-permute-start(f32[16,16,128]{2,1,0:T(8,128)S(1)} %get-tuple-element.117), channel_id=1, source_target_pairs={{0,16},{16,0},{1,17},{17,1},{2,18},{18,2},{3,19},{19,3},{4,20},{20... | collective-permute-start | bytes 393224 | tf_op jit(solution)/shard_map/ppermute | solution.py:21
  30.2 15.2 %all-to-all-start.1 = ((f32[32,4,128]{2,1,0:T(4,128)}), f32[32,4,128]{2,1,0:T(4,128)S(1)}, u32[]{:S(2)}, u32[]{:S(2)}) async-start(f32[32,4,128]{2,1,0:T(4,128)} %bitcast.9), calls=%async_computation.1 | async-start | bytes 131072 | tf_op jit(solution)/shard_map/all_to_all | solution.py:45
  33.3 12.1 %collective-permute-start.13 = (f32[1,1024]{1,0:T(1,128)S(1)}, f32[1,1024]{1,0:T(1,128)S(1)}, u32[]{:S(2)}, u32[]{:S(2)}) collective-permute-start(f32[1,1024]{1,0:T(1,128)S(1)} %get-tuple-element.124), channel_id=1, source_target_pairs={{0,1},{1,0},{2,3},{3,2},{4,5},{5,4},{6,7},{7,6},{8,9},{9,8},{10,11... | collective-permute-start | bytes 12296 | tf_op jit(solution)/shard_map/ppermute | solution.py:21
  35.1 10.3 %collective-permute-start.14 = (f32[1,1024]{1,0:T(1,128)S(1)}, f32[1,1024]{1,0:T(1,128)S(1)}, u32[]{:S(2)}, u32[]{:S(2)}) collective-permute-start(f32[1,1024]{1,0:T(1,128)S(1)} %get-tuple-element.125), channel_id=1, source_target_pairs={{0,16},{1,2},{2,1},{3,19},{16,0},{17,18},{18,17},{19,3},{4,20},{5,... | collective-permute-start | bytes 12296 | tf_op jit(solution)/shard_map/ppermute | solution.py:41
  36.6 8.8 %collective-permute-start.12 = (f32[4,16,128]{2,1,0:T(8,128)S(1)}, f32[4,16,128]{2,1,0:T(8,128)S(1)}, u32[]{:S(2)}, u32[]{:S(2)}) collective-permute-start(f32[4,16,128]{2,1,0:T(8,128)S(1)} %get-tuple-element.123), channel_id=1, source_target_pairs={{0,16},{4,8},{8,4},{12,28},{16,0},{20,24},{24,20},{28,12},{1,17},{... | collective-permute-start | bytes 98312 | tf_op jit(solution)/shard_map/ppermute | solution.py:41
  49.4 14.9 %all-to-all-start.2 = ((f32[32,20,128]{2,1,0:T(8,128)}), f32[32,20,128]{2,1,0:T(8,128)S(1)}, u32[]{:S(2)}, u32[]{:S(2)}) async-start(f32[32,20,128]{2,1,0:T(8,128)} %all_to_all.66), calls=%async_computation.2 | async-start | bytes 786432 | tf_op jit(solution)/shard_map/all_to_all | solution.py:45
  52.5 8.3 %collective-permute-start.15 = (f32[16,16,128]{2,1,0:T(8,128)S(1)}, f32[16,16,128]{2,1,0:T(8,128)S(1)}, u32[]{:S(2)}, u32[]{:S(2)}) collective-permute-start(f32[16,16,128]{2,1,0:T(8,128)S(1)} %get-tuple-element.128), channel_id=1, source_target_pairs={{0,16},{16,0},{1,17},{17,1},{2,18},{18,2},{3,19},{19,3},{4,20},{20... | collective-permute-start | bytes 393224 | tf_op jit(solution)/shard_map/ppermute | solution.py:21
  54.2 10.1 %collective-permute-start.17 = (f32[4,16,128]{2,1,0:T(8,128)S(1)}, f32[4,16,128]{2,1,0:T(8,128)S(1)}, u32[]{:S(2)}, u32[]{:S(2)}) collective-permute-start(f32[4,16,128]{2,1,0:T(8,128)S(1)} %get-tuple-element.135), channel_id=1, source_target_pairs={{0,16},{4,8},{8,4},{12,28},{16,0},{20,24},{24,20},{28,12},{1,17},{... | collective-permute-start | bytes 98312 | tf_op jit(solution)/shard_map/ppermute | solution.py:41
  54.6 9.7 %collective-permute-start.18 = (f32[1,1024]{1,0:T(1,128)S(1)}, f32[1,1024]{1,0:T(1,128)S(1)}, u32[]{:S(2)}, u32[]{:S(2)}) collective-permute-start(f32[1,1024]{1,0:T(1,128)S(1)} %get-tuple-element.136), channel_id=1, source_target_pairs={{0,1},{1,0},{2,3},{3,2},{4,5},{5,4},{6,7},{7,6},{8,9},{9,8},{10,11... | collective-permute-start | bytes 12296 | tf_op jit(solution)/shard_map/ppermute | solution.py:21
  56.2 8.1 %collective-permute-start.19 = (f32[1,1024]{1,0:T(1,128)S(1)}, f32[1,1024]{1,0:T(1,128)S(1)}, u32[]{:S(2)}, u32[]{:S(2)}) collective-permute-start(f32[1,1024]{1,0:T(1,128)S(1)} %get-tuple-element.137), channel_id=1, source_target_pairs={{0,16},{1,2},{2,1},{3,19},{16,0},{17,18},{18,17},{19,3},{4,20},{5,... | collective-permute-start | bytes 12296 | tf_op jit(solution)/shard_map/ppermute | solution.py:41
  68.4 15.0 %all-to-all-start.3 = ((f32[32,20,128]{2,1,0:T(8,128)}), f32[32,20,128]{2,1,0:T(8,128)S(1)}, u32[]{:S(2)}, u32[]{:S(2)}) async-start(f32[32,20,128]{2,1,0:T(8,128)} %all_to_all.69), calls=%async_computation.3 | async-start | bytes 786432 | tf_op jit(solution)/shard_map/all_to_all | solution.py:45
  71.5 8.5 %collective-permute-start.20 = (f32[16,16,128]{2,1,0:T(8,128)S(1)}, f32[16,16,128]{2,1,0:T(8,128)S(1)}, u32[]{:S(2)}, u32[]{:S(2)}) collective-permute-start(f32[16,16,128]{2,1,0:T(8,128)S(1)} %get-tuple-element.140), channel_id=1, source_target_pairs={{0,16},{16,0},{1,17},{17,1},{2,18},{18,2},{3,19},{19,3},{4,20},{20... | collective-permute-start | bytes 393224 | tf_op jit(solution)/shard_map/ppermute | solution.py:21
  73.3 10.1 %collective-permute-start.22 = (f32[4,16,128]{2,1,0:T(8,128)S(1)}, f32[4,16,128]{2,1,0:T(8,128)S(1)}, u32[]{:S(2)}, u32[]{:S(2)}) collective-permute-start(f32[4,16,128]{2,1,0:T(8,128)S(1)} %get-tuple-element.147), channel_id=1, source_target_pairs={{0,16},{4,8},{8,4},{12,28},{16,0},{20,24},{24,20},{28,12},{1,17},{... | collective-permute-start | bytes 98312 | tf_op jit(solution)/shard_map/ppermute | solution.py:41
  73.6 9.8 %collective-permute-start.23 = (f32[1,1024]{1,0:T(1,128)S(1)}, f32[1,1024]{1,0:T(1,128)S(1)}, u32[]{:S(2)}, u32[]{:S(2)}) collective-permute-start(f32[1,1024]{1,0:T(1,128)S(1)} %get-tuple-element.148), channel_id=1, source_target_pairs={{0,1},{1,0},{2,3},{3,2},{4,5},{5,4},{6,7},{7,6},{8,9},{9,8},{10,11... | collective-permute-start | bytes 12296 | tf_op jit(solution)/shard_map/ppermute | solution.py:21
  75.3 8.1 %collective-permute-start.24 = (f32[1,1024]{1,0:T(1,128)S(1)}, f32[1,1024]{1,0:T(1,128)S(1)}, u32[]{:S(2)}, u32[]{:S(2)}) collective-permute-start(f32[1,1024]{1,0:T(1,128)S(1)} %get-tuple-element.149), channel_id=1, source_target_pairs={{0,16},{1,2},{2,1},{3,19},{16,0},{17,18},{18,17},{19,3},{4,20},{5,... | collective-permute-start | bytes 12296 | tf_op jit(solution)/shard_map/ppermute | solution.py:41
  85.9 9.3 %collective-permute-start.25 = (f32[16,16,128]{2,1,0:T(8,128)S(1)}, f32[16,16,128]{2,1,0:T(8,128)S(1)}, u32[]{:S(2)}, u32[]{:S(2)}) collective-permute-start(f32[16,16,128]{2,1,0:T(8,128)S(1)} %get-tuple-element.152), channel_id=1, source_target_pairs={{0,16},{16,0},{1,17},{17,1},{2,18},{18,2},{3,19},{19,3},{4,20},{20... | collective-permute-start | bytes 393224 | tf_op jit(solution)/shard_map/ppermute | solution.py:21
  88.5 10.5 %all-to-all-start.4 = ((f32[32,4,128]{2,1,0:T(4,128)}), f32[32,4,128]{2,1,0:T(4,128)S(1)}, u32[]{:S(2)}, u32[]{:S(2)}) async-start(f32[32,4,128]{2,1,0:T(4,128)} %bitcast.13), calls=%async_computation.4 | async-start | bytes 131072 | tf_op jit(solution)/shard_map/all_to_all | solution.py:45
  100.2 8.8 %collective-permute-start.30 = (f32[16,16,128]{2,1,0:T(8,128)S(1)}, f32[16,16,128]{2,1,0:T(8,128)S(1)}, u32[]{:S(2)}, u32[]{:S(2)}) collective-permute-start(f32[16,16,128]{2,1,0:T(8,128)S(1)} %get-tuple-element.163), channel_id=1, source_target_pairs={{0,16},{16,0},{1,17},{17,1},{2,18},{18,2},{3,19},{19,3},{4,20},{20... | collective-permute-start | bytes 393224 | tf_op jit(solution)/shard_map/ppermute | solution.py:21
  102.2 10.5 %all-to-all-start.5 = ((f32[32,4,128]{2,1,0:T(4,128)}), f32[32,4,128]{2,1,0:T(4,128)S(1)}, u32[]{:S(2)}, u32[]{:S(2)}) async-start(f32[32,4,128]{2,1,0:T(4,128)} %bitcast.15), calls=%async_computation.5 | async-start | bytes 131072 | tf_op jit(solution)/shard_map/all_to_all | solution.py:45
  114.0 8.8 %collective-permute-start.35 = (f32[16,16,128]{2,1,0:T(8,128)S(1)}, f32[16,16,128]{2,1,0:T(8,128)S(1)}, u32[]{:S(2)}, u32[]{:S(2)}) collective-permute-start(f32[16,16,128]{2,1,0:T(8,128)S(1)} %get-tuple-element.174), channel_id=1, source_target_pairs={{0,16},{16,0},{1,17},{17,1},{2,18},{18,2},{3,19},{19,3},{4,20},{20... | collective-permute-start | bytes 393224 | tf_op jit(solution)/shard_map/ppermute | solution.py:21
  116.0 10.5 %all-to-all-start.6 = ((f32[32,4,128]{2,1,0:T(4,128)}), f32[32,4,128]{2,1,0:T(4,128)S(1)}, u32[]{:S(2)}, u32[]{:S(2)}) async-start(f32[32,4,128]{2,1,0:T(4,128)} %bitcast.17), calls=%async_computation.6 | async-start | bytes 131072 | tf_op jit(solution)/shard_map/all_to_all | solution.py:45
  (25 other events, 125.9 us)

commit v3 on v2

--- a/solution.py
+++ b/solution.py
@@ -113,7 +113,7 @@
 
 
 def gather_kernel(dims, early, *refs):
-    extra, goes = early
+    extra, goes, parity, begin = early
     direction_ref, send_ref = refs[:2]
     faults_out = refs[-1]
     columns, size_x, size_y, size_z, slots = dims
@@ -122,11 +122,14 @@
     half = lines // 2
     field = direction_ref[...].astype(BF16)
     field = jnp.concatenate([field[:, :half, :], field[:, half:, :]], axis=2).reshape(columns * half, 2 * size_z)
-    if goes:
-        for i in range(send_ref.shape[1] // slots):
-            at = i * (rows + extra) + rows
-            source = refs[2][...] if goes == "sums" else refs[2][i * extra : (i + 1) * extra, :]
-            faults_out[at : at + extra, :] = source
+    for i in range(send_ref.shape[1] // slots if goes else 0):
+        at = i * (rows + extra) + rows
+        if goes == "sums":
+            source = refs[2][parity[i] * extra : (parity[i] + 1) * extra, :]
+        else:
+            own = slice(begin + i * extra, begin + (i + 1) * extra)
+            source = refs[2][own, :] + refs[3][own, :]
+        faults_out[at : at + extra, :] = source
     total = send_ref.shape[1]
     width = min(256, total)
     for start in range(0, total, width):
@@ -272,7 +275,7 @@
 def update_kernel(dims, has_b, keep, gain, last_round, early, *refs):
     refs = list(refs)
     columns, size_x, size_y, size_z, slots = dims
-    extra, comes = early
+    extra, comes, parity = early
     ops_ref, residual_ref, direction_ref, recv_ref, weight_ref, arrived_ref = refs[:6]
     refs = refs[6:]
     ya_ref, yb_ref, za_ref, zb_ref = unpack_faces(refs[: 2 + has_b[1] + has_b[2]], has_b[1:])
@@ -280,8 +283,11 @@
     yb_ref = ya_ref if yb_ref is None else yb_ref
     zb_ref = za_ref if zb_ref is None else zb_ref
     if last_round:
-        solution_ref, well_ref, basis_source, sums_out, flat_out, landed_ref, solution_out, basis_ref, sem = refs
-        (basis_copy,) = start_copies([(basis_source, basis_ref)], sem)
+        solution_ref, well_ref, *refs = refs
+        blocks = (len(refs) - 5) // 2
+        sources, (sums_out, flat_out, landed_ref, solution_out) = refs[:blocks], refs[blocks : blocks + 4]
+        basis_refs, sem = refs[blocks + 4 : -1], refs[-1]
+        fetches = start_copies(zip(sources, basis_refs), sem)
     else:
         landed_ref = refs.pop()
     table_out = refs.pop(0) if comes else None
@@ -306,11 +312,11 @@
     for j in range(total // LANES):
         tiles.append(regroup(source_ref[j * columns : (j + 1) * columns, :LANES], rows, slots))
     if comes == "parts":
-        added = arrived_ref[rows : rows + extra, :]
-        for i in range(1, devices):
+        added = [jnp.zeros((extra, LANES), F32)] * 2
+        for i in range(devices):
             at = i * per_device + rows
-            added = added + arrived_ref[at : at + extra, :]
-        table_out[...] = added
+            added[parity[i]] = added[parity[i]] + arrived_ref[at : at + extra, :]
+        table_out[:extra, :], table_out[extra:, :] = added
     if comes == "sums":
         for i in range(devices):
             at = i * per_device + rows
@@ -345,30 +351,45 @@
     if not last_round:
         emit_faces(direction_out, faces_out, dims)
     else:
-        basis_copy.wait()
-        sums_of(dims, solution_out, basis_ref, well_ref, flat_out, sums_out)
-
-
-def basis_kernel(dims, well_ref, source_ref, parts_out, flat_target, basis_ref, flat_out, hot_ref, sem, out_sem):
+        for copy in fetches:
+            copy.wait()
+        sums_of(dims, solution_out, basis_refs, well_ref, flat_out, sums_out)
+
+
+def basis_kernel(dims, piece, blocks, *refs):
+    well_ref, source_ref = refs[:2]
+    others = refs[2 : 2 + piece]
+    last = piece == blocks - 1
+    before = refs[2 + piece : 2 + 3 * piece] if last else ()
+    refs = refs[2 + piece + len(before) :]
+    flat_target, gram_out, wells_out, basis_ref, hot_ref, flat_out, sem, out_sem = refs[:8]
+    held = refs[8 : 8 + piece]
     columns, size_x, size_y, size_z, slots = dims
     lines = size_x * size_y
-    count = basis_ref.shape[0]
     wells = well_ref.shape[1]
     side = 16
-    groups = [pl.ds(first, side) for first in range(0, count, side)]
-    copies = [pltpu.make_async_copy(source_ref.at[g], basis_ref.at[g], sem.at[i]) for i, g in enumerate(groups)]
-    ahead = 4
-    for copy in copies[:ahead]:
+    groups = [pl.ds(first, side) for first in range(0, LANES, side)]
+    copies = [
+        pltpu.make_async_copy(source_ref.at[pl.ds(piece * LANES + i * side, side)], basis_ref.at[g], sem.at[i])
+        for i, g in enumerate(groups)
+    ]
+    for copy in copies:
         copy.start()
+    fetches = start_copies(zip(others, held), refs[8 + piece]) if piece else []
+    stores = []
     row = lax.broadcasted_iota(jnp.int32, (side * side, side * side), 0)
     lane = lax.broadcasted_iota(jnp.int32, (side * side, side * side), 1)
     turn = jnp.where((row % side == lane // side) & (row // side == lane % side), 1.0, 0.0).astype(BF16)
-    stores = []
+    cell = well_ref[...]
+    lane_of = jnp.broadcast_to(lax.rem(cell + size_z, size_z), (size_z, wells))
+    lane_of = lane_of == lax.broadcasted_iota(jnp.int32, (size_z, wells), 0)
+    line_of = jnp.broadcast_to(jnp.where(cell < 0, -1, cell // size_z), (size_z, wells))
+    for line in range(lines):
+        hot = jnp.where(lane_of & (line_of == line), 1.0, 0.0)
+        hot_ref[line * size_z : (line + 1) * size_z, :] = hot.astype(BF16)
     for index in range(0, len(groups), 2):
-        for i in (index, index + 1):
-            copies[i].wait()
-            if i + ahead < len(copies):
-                copies[i + ahead].start()
+        copies[index].wait()
+        copies[index + 1].wait()
         first = index * side
         for begin in range(0, lines, side):
             tile = [
@@ -380,33 +401,36 @@
                 lanes = slice((begin + i) * size_z, (begin + i + 1) * size_z)
                 flat_out[first : first + side, lanes] = tile[i * side : (i + 1) * side, :size_z]
                 flat_out[first + side : first + 2 * side, lanes] = tile[i * side : (i + 1) * side, size_z:]
-        for i in (index, index + 1):
-            stores.append(
-                pltpu.make_async_copy(flat_out.at[groups[i]], flat_target.at[groups[i]], out_sem.at[i])
-            )
-            stores[-1].start()
-    cell = well_ref[...]
-    lane_of = jnp.broadcast_to(lax.rem(cell + size_z, size_z), (size_z, wells))
-    lane_of = lane_of == lax.broadcasted_iota(jnp.int32, (size_z, wells), 0)
-    line_of = jnp.broadcast_to(jnp.where(cell < 0, -1, cell // size_z), (size_z, wells))
-    for line in range(lines):
-        hot = jnp.where(lane_of & (line_of == line), 1.0, 0.0)
-        hot_ref[line * size_z : (line + 1) * size_z, :] = hot.astype(BF16)
+        pair = pl.ds(first, 2 * side)
+        stores.append(pltpu.make_async_copy(flat_out.at[pair], flat_target.at[pair], out_sem.at[index // 2]))
+        stores[-1].start()
     flat = flat_out[...]
-    gram = nt_dot(flat, flat)
+    for copy in fetches:
+        copy.wait()
+    for i, other in enumerate(held + (flat_out,)):
+        product = nt_dot(other[...], flat)
+        if last:
+            place = (piece * (piece + 1) // 2 + i) * LANES
+            refs[-1][place : place + LANES, :] = product
+        else:
+            gram_out[i * LANES : (i + 1) * LANES, :] = product
     at_wells = jnp.dot(flat, hot_ref[...], preferred_element_type=F32)
-    parts_out[...] = jnp.zeros(parts_out.shape, F32)
-    blocks = count // LANES
-    at = 0
-    for i in range(blocks):
-        for j in range(i, blocks):
-            parts_out[at : at + LANES, :] = gram[i * LANES : (i + 1) * LANES, j * LANES : (j + 1) * LANES]
-            at += LANES
-    beside = LANES // wells
-    for i in range(blocks):
-        place = at + i // beside * LANES
-        lanes = slice(i % beside * wells, (i % beside + 1) * wells)
-        parts_out[place : place + LANES, lanes] = at_wells[i * LANES : (i + 1) * LANES, :]
+    if last:
+        full_ref, beside, place = refs[-1], LANES // wells, 0
+        for i in range(piece):
+            full_ref[place : place + (i + 1) * LANES, :] = before[2 * i][...]
+            place += (i + 1) * LANES
+        place += (piece + 1) * LANES
+        full_ref[place:, :] = jnp.zeros((full_ref.shape[0] - place, LANES), F32)
+        for i in range(blocks):
+            value = at_wells if i == piece else before[2 * i + 1][...]
+            at, lanes = place + i // beside * LANES, slice(i % beside * wells, (i % beside + 1) * wells)
+            full_ref[at : at + LANES, lanes] = value
+        half, even = full_ref.shape[0] // 2, even_places()[1]
+        gram_out[...] = jnp.where(even, full_ref[:half, :], full_ref[half:, :])
+        wells_out[...] = jnp.where(even, full_ref[half:, :], full_ref[:half, :])
+    else:
+        wells_out[...] = at_wells
     for store in stores:
         store.wait()
 
@@ -418,18 +442,17 @@
     return high, middle, (left - middle.astype(F32)).astype(BF16)
 
 
-def sums_of(dims, solution_ref, basis_ref, well_ref, flat_out, sums_out):
+def sums_of(dims, solution_ref, basis_refs, well_ref, flat_out, sums_out):
     columns, size_x, size_y, size_z, slots = dims
     lines = size_x * size_y
-    count = basis_ref.shape[0]
     wells = well_ref.shape[1]
     for line in range(lines):
         flat_out[:, line * size_z : (line + 1) * size_z] = solution_ref[:, line, :]
     parts = jnp.concatenate(split_three(flat_out[...]), axis=0)
-    with_basis = nt_dot(parts, basis_ref[...])
+    with_basis = jnp.concatenate([nt_dot(parts, ref[...]) for ref in basis_refs], axis=1)
     with_self = nt_dot(parts, parts)
     sums_out[...] = jnp.zeros(sums_out.shape, F32)
-    blocks = count // LANES
+    blocks = len(basis_refs)
     first = with_basis[:columns]
     beyond = with_basis[columns : 2 * columns] + with_basis[2 * columns :]
     for i in range(blocks):
@@ -461,19 +484,23 @@
 
 
 def finish_kernel(
-    dims, scale, wells, sums_ref, table_ref, flat_ref, basis_source,
-    block_out, first_out, coeffs_out, wells_out, basis_ref, sem,
+    dims, scale, wells, blocks, groups, sums_ref, flat_ref, *refs
 ):
-    (basis_copy,) = start_copies([(basis_source, basis_ref)], sem)
+    mine, other = ([ref[...] for ref in refs[i * groups : (i + 1) * groups]] for i in range(2))
+    mine, other, refs = jnp.concatenate(mine, axis=0), jnp.concatenate(other, axis=0), refs[2 * groups :]
+    even = even_places()[1]
+    table = [jnp.where(even, mine, other), jnp.where(even, other, mine)]
+    table = jnp.concatenate(table, axis=0)
+    block_out, first_out, coeffs_out, wells_out = refs[blocks : blocks + 4]
+    basis_refs = refs[blocks + 4 : -1]
+    fetches = start_copies(zip(refs[:blocks], basis_refs), refs[-1])
     columns, size_x, size_y, size_z, slots = dims
     lines = size_x * size_y
-    count = basis_ref.shape[0]
-    blocks = count // LANES
     pieces, at = {}, 0
     for i in range(blocks):
-        for j in range(i, blocks):
-            pieces[i, j] = table_ref[at : at + LANES, :]
-            pieces[j, i] = pieces[i, j] if i == j else pieces[i, j].T
+        for j in range(i + 1):
+            pieces[j, i] = table[at : at + LANES, :]
+            pieces[i, j] = pieces[j, i] if i == j else pieces[j, i].T
             at += LANES
     basis_gram = jnp.concatenate(
         [jnp.concatenate([pieces[i, j] for j in range(blocks)], axis=1) for i in range(blocks)], axis=0
@@ -482,7 +509,7 @@
     wells_basis = []
     for i in range(blocks):
         place = at + i // beside * LANES
-        wells_basis.append(table_ref[place : place + LANES, i % beside * wells : (i % beside + 1) * wells])
+        wells_basis.append(table[place : place + LANES, i % beside * wells : (i % beside + 1) * wells])
     wells_basis = jnp.concatenate(wells_basis, axis=0)
 
     def block(i):
@@ -517,12 +544,14 @@
     wells_out[...] = exact_dot(inverse, rest_wells)
     high, low = split_two(inverse)
     factors = jnp.concatenate([high, high, low], axis=1)
-    basis_copy.wait()
+    for copy in fetches:
+        copy.wait()
     rounds = jnp.concatenate([first_round, second_round], axis=0)
     step = min(8, lines)
     for begin in range(0, lines, step):
         lanes = slice(begin * size_z, (begin + step) * size_z)
-        spans = jnp.dot(rounds, basis_ref[:, lanes], preferred_element_type=F32)
+        basis_part = jnp.concatenate([ref[:, lanes] for ref in basis_refs], axis=0)
+        spans = jnp.dot(rounds, basis_part, preferred_element_type=F32)
         rest = flat_ref[:, lanes] - spans[:columns] - spans[columns:]
         rest_high, rest_low = split_two(rest)
         stacked = jnp.concatenate([rest_high, rest_low, rest_high], axis=0)
@@ -592,56 +621,6 @@
     for axis, edge, more in zip(AXES, (edge_x, edge_y, edge_z), has_b):
         edges += [swap_even(edge, axis)] + ([swap_odd(edge, axis)] if more else [])
 
-    def gather(direction, goes="", source=()):
-        sent_rows = devices * (rows + (extra if goes else 0))
-        return pl.pallas_call(
-            functools.partial(gather_kernel, dims, (extra, goes)),
-            out_shape=jax.ShapeDtypeStruct((sent_rows, LANES), F32),
-            in_specs=[vmem] * (2 + len(source)),
-            out_specs=vmem,
-            compiler_params=params,
-            cost_estimate=pl.CostEstimate(
-                flops=4 * columns * cells * total, bytes_accessed=4 * columns * cells, transcendentals=0
-            ),
-            name="fault_gather",
-        )(direction, send, *source)
-
-    def transfers(faults, faces):
-        faces = list(faces)
-        came = {}
-        for axis, more in zip(AXES, has_b):
-            came[axis] = [swap_even(faces.pop(0), axis)] + ([swap_odd(faces.pop(0), axis)] if more else [])
-        faults, came["gy"][0] = lax.optimization_barrier((faults, came["gy"][0]))
-        return exchange(faults), came["gx"], came["gy"] + came["gz"]
-
-    def stencil(residual, direction, came, solution):
-        more = [] if solution is None else [solution]
-        return pl.pallas_call(
-            functools.partial(stencil_kernel, dims, has_b, solution is None),
-            out_shape=[field_type, field_type],
-            in_specs=[vmem] * (3 + len(came) + len(more)),
-            out_specs=[vmem] * 2,
-            input_output_aliases={1: 0, 3 + len(came): 1} if more else {1: 0},
-            compiler_params=params,
-            cost_estimate=pl.CostEstimate(
-                flops=20 * columns * cells, bytes_accessed=12 * columns * cells, transcendentals=0
-            ),
-            name="stencil",
-        )(ops, residual, direction, *came, *more)
-
-    ops, residual, direction, *faces = pl.pallas_call(
-        functools.partial(setup_kernel, dims, has_b),
-        out_shape=[jax.ShapeDtypeStruct((10, lines, size_z), F32), field_type, field_type] + face_types,
-        in_specs=[vmem] * 4 + [anywhere] * 5 + [vmem] * len(edges),
-        out_specs=[vmem] * (3 + len(face_types)),
-        scratch_shapes=[pltpu.VMEM(shape2, F32)] * 4
-        + [pltpu.SemaphoreType.DMA((5,))],
-        compiler_params=params,
-        name="setup",
-    )(
-        shift_table.reshape(1, -1), shift_index.reshape(1, 1), recv, weight,
-        *in_hbm(*trans, pore_volume.reshape(shape2), start), *edges,
-    )
     plane = full_y * full_z
     well_x = well_cells // plane
     well_y = well_cells // full_z % full_y
@@ -657,27 +636,95 @@
     count = basis.shape[0]
     blocks = count // LANES
     early_rows = LANES * (blocks * (blocks + 1) // 2 + -(-blocks // (LANES // wells)))
-    extra = -(-early_rows // devices)
-    flat_basis_type = pltpu.HBM((count, cells), BF16)
-    parts, flat_basis = pl.pallas_call(
-        functools.partial(basis_kernel, dims),
-        out_shape=[jax.ShapeDtypeStruct((devices * extra, LANES), F32), flat_basis_type],
-        in_specs=[vmem, anywhere],
-        out_specs=[vmem, anywhere],
-        scratch_shapes=[
-            pltpu.VMEM((count, lines, size_z), BF16),
-            pltpu.VMEM((count, cells), BF16),
-            pltpu.VMEM((cells, wells), BF16),
-            pltpu.SemaphoreType.DMA((count // 16,)),
-            pltpu.SemaphoreType.DMA((count // 16,)),
-        ],
-        compiler_params=wide_params,
-        cost_estimate=pl.CostEstimate(
-            flops=2 * count * cells * (count + wells), bytes_accessed=4 * count * cells, transcendentals=0
-        ),
-        name="basis_gram",
-    )(well_local, *in_hbm(basis.reshape(count, lines, size_z)))
-
+    groups = 2
+    extra = -(-early_rows // (2 * groups * devices))
+    half_rows = groups * devices * extra
+    parity = [i // sizes[2] % sizes[1] % 2 for i in range(devices)]
+    flats, parts = [], []
+    for piece in range(blocks):
+        last = piece == blocks - 1
+        shapes = [(half_rows, LANES)] * 2 if last else [((piece + 1) * LANES, LANES), (LANES, wells)]
+        before = parts if last else []
+        flat_piece, *part = pl.pallas_call(
+            functools.partial(basis_kernel, dims, piece, blocks),
+            out_shape=[pltpu.HBM((LANES, cells), BF16)] + [jax.ShapeDtypeStruct(shape, F32) for shape in shapes],
+            in_specs=[vmem] + [anywhere] * (1 + piece) + [vmem] * len(before),
+            out_specs=[anywhere, vmem, vmem],
+            scratch_shapes=[
+                pltpu.VMEM((LANES, lines, size_z), BF16),
+                pltpu.VMEM((cells, wells), BF16),
+                pltpu.VMEM((LANES, cells), BF16),
+                pltpu.SemaphoreType.DMA((LANES // 16,)),
+                pltpu.SemaphoreType.DMA((LANES // 32,)),
+            ]
+            + [pltpu.VMEM((LANES, cells), BF16)] * piece
+            + [pltpu.SemaphoreType.DMA((max(piece, 1),))]
+            + [pltpu.VMEM((2 * half_rows, LANES), F32)] * last,
+            compiler_params=wide_params,
+            cost_estimate=pl.CostEstimate(
+                flops=2 * LANES * cells * ((piece + 1) * LANES + wells),
+                bytes_accessed=4 * LANES * cells,
+                transcendentals=0,
+            ),
+            name="basis_gram",
+        )(well_local, *in_hbm(basis.reshape(count, lines, size_z), *flats), *before)
+        flats.append(flat_piece)
+        if not piece:
+            part[0], *edges = lax.optimization_barrier((part[0], *edges))
+        parts += part
+
+    keep_parts, give_parts = parts[-2:]
+
+    def gather(direction, goes, source, group):
+        sent_rows = devices * (rows + (extra if goes else 0))
+        return pl.pallas_call(
+            functools.partial(gather_kernel, dims, (extra, goes, parity, group * devices * extra)),
+            out_shape=jax.ShapeDtypeStruct((sent_rows, LANES), F32),
+            in_specs=[vmem] * (2 + len(source)),
+            out_specs=vmem,
+            compiler_params=params,
+            cost_estimate=pl.CostEstimate(
+                flops=4 * columns * cells * total, bytes_accessed=4 * columns * cells, transcendentals=0
+            ),
+            name="fault_gather",
+        )(direction, send, *source)
+
+    def transfers(faults, faces):
+        faces = list(faces)
+        came = {}
+        for axis, more in zip(AXES, has_b):
+            came[axis] = [swap_even(faces.pop(0), axis)] + ([swap_odd(faces.pop(0), axis)] if more else [])
+        faults, came["gy"][0] = lax.optimization_barrier((faults, came["gy"][0]))
+        return exchange(faults), came["gx"], came["gy"] + came["gz"]
+
+    def stencil(residual, direction, came, solution):
+        more = [] if solution is None else [solution]
+        return pl.pallas_call(
+            functools.partial(stencil_kernel, dims, has_b, solution is None),
+            out_shape=[field_type, field_type],
+            in_specs=[vmem] * (3 + len(came) + len(more)),
+            out_specs=[vmem] * 2,
+            input_output_aliases={1: 0, 3 + len(came): 1} if more else {1: 0},
+            compiler_params=params,
+            cost_estimate=pl.CostEstimate(
+                flops=20 * columns * cells, bytes_accessed=12 * columns * cells, transcendentals=0
+            ),
+            name="stencil",
+        )(ops, residual, direction, *came, *more)
+
+    ops, residual, direction, *faces = pl.pallas_call(
+        functools.partial(setup_kernel, dims, has_b),
+        out_shape=[jax.ShapeDtypeStruct((10, lines, size_z), F32), field_type, field_type] + face_types,
+        in_specs=[vmem] * 4 + [anywhere] * 5 + [vmem] * len(edges),
+        out_specs=[vmem] * (3 + len(face_types)),
+        scratch_shapes=[pltpu.VMEM(shape2, F32)] * 4
+        + [pltpu.SemaphoreType.DMA((5,))],
+        compiler_params=params,
+        name="setup",
+    )(
+        shift_table.reshape(1, -1), shift_index.reshape(1, 1), recv, weight,
+        *in_hbm(*trans, pore_volume.reshape(shape2), start), *edges,
+    )
     needed = columns * (2 * blocks + 2)
     per_device = 1 << (-(-needed // devices) - 1).bit_length()
     sums_type = jax.ShapeDtypeStruct((devices * per_device, LANES), F32)
@@ -685,22 +732,26 @@
     sigma = 1.0 / 0.9
     weight_now = 1.0 / sigma
     solution = None
+    tables = {}
+    came_parts = swap_even(give_parts, "gy")
     for number in range(TERMS - 1):
-        goes = {2: "parts", 3: "sums"}.get(number, "")
-        faults = gather(direction, goes, [parts] if goes == "parts" else [table] if goes else [])
+        goes = ("", "parts", "sums", "")[number // 2]
+        group = number % groups
+        source = {"parts": [keep_parts, came_parts], "sums": [tables.get(group)]}.get(goes, [])
+        faults = gather(direction, goes, source, group)
         arrived, came, far = transfers(faults, faces)
         residual, solution = stencil(residual, direction, came, solution)
         weight_new = 1.0 / (2.0 * sigma - weight_now)
         last_round = number == TERMS - 2
         body = functools.partial(
             update_kernel, dims, has_b, weight_new * weight_now, 2.0 * weight_new / 0.9,
-            last_round, (extra, goes),
+            last_round, (extra, goes, parity),
         )
         weight_now = weight_new
         scratch = [pltpu.VMEM((columns * lines // 2, 2 * size_z), F32)]
         out_types = [sums_type, flat_type] if last_round else []
         if goes:
-            table_rows = extra if goes == "parts" else devices * extra
+            table_rows = 2 * extra if goes == "parts" else devices * extra
             out_types.append(jax.ShapeDtypeStruct((table_rows, LANES), F32))
         operands = [ops, residual, direction, recv, weight, arrived, *far]
         aliases = {}
@@ -711,13 +762,10 @@
             aliases[1], aliases[2] = len(out_types), len(out_types) + 1
             out_types += [field_type, field_type] + face_types
         else:
-            operands += [well_local, *in_hbm(flat_basis)]
-            in_specs += [vmem, anywhere]
-            scratch += [
-                pltpu.VMEM((columns, lines, size_z), F32),
-                pltpu.VMEM((count, cells), BF16),
-                pltpu.SemaphoreType.DMA((1,)),
-            ]
+            operands += [well_local, *in_hbm(*flats)]
+            in_specs += [vmem] + [anywhere] * blocks
+            scratch.append(pltpu.VMEM((columns, lines, size_z), F32))
+            scratch += [pltpu.VMEM((LANES, cells), BF16)] * blocks + [pltpu.SemaphoreType.DMA((blocks,))]
         outs = pl.pallas_call(
             body,
             out_shape=out_types,
@@ -733,26 +781,28 @@
             break
         if goes:
             table, *outs = outs
+            tables[group] = table
         residual, direction, *faces = outs
 
     mine = exchange(sums).reshape(devices, per_device, LANES).sum(axis=0)
     sums = exchange(jnp.tile(mine, (devices, 1)))
 
+    mine = [tables[group] for group in range(groups)]
     scale = math.sqrt(full_x * full_y * full_z)
     new_block, first_coeffs, coeffs, well_resp = pl.pallas_call(
-        functools.partial(finish_kernel, dims, scale, wells),
+        functools.partial(finish_kernel, dims, scale, wells, blocks, groups),
         out_shape=[
             field_type,
             jax.ShapeDtypeStruct((columns, count), F32),
             jax.ShapeDtypeStruct((columns, count), F32),
             jax.ShapeDtypeStruct((columns, wells), F32),
         ],
-        in_specs=[vmem] * 3 + [anywhere],
+        in_specs=[vmem] * (2 + 2 * groups) + [anywhere] * blocks,
         out_specs=[vmem] * 4,
-        scratch_shapes=[pltpu.VMEM((count, cells), BF16), pltpu.SemaphoreType.DMA((1,))],
+        scratch_shapes=[pltpu.VMEM((LANES, cells), BF16)] * blocks + [pltpu.SemaphoreType.DMA((blocks,))],
         compiler_params=wide_params,
         name="finish",
-    )(sums, table, flat, *in_hbm(flat_basis))
+    )(sums, flat, *mine, *[swap_even(table, "gy") for table in mine], *in_hbm(*flats))
     return new_block.reshape(start_block.shape), first_coeffs.T, coeffs.T, well_resp.T
 
 

time: 156 us -> 153 us (0.981)
  blocking collectives: 19.3 us -> 10.1 us
  starting transfers between devices: 67.6 us -> 75 us
  waiting for transfers between devices: 25.4 us -> 23.3 us
  local copies, waits for them, and re-layouts: 2.26 us -> 0.65 us
    all_to_all x2 -> x1, blocking collectives: 19.3 us -> 10.1 us  [exchange(): return lax.all_to_all(value, AXES, split_axis=0, concat_axis=0, tiled=True)]
    all_to_all x7 -> x8, starting transfers between devices: 22.3 us -> 30.4 us  [exchange(): return lax.all_to_all(value, AXES, split_axis=0, concat_axis=0, tiled=True)]
    ppermute x24 -> x27, starting transfers between devices: 29.6 us -> 26.3 us  [swap_even(): return lax.ppermute(value, axis, pairs)]
    all_to_all x7 -> x8, waiting for transfers between devices: 7.94 us -> 11.1 us  [exchange(): return lax.all_to_all(value, AXES, split_axis=0, concat_axis=0, tiled=True)]
    ppermute x24 -> x27, waiting for transfers between devices: 11.8 us -> 8.96 us  [swap_even(): return lax.ppermute(value, axis, pairs)]
    ppermute x16, starting transfers between devices: 15.6 us -> 18.2 us  [swap_odd(): return lax.ppermute(value, names, pairs)]
    ppermute x16, waiting for transfers between devices: 5.72 us -> 3.17 us  [swap_odd(): return lax.ppermute(value, names, pairs)]
    pallas_call x9 -> x10, Pallas kernels: 19.7 us -> 21.5 us  [the longest x7 8.57 us: gather(): pl.pallas_call(functools.partial(gather_kernel, dims, (extra, goes, parit...]
  transfers between devices with their start and end apart: 47 -> 51, of which waited for: 19 -> 21; matrix products, arithmetic and copies ran while one was open for 0% -> 0% of each run, Pallas kernels for 12% -> 15%
where the time goes in v3:
time: 153 us; the launch traced here: 152 us
  starting transfers between devices  75 us (49%)
  Pallas kernels  40.3 us (26%)
  waiting for transfers between devices  23.3 us (15%)
  blocking collectives  10.1 us (7%)
  between operations  1.83 us (1%)
    all_to_all x8, starting transfers between devices, exchange(): return lax.all_to_all(value, AXES, split_axis=0, concat_axis=0, tiled=True)  30.4 us
    ppermute x27, starting transfers between devices, swap_even(): return lax.ppermute(value, axis, pairs)  26.3 us
    ppermute x16, starting transfers between devices, swap_odd(): return lax.ppermute(value, names, pairs)  18.2 us
    pallas_call x7, Pallas kernels, local(): pl.pallas_call(body, out_shape=out_types, in_specs=in_specs, out_specs=[v...  12.4 us
    all_to_all x8, waiting for transfers between devices, exchange(): return lax.all_to_all(value, AXES, split_axis=0, concat_axis=0, tiled=True)  11.1 us
    all_to_all x1, blocking collectives, exchange(): return lax.all_to_all(value, AXES, split_axis=0, concat_axis=0, tiled=True)  10.1 us
    ppermute x27, waiting for transfers between devices, swap_even(): return lax.ppermute(value, axis, pairs)  8.96 us
    pallas_call x7, Pallas kernels, gather(): pl.pallas_call(functools.partial(gather_kernel, dims, (extra, goes, parit...  8.57 us
  transfers between devices with their start and end apart: 51, of which 21 were waited for; matrix products, arithmetic and copies ran while one was open for 0% of the time, Pallas kernels for 15%

profile of v3, /device:TPU:0, one launch (start us, length us, event | category | flops | bytes accessed | tf_op | source)
XLA Modules:
  0.0 151.9 jit_solution(4412912425323761781)
XLA Ops:
  1.7 3.0 %collective-permute-start.4 = (f32[1,64]{1,0:T(1,128)S(1)}, f32[1,64]{1,0:T(1,128)S(1)}, u32[]{:S(2)}, u32[]{:S(2)}) collective-permute-start(f32[1,64]{1,0:T(1,128)S(1)} %get-tuple-element.115), channel_id=1, source_target_pairs={{0,16},{1,2},{2,1},{3,19},{16,0},{17,18},{18,17},{19,3},{4,20},{5,... | collective-permute-start | bytes 776 | tf_op jit(solution)/shard_map/ppermute | solution.py:41
  4.7 1.7 %collective-permute-start.3 = (f32[1,64]{1,0:T(1,128)S(1)}, f32[1,64]{1,0:T(1,128)S(1)}, u32[]{:S(2)}, u32[]{:S(2)}) collective-permute-start(f32[1,64]{1,0:T(1,128)S(1)} %get-tuple-element.115), channel_id=1, source_target_pairs={{0,1},{1,0},{2,3},{3,2},{4,5},{5,4},{6,7},{7,6},{8,9},{9,8},{10,11... | collective-permute-start | bytes 776 | tf_op jit(solution)/shard_map/ppermute | solution.py:21
  10.2 3.5 %basis_gram.2 = (bf16[128,8192]{1,0:T(8,128)(2,1)}, f32[128,128]{1,0:T(8,128)S(1)}, f32[128,64]{1,0:T(8,128)S(1)}) custom-call(s32[1,64]{1,0:T(1,128)S(1)} %fusion.4.refs_0_.refs_11_, bf16[256,64,128]{2,1,0:T(8,128)(2,1)} %bitcast.41), custom_call_target="tpu_custom_call" | custom-call | flops 402653184 | bytes 4194304 | tf_op jit(solution)/shard_map/basis_gram/pallas_call | solution.py:648
  17.8 2.9 %all-to-all-start = ((f32[32,4,128]{2,1,0:T(4,128)}), f32[32,4,128]{2,1,0:T(4,128)S(1)}, u32[]{:S(2)}, u32[]{:S(2)}) async-start(f32[32,4,128]{2,1,0:T(4,128)} %bitcast.9), calls=%async_computation | async-start | bytes 131072 | tf_op jit(solution)/shard_map/all_to_all | solution.py:45
  20.6 1.8 %collective-permute-start.8 = (f32[1,1024]{1,0:T(1,128)S(1)}, f32[1,1024]{1,0:T(1,128)S(1)}, u32[]{:S(2)}, u32[]{:S(2)}) collective-permute-start(f32[1,1024]{1,0:T(1,128)S(1)} %get-tuple-element.131), channel_id=1, source_target_pairs={{0,1},{1,0},{2,3},{3,2},{4,5},{5,4},{6,7},{7,6},{8,9},{9,8},{10,11... | collective-permute-start | bytes 12296 | tf_op jit(solution)/shard_map/ppermute | solution.py:21
  24.5 4.4 %basis_gram.3 = (bf16[128,8192]{1,0:T(8,128)(2,1)}, f32[256,128]{1,0:T(8,128)S(1)}, f32[256,128]{1,0:T(8,128)S(1)}) custom-call(s32[1,64]{1,0:T(1,128)S(1)} %fusion.4.refs_0_.refs_11_, bf16[256,64,128]{2,1,0:T(8,128)(2,1)} %bitcast.42, bf16[128,8192]{1,0:T(8,128)(2,1)} %get-tuple-element.149.refs_2_.refs_12_.refs_4_, ...), custom_call_target="tpu_custom_call" | custom-call | flops 671088640 | bytes 4194304 | tf_op jit(solution)/shard_map/basis_gram/pallas_call | solution.py:648
  34.0 3.5 %all-to-all-start.1 = ((f32[32,4,128]{2,1,0:T(4,128)}), f32[32,4,128]{2,1,0:T(4,128)S(1)}, u32[]{:S(2)}, u32[]{:S(2)}) async-start(f32[32,4,128]{2,1,0:T(4,128)} %bitcast.11), calls=%async_computation.1 | async-start | bytes 131072 | tf_op jit(solution)/shard_map/all_to_all | solution.py:45
  47.4 2.9 %all-to-all-start.2 = ((f32[32,8,128]{2,1,0:T(8,128)}), f32[32,8,128]{2,1,0:T(8,128)S(1)}, u32[]{:S(2)}, u32[]{:S(2)}) async-start(f32[32,8,128]{2,1,0:T(8,128)} %bitcast.13), calls=%async_computation.2 | async-start | bytes 262144 | tf_op jit(solution)/shard_map/all_to_all | solution.py:45
  50.3 1.8 %collective-permute-start.15 = (f32[16,16,128]{2,1,0:T(8,128)S(1)}, f32[16,16,128]{2,1,0:T(8,128)S(1)}, u32[]{:S(2)}, u32[]{:S(2)}) collective-permute-start(f32[16,16,128]{2,1,0:T(8,128)S(1)} %get-tuple-element.146), channel_id=1, source_target_pairs={{0,16},{16,0},{1,17},{17,1},{2,18},{18,2},{3,19},{19,3},{4,20},{20... | collective-permute-start | bytes 393224 | tf_op jit(solution)/shard_map/ppermute | solution.py:21
  52.4 1.8 %collective-permute-start.19 = (f32[1,1024]{1,0:T(1,128)S(1)}, f32[1,1024]{1,0:T(1,128)S(1)}, u32[]{:S(2)}, u32[]{:S(2)}) collective-permute-start(f32[1,1024]{1,0:T(1,128)S(1)} %get-tuple-element.158), channel_id=1, source_target_pairs={{0,1},{1,0},{2,3},{3,2},{4,5},{5,4},{6,7},{7,6},{8,9},{9,8},{10,11... | collective-permute-start | bytes 12296 | tf_op jit(solution)/shard_map/ppermute | solution.py:21
  61.4 4.5 %all-to-all-start.3 = ((f32[32,8,128]{2,1,0:T(8,128)}), f32[32,8,128]{2,1,0:T(8,128)S(1)}, u32[]{:S(2)}, u32[]{:S(2)}) async-start(f32[32,8,128]{2,1,0:T(8,128)} %bitcast.15), calls=%async_computation.3 | async-start | bytes 262144 | tf_op jit(solution)/shard_map/all_to_all | solution.py:45
  65.9 1.8 %collective-permute-start.21 = (f32[16,16,128]{2,1,0:T(8,128)S(1)}, f32[16,16,128]{2,1,0:T(8,128)S(1)}, u32[]{:S(2)}, u32[]{:S(2)}) collective-permute-start(f32[16,16,128]{2,1,0:T(8,128)S(1)} %get-tuple-element.162), channel_id=1, source_target_pairs={{0,16},{16,0},{1,17},{17,1},{2,18},{18,2},{3,19},{19,3},{4,20},{20... | collective-permute-start | bytes 393224 | tf_op jit(solution)/shard_map/ppermute | solution.py:21
  68.0 1.8 %collective-permute-start.24 = (f32[1,1024]{1,0:T(1,128)S(1)}, f32[1,1024]{1,0:T(1,128)S(1)}, u32[]{:S(2)}, u32[]{:S(2)}) collective-permute-start(f32[1,1024]{1,0:T(1,128)S(1)} %get-tuple-element.169), channel_id=1, source_target_pairs={{0,1},{1,0},{2,3},{3,2},{4,5},{5,4},{6,7},{7,6},{8,9},{9,8},{10,11... | collective-permute-start | bytes 12296 | tf_op jit(solution)/shard_map/ppermute | solution.py:21
  76.9 4.5 %all-to-all-start.4 = ((f32[32,8,128]{2,1,0:T(8,128)}), f32[32,8,128]{2,1,0:T(8,128)S(1)}, u32[]{:S(2)}, u32[]{:S(2)}) async-start(f32[32,8,128]{2,1,0:T(8,128)} %bitcast.17), calls=%async_computation.4 | async-start | bytes 262144 | tf_op jit(solution)/shard_map/all_to_all | solution.py:45
  81.5 1.8 %collective-permute-start.26 = (f32[16,16,128]{2,1,0:T(8,128)S(1)}, f32[16,16,128]{2,1,0:T(8,128)S(1)}, u32[]{:S(2)}, u32[]{:S(2)}) collective-permute-start(f32[16,16,128]{2,1,0:T(8,128)S(1)} %get-tuple-element.173), channel_id=1, source_target_pairs={{0,16},{16,0},{1,17},{17,1},{2,18},{18,2},{3,19},{19,3},{4,20},{20... | collective-permute-start | bytes 393224 | tf_op jit(solution)/shard_map/ppermute | solution.py:21
  83.6 1.8 %collective-permute-start.29 = (f32[1,1024]{1,0:T(1,128)S(1)}, f32[1,1024]{1,0:T(1,128)S(1)}, u32[]{:S(2)}, u32[]{:S(2)}) collective-permute-start(f32[1,1024]{1,0:T(1,128)S(1)} %get-tuple-element.181), channel_id=1, source_target_pairs={{0,1},{1,0},{2,3},{3,2},{4,5},{5,4},{6,7},{7,6},{8,9},{9,8},{10,11... | collective-permute-start | bytes 12296 | tf_op jit(solution)/shard_map/ppermute | solution.py:21
  92.5 4.8 %all-to-all-start.5 = ((f32[32,8,128]{2,1,0:T(8,128)}), f32[32,8,128]{2,1,0:T(8,128)S(1)}, u32[]{:S(2)}, u32[]{:S(2)}) async-start(f32[32,8,128]{2,1,0:T(8,128)} %bitcast.19), calls=%async_computation.5 | async-start | bytes 262144 | tf_op jit(solution)/shard_map/all_to_all | solution.py:45
  108.9 4.7 %all-to-all-start.6 = ((f32[32,4,128]{2,1,0:T(4,128)}), f32[32,4,128]{2,1,0:T(4,128)S(1)}, u32[]{:S(2)}, u32[]{:S(2)}) async-start(f32[32,4,128]{2,1,0:T(4,128)} %bitcast.21), calls=%async_computation.6 | async-start | bytes 131072 | tf_op jit(solution)/shard_map/all_to_all | solution.py:45
  113.6 1.8 %collective-permute-start.38 = (f32[4,16,128]{2,1,0:T(8,128)S(1)}, f32[4,16,128]{2,1,0:T(8,128)S(1)}, u32[]{:S(2)}, u32[]{:S(2)}) collective-permute-start(f32[4,16,128]{2,1,0:T(8,128)S(1)} %get-tuple-element.203), channel_id=1, source_target_pairs={{0,16},{4,8},{8,4},{12,28},{16,0},{20,24},{24,20},{28,12},{1,17},{... | collective-permute-start | bytes 98312 | tf_op jit(solution)/shard_map/ppermute | solution.py:41
  121.2 4.7 %update.13 = (f32[128,128]{1,0:T(8,128)S(1)}, f32[16,8192]{1,0:T(8,128)S(1)}) custom-call(f32[10,64,128]{2,1,0:T(8,128)S(1)} %get-tuple-element.121.refs_0_, f32[16,64,128]{2,1,0:T(8,128)S(1)} %get-tuple-element.199.refs_1_, f32[16,64,128]{2,1,0:T(8,128)S(1)} %get-tuple-element.196.refs_2_.refs_0_, s32[1,1024]{1,0:T(1,128)S(1)} %get-tuple-element.110.refs_2_.refs_3_, ...), custom_call_target="tpu_custom_call" | custom-call | tf_op jit(solution)/shard_map/update/pallas_call | solution.py:769
  125.9 10.1 %all_to_all.94 = f32[32,4,128]{2,1,0:T(4,128)S(1)} all-to-all(f32[32,4,128]{2,1,0:T(4,128)S(1)} %bitcast.39), channel_id=1, replica_groups=mesh['gx'=2,'gy'=4,'gz'=4] {'gx','gy','gz'}, dimensions={0} | all-to-all | bytes 131072 | tf_op jit(solution)/shard_map/all_to_all | solution.py:45
  136.7 2.6 %all-to-all-start.8 = ((f32[32,4,128]{2,1,0:T(4,128)}), f32[32,4,128]{2,1,0:T(4,128)S(1)}, u32[]{:S(2)}, u32[]{:S(2)}) async-start(f32[32,4,128]{2,1,0:T(4,128)} %tile.2), calls=%async_computation.8 | async-start | bytes 131072 | tf_op jit(solution)/shard_map/all_to_all | solution.py:45
  140.8 6.0 %all-to-all-done.8 = f32[32,4,128]{2,1,0:T(4,128)S(1)} async-done(((f32[32,4,128]{2,1,0:T(4,128)}), f32[32,4,128]{2,1,0:T(4,128)S(1)}, u32[]{:S(2)}, u32[]{:S(2)}) %all-to-all-start.8) | async-done | bytes 65568 | tf_op jit(solution)/shard_map/all_to_all | solution.py:45
  146.8 5.0 %finish.1 = (f32[16,64,128]{2,1,0:T(8,128)}, f32[16,256]{1,0:T(8,128)}, f32[16,256]{1,0:T(8,128)}, f32[16,64]{1,0:T(8,128)}) custom-call(f32[128,128]{1,0:T(8,128)S(1)} %bitcast.36, f32[16,8192]{1,0:T(8,128)S(1)} %get-tuple-element.209.flat_ref, f32[128,128]{1,0:T(8,128)S(1)} %get-tuple-element.210.refs_0_, f32[128,128]{1,0:T(8,128)S(1)} %get-tuple-element.211.refs_1_, ...), custom_call_target="tpu_custom_call" | custom-call | tf_op jit(solution)/shard_map/finish/pallas_call | solution.py:792
  (110 shorter events, 66.8 us)
Async XLA Ops:
  1.7 12.6 %collective-permute-start.4 = (f32[1,64]{1,0:T(1,128)S(1)}, f32[1,64]{1,0:T(1,128)S(1)}, u32[]{:S(2)}, u32[]{:S(2)}) collective-permute-start(f32[1,64]{1,0:T(1,128)S(1)} %get-tuple-element.115), channel_id=1, source_target_pairs={{0,16},{1,2},{2,1},{3,19},{16,0},{17,18},{18,17},{19,3},{4,20},{5,... | collective-permute-start | bytes 776 | tf_op jit(solution)/shard_map/ppermute | solution.py:41
  4.7 9.6 %collective-permute-start.3 = (f32[1,64]{1,0:T(1,128)S(1)}, f32[1,64]{1,0:T(1,128)S(1)}, u32[]{:S(2)}, u32[]{:S(2)}) collective-permute-start(f32[1,64]{1,0:T(1,128)S(1)} %get-tuple-element.115), channel_id=1, source_target_pairs={{0,1},{1,0},{2,3},{3,2},{4,5},{5,4},{6,7},{7,6},{8,9},{9,8},{10,11... | collective-permute-start | bytes 776 | tf_op jit(solution)/shard_map/ppermute | solution.py:21
  6.3 8.0 %collective-permute-start.2 = (f32[4,128]{1,0:T(4,128)S(1)}, f32[4,128]{1,0:T(4,128)S(1)}, u32[]{:S(2)}, u32[]{:S(2)}) collective-permute-start(f32[4,128]{1,0:T(4,128)S(1)} %get-tuple-element.114), channel_id=1, source_target_pairs={{0,16},{4,8},{8,4},{12,28},{16,0},{20,24},{24,20},{28,12},{1,17},{... | collective-permute-start | bytes 6152 | tf_op jit(solution)/shard_map/ppermute | solution.py:41
  15.9 14.1 %collective-permute-start.5 = (f32[16,16,128]{2,1,0:T(8,128)S(1)}, f32[16,16,128]{2,1,0:T(8,128)S(1)}, u32[]{:S(2)}, u32[]{:S(2)}) collective-permute-start(f32[16,16,128]{2,1,0:T(8,128)S(1)} %get-tuple-element.124), channel_id=1, source_target_pairs={{0,16},{16,0},{1,17},{17,1},{2,18},{18,2},{3,19},{19,3},{4,20},{20... | collective-permute-start | bytes 393224 | tf_op jit(solution)/shard_map/ppermute | solution.py:21
  17.8 12.8 %all-to-all-start = ((f32[32,4,128]{2,1,0:T(4,128)}), f32[32,4,128]{2,1,0:T(4,128)S(1)}, u32[]{:S(2)}, u32[]{:S(2)}) async-start(f32[32,4,128]{2,1,0:T(4,128)} %bitcast.9), calls=%async_computation | async-start | bytes 131072 | tf_op jit(solution)/shard_map/all_to_all | solution.py:45
  20.6 9.9 %collective-permute-start.8 = (f32[1,1024]{1,0:T(1,128)S(1)}, f32[1,1024]{1,0:T(1,128)S(1)}, u32[]{:S(2)}, u32[]{:S(2)}) collective-permute-start(f32[1,1024]{1,0:T(1,128)S(1)} %get-tuple-element.131), channel_id=1, source_target_pairs={{0,1},{1,0},{2,3},{3,2},{4,5},{5,4},{6,7},{7,6},{8,9},{9,8},{10,11... | collective-permute-start | bytes 12296 | tf_op jit(solution)/shard_map/ppermute | solution.py:21
  22.5 8.1 %collective-permute-start.9 = (f32[1,1024]{1,0:T(1,128)S(1)}, f32[1,1024]{1,0:T(1,128)S(1)}, u32[]{:S(2)}, u32[]{:S(2)}) collective-permute-start(f32[1,1024]{1,0:T(1,128)S(1)} %get-tuple-element.132), channel_id=1, source_target_pairs={{0,16},{1,2},{2,1},{3,19},{16,0},{17,18},{18,17},{19,3},{4,20},{5,... | collective-permute-start | bytes 12296 | tf_op jit(solution)/shard_map/ppermute | solution.py:41
  23.9 6.6 %collective-permute-start.7 = (f32[4,16,128]{2,1,0:T(8,128)S(1)}, f32[4,16,128]{2,1,0:T(8,128)S(1)}, u32[]{:S(2)}, u32[]{:S(2)}) collective-permute-start(f32[4,16,128]{2,1,0:T(8,128)S(1)} %get-tuple-element.130), channel_id=1, source_target_pairs={{0,16},{4,8},{8,4},{12,28},{16,0},{20,24},{24,20},{28,12},{1,17},{... | collective-permute-start | bytes 98312 | tf_op jit(solution)/shard_map/ppermute | solution.py:41
  28.9 17.2 %collective-permute-start.16 = (f32[256,128]{1,0:T(8,128)S(1)}, f32[256,128]{1,0:T(8,128)S(1)}, u32[]{:S(2)}, u32[]{:S(2)}) collective-permute-start(f32[256,128]{1,0:T(8,128)S(1)} %get-tuple-element.153), channel_id=1, source_target_pairs={{0,4},{4,0},{8,12},{12,8},{1,5},{5,1},{9,13},{13,9},{2,6},{6,2},{1... | collective-permute-start | bytes 393224 | tf_op jit(solution)/shard_map/ppermute | solution.py:21
  31.9 9.4 %collective-permute-start.10 = (f32[16,16,128]{2,1,0:T(8,128)S(1)}, f32[16,16,128]{2,1,0:T(8,128)S(1)}, u32[]{:S(2)}, u32[]{:S(2)}) collective-permute-start(f32[16,16,128]{2,1,0:T(8,128)S(1)} %get-tuple-element.135), channel_id=1, source_target_pairs={{0,16},{16,0},{1,17},{17,1},{2,18},{18,2},{3,19},{19,3},{4,20},{20... | collective-permute-start | bytes 393224 | tf_op jit(solution)/shard_map/ppermute | solution.py:21
  34.0 10.9 %all-to-all-start.1 = ((f32[32,4,128]{2,1,0:T(4,128)}), f32[32,4,128]{2,1,0:T(4,128)S(1)}, u32[]{:S(2)}, u32[]{:S(2)}) async-start(f32[32,4,128]{2,1,0:T(4,128)} %bitcast.11), calls=%async_computation.1 | async-start | bytes 131072 | tf_op jit(solution)/shard_map/all_to_all | solution.py:45
  37.5 6.7 %collective-permute-start.12 = (f32[4,16,128]{2,1,0:T(8,128)S(1)}, f32[4,16,128]{2,1,0:T(8,128)S(1)}, u32[]{:S(2)}, u32[]{:S(2)}) collective-permute-start(f32[4,16,128]{2,1,0:T(8,128)S(1)} %get-tuple-element.141), channel_id=1, source_target_pairs={{0,16},{4,8},{8,4},{12,28},{16,0},{20,24},{24,20},{28,12},{1,17},{... | collective-permute-start | bytes 98312 | tf_op jit(solution)/shard_map/ppermute | solution.py:41
  47.4 11.4 %all-to-all-start.2 = ((f32[32,8,128]{2,1,0:T(8,128)}), f32[32,8,128]{2,1,0:T(8,128)S(1)}, u32[]{:S(2)}, u32[]{:S(2)}) async-start(f32[32,8,128]{2,1,0:T(8,128)} %bitcast.13), calls=%async_computation.2 | async-start | bytes 262144 | tf_op jit(solution)/shard_map/all_to_all | solution.py:45
  50.3 6.8 %collective-permute-start.15 = (f32[16,16,128]{2,1,0:T(8,128)S(1)}, f32[16,16,128]{2,1,0:T(8,128)S(1)}, u32[]{:S(2)}, u32[]{:S(2)}) collective-permute-start(f32[16,16,128]{2,1,0:T(8,128)S(1)} %get-tuple-element.146), channel_id=1, source_target_pairs={{0,16},{16,0},{1,17},{17,1},{2,18},{18,2},{3,19},{19,3},{4,20},{20... | collective-permute-start | bytes 393224 | tf_op jit(solution)/shard_map/ppermute | solution.py:21
  61.4 13.0 %all-to-all-start.3 = ((f32[32,8,128]{2,1,0:T(8,128)}), f32[32,8,128]{2,1,0:T(8,128)S(1)}, u32[]{:S(2)}, u32[]{:S(2)}) async-start(f32[32,8,128]{2,1,0:T(8,128)} %bitcast.15), calls=%async_computation.3 | async-start | bytes 262144 | tf_op jit(solution)/shard_map/all_to_all | solution.py:45
  65.9 6.8 %collective-permute-start.21 = (f32[16,16,128]{2,1,0:T(8,128)S(1)}, f32[16,16,128]{2,1,0:T(8,128)S(1)}, u32[]{:S(2)}, u32[]{:S(2)}) collective-permute-start(f32[16,16,128]{2,1,0:T(8,128)S(1)} %get-tuple-element.162), channel_id=1, source_target_pairs={{0,16},{16,0},{1,17},{17,1},{2,18},{18,2},{3,19},{19,3},{4,20},{20... | collective-permute-start | bytes 393224 | tf_op jit(solution)/shard_map/ppermute | solution.py:21
  76.9 13.0 %all-to-all-start.4 = ((f32[32,8,128]{2,1,0:T(8,128)}), f32[32,8,128]{2,1,0:T(8,128)S(1)}, u32[]{:S(2)}, u32[]{:S(2)}) async-start(f32[32,8,128]{2,1,0:T(8,128)} %bitcast.17), calls=%async_computation.4 | async-start | bytes 262144 | tf_op jit(solution)/shard_map/all_to_all | solution.py:45
  81.5 6.8 %collective-permute-start.26 = (f32[16,16,128]{2,1,0:T(8,128)S(1)}, f32[16,16,128]{2,1,0:T(8,128)S(1)}, u32[]{:S(2)}, u32[]{:S(2)}) collective-permute-start(f32[16,16,128]{2,1,0:T(8,128)S(1)} %get-tuple-element.173), channel_id=1, source_target_pairs={{0,16},{16,0},{1,17},{17,1},{2,18},{18,2},{3,19},{19,3},{4,20},{20... | collective-permute-start | bytes 393224 | tf_op jit(solution)/shard_map/ppermute | solution.py:21
  92.5 13.0 %all-to-all-start.5 = ((f32[32,8,128]{2,1,0:T(8,128)}), f32[32,8,128]{2,1,0:T(8,128)S(1)}, u32[]{:S(2)}, u32[]{:S(2)}) async-start(f32[32,8,128]{2,1,0:T(8,128)} %bitcast.19), calls=%async_computation.5 | async-start | bytes 262144 | tf_op jit(solution)/shard_map/all_to_all | solution.py:45
  97.3 6.6 %collective-permute-start.31 = (f32[16,16,128]{2,1,0:T(8,128)S(1)}, f32[16,16,128]{2,1,0:T(8,128)S(1)}, u32[]{:S(2)}, u32[]{:S(2)}) collective-permute-start(f32[16,16,128]{2,1,0:T(8,128)S(1)} %get-tuple-element.185), channel_id=1, source_target_pairs={{0,16},{16,0},{1,17},{17,1},{2,18},{18,2},{3,19},{19,3},{4,20},{20... | collective-permute-start | bytes 393224 | tf_op jit(solution)/shard_map/ppermute | solution.py:21
  106.9 10.6 %collective-permute-start.36 = (f32[16,16,128]{2,1,0:T(8,128)S(1)}, f32[16,16,128]{2,1,0:T(8,128)S(1)}, u32[]{:S(2)}, u32[]{:S(2)}) collective-permute-start(f32[16,16,128]{2,1,0:T(8,128)S(1)} %get-tuple-element.197), channel_id=1, source_target_pairs={{0,16},{16,0},{1,17},{17,1},{2,18},{18,2},{3,19},{19,3},{4,20},{20... | collective-permute-start | bytes 393224 | tf_op jit(solution)/shard_map/ppermute | solution.py:21
  108.9 12.2 %all-to-all-start.6 = ((f32[32,4,128]{2,1,0:T(4,128)}), f32[32,4,128]{2,1,0:T(4,128)S(1)}, u32[]{:S(2)}, u32[]{:S(2)}) async-start(f32[32,4,128]{2,1,0:T(4,128)} %bitcast.21), calls=%async_computation.6 | async-start | bytes 131072 | tf_op jit(solution)/shard_map/all_to_all | solution.py:45
  113.6 6.9 %collective-permute-start.38 = (f32[4,16,128]{2,1,0:T(8,128)S(1)}, f32[4,16,128]{2,1,0:T(8,128)S(1)}, u32[]{:S(2)}, u32[]{:S(2)}) collective-permute-start(f32[4,16,128]{2,1,0:T(8,128)S(1)} %get-tuple-element.203), channel_id=1, source_target_pairs={{0,16},{4,8},{8,4},{12,28},{16,0},{20,24},{24,20},{28,12},{1,17},{... | collective-permute-start | bytes 98312 | tf_op jit(solution)/shard_map/ppermute | solution.py:41
  136.7 10.1 %all-to-all-start.8 = ((f32[32,4,128]{2,1,0:T(4,128)}), f32[32,4,128]{2,1,0:T(4,128)S(1)}, u32[]{:S(2)}, u32[]{:S(2)}) async-start(f32[32,4,128]{2,1,0:T(4,128)} %tile.2), calls=%async_computation.8 | async-start | bytes 131072 | tf_op jit(solution)/shard_map/all_to_all | solution.py:45
  (28 other events, 103.4 us)

commit v4 on v3

--- a/solution.py
+++ b/solution.py
@@ -155,11 +155,23 @@
     return copies
 
 
+def local_wells(cell, dims):
+    _, size_x, size_y, size_z, _ = dims
+    full_y, full_z = size_y * lax.axis_size("gy"), size_z * lax.axis_size("gz")
+    at_x, at_y, at_z = cell // (full_y * full_z), cell // full_z % full_y, cell % full_z
+    owned = (
+        (at_x // size_x == lax.axis_index("gx"))
+        & (at_y // size_y == lax.axis_index("gy"))
+        & (at_z // size_z == lax.axis_index("gz"))
+    )
+    return jnp.where(owned, (at_x % size_x * size_y + at_y % size_y) * size_z + at_z % size_z, -1)
+
+
 def edges_kernel(dims, *refs):
     columns, size_x, size_y, size_z, slots = dims
-    ex_out, ey_out, ez_out = refs[6:9]
-    tables_out, held, sem = refs[9:12], refs[12:18], refs[18]
-    copies = start_copies(zip(refs[:6], held), sem)
+    ex_out, ey_out, ez_out = refs[7:10]
+    tables_out, wells_out, held, sem = refs[10:13], refs[13], refs[14:21], refs[21]
+    copies = start_copies(zip(refs[:7], held), sem)
     for copy in copies:
         copy.wait()
     tx, ty, tz = held[:3]
@@ -168,7 +180,8 @@
     for i in range(size_x):
         ey_out[i : i + 1, :] = ty[(i + 1) * size_y - 1 : (i + 1) * size_y, :]
     ez_out[...] = tz[...].T[size_z - 1 : size_z, :]
-    for table, out in zip(held[3:], tables_out):
+    wells_out[...] = local_wells(held[6][...], dims)
+    for table, out in zip(held[3:6], tables_out):
         value = table[0]
         out[...] = jnp.concatenate([value[i : i + 1, :] for i in range(value.shape[0])], axis=1)
 
@@ -520,14 +533,23 @@
     full = first + beyond
     square = block(2 * blocks)[:, :columns]
     at_wells = block(2 * blocks + 1)[:, :wells]
+    gram_parts = split_three(basis_gram)
+
+    def times_gram(value):
+        return sum(jnp.dot(value, part, preferred_element_type=F32) for part in gram_parts)
+
     first_round = first.astype(BF16)
-    second = full - exact_dot(first_round.astype(F32), basis_gram)
+    first_gram = times_gram(first_round)
+    second = full - first_gram
     second_round = second.astype(BF16)
-    taken = first_round.astype(F32) + second_round.astype(F32)
-    half = full - 0.5 * exact_dot(taken, basis_gram)
-    cross = exact_dot(taken, half, transposed=True)
+    rounds = jnp.concatenate([first_round, second_round], axis=0)
+    half = full - 0.5 * (first_gram + times_gram(second_round))
+    products = nt_dot(rounds, jnp.concatenate(split_three(half), axis=0))
+    products = products[:columns] + products[columns:]
+    cross = products[:, :columns] + products[:, columns : 2 * columns] + products[:, 2 * columns :]
     gram = square - cross - cross.T
-    rest_wells = at_wells - exact_dot(taken, wells_basis)
+    spans = jnp.dot(rounds, wells_basis.astype(BF16), preferred_element_type=F32)
+    rest_wells = at_wells - spans[:columns] - spans[columns:]
     first_out[...] = first
     coeffs_out[...] = first + second
     row = lax.broadcasted_iota(jnp.int32, (columns, columns), 0)
@@ -546,7 +568,6 @@
     factors = jnp.concatenate([high, high, low], axis=1)
     for copy in fetches:
         copy.wait()
-    rounds = jnp.concatenate([first_round, second_round], axis=0)
     step = min(8, lines)
     for begin in range(0, lines, step):
         lanes = slice(begin * size_z, (begin + step) * size_z)
@@ -580,7 +601,6 @@
     cells = lines * size_z
     total = devices * slots
     sizes = [lax.axis_size(axis) for axis in AXES]
-    index_x, index_y, index_z = (lax.axis_index(axis) for axis in AXES)
     full_x, full_y, full_z = size_x * sizes[0], size_y * sizes[1], size_z * sizes[2]
     has_b = tuple(size > 2 for size in sizes)
     dims = (columns, size_x, size_y, size_z, slots)
@@ -606,33 +626,22 @@
     edge_types = [
         jax.ShapeDtypeStruct(shape, F32) for shape in ((size_y, size_z), (size_x, size_z), (1, lines))
     ]
-    edge_x, edge_y, edge_z, send, recv, weight = pl.pallas_call(
+    wells = well_cells.shape[0]
+    edge_x, edge_y, edge_z, send, recv, weight, well_row = pl.pallas_call(
         functools.partial(edges_kernel, dims),
-        out_shape=edge_types + row_types,
-        in_specs=[anywhere] * 6,
-        out_specs=[vmem] * 6,
+        out_shape=edge_types + row_types + [jax.ShapeDtypeStruct((1, wells), jnp.int32)],
+        in_specs=[anywhere] * 7,
+        out_specs=[vmem] * 7,
         scratch_shapes=[pltpu.VMEM(shape2, F32)] * 3
         + [pltpu.VMEM(fault_send.shape, kind) for kind in (jnp.int32, jnp.int32, F32)]
-        + [pltpu.SemaphoreType.DMA((6,))],
+        + [pltpu.VMEM((1, wells), jnp.int32), pltpu.SemaphoreType.DMA((7,))],
         compiler_params=params,
         name="edges",
-    )(*in_hbm(*trans, fault_send, fault_recv, fault_trans))
+    )(*in_hbm(*trans, fault_send, fault_recv, fault_trans, well_cells.reshape(1, wells)))
     edges = []
     for axis, edge, more in zip(AXES, (edge_x, edge_y, edge_z), has_b):
         edges += [swap_even(edge, axis)] + ([swap_odd(edge, axis)] if more else [])
 
-    plane = full_y * full_z
-    well_x = well_cells // plane
-    well_y = well_cells // full_z % full_y
-    well_z = well_cells % full_z
-    owned = (
-        (well_x // size_x == index_x)
-        & (well_y // size_y == index_y)
-        & (well_z // size_z == index_z)
-    )
-    local_cell = (well_x % size_x * size_y + well_y % size_y) * size_z + well_z % size_z
-    wells = well_cells.shape[0]
-    well_local = jnp.where(owned, local_cell, -1).reshape(1, wells)
     count = basis.shape[0]
     blocks = count // LANES
     early_rows = LANES * (blocks * (blocks + 1) // 2 + -(-blocks // (LANES // wells)))
@@ -667,7 +676,7 @@
                 transcendentals=0,
             ),
             name="basis_gram",
-        )(well_local, *in_hbm(basis.reshape(count, lines, size_z), *flats), *before)
+        )(well_row, *in_hbm(basis.reshape(count, lines, size_z), *flats), *before)
         flats.append(flat_piece)
         if not piece:
             part[0], *edges = lax.optimization_barrier((part[0], *edges))
@@ -762,7 +771,7 @@
             aliases[1], aliases[2] = len(out_types), len(out_types) + 1
             out_types += [field_type, field_type] + face_types
         else:
-            operands += [well_local, *in_hbm(*flats)]
+            operands += [well_row, *in_hbm(*flats)]
             in_specs += [vmem] + [anywhere] * blocks
             scratch.append(pltpu.VMEM((columns, lines, size_z), F32))
             scratch += [pltpu.VMEM((LANES, cells), BF16)] * blocks + [pltpu.SemaphoreType.DMA((blocks,))]

time: 153 us -> 152 us (level)
  no operation moved by 1% of the time
where the time goes in v4:
time: 152 us; the launch traced here: 151 us
  starting transfers between devices  75 us (49%)
  Pallas kernels  40.2 us (26%)
  waiting for transfers between devices  23.3 us (15%)
  blocking collectives  10.1 us (7%)
  between operations  1.82 us (1%)
    all_to_all x8, starting transfers between devices, exchange(): return lax.all_to_all(value, AXES, split_axis=0, concat_axis=0, tiled=True)  30.4 us
    ppermute x27, starting transfers between devices, swap_even(): return lax.ppermute(value, axis, pairs)  26.3 us
    ppermute x16, starting transfers between devices, swap_odd(): return lax.ppermute(value, names, pairs)  18.2 us
    pallas_call x7, Pallas kernels, local(): pl.pallas_call(body, out_shape=out_types, in_specs=in_specs, out_specs=[v...  12.4 us
    all_to_all x8, waiting for transfers between devices, exchange(): return lax.all_to_all(value, AXES, split_axis=0, concat_axis=0, tiled=True)  11.1 us
    all_to_all x1, blocking collectives, exchange(): return lax.all_to_all(value, AXES, split_axis=0, concat_axis=0, tiled=True)  10.1 us
    ppermute x27, waiting for transfers between devices, swap_even(): return lax.ppermute(value, axis, pairs)  8.96 us
    pallas_call x7, Pallas kernels, gather(): pl.pallas_call(functools.partial(gather_kernel, dims, (extra, goes, parit...  8.57 us
  transfers between devices with their start and end apart: 51, of which 21 were waited for; matrix products, arithmetic and copies ran while one was open for 0% of the time, Pallas kernels for 15%

profile of v4, /device:TPU:0, one launch (start us, length us, event | category | flops | bytes accessed | tf_op | source)
XLA Modules:
  0.0 151.1 jit_solution(13107500715040988769)
XLA Ops:
  1.7 3.0 %collective-permute-start.4 = (f32[1,64]{1,0:T(1,128)S(1)}, f32[1,64]{1,0:T(1,128)S(1)}, u32[]{:S(2)}, u32[]{:S(2)}) collective-permute-start(f32[1,64]{1,0:T(1,128)S(1)} %get-tuple-element.117), channel_id=1, source_target_pairs={{0,16},{1,2},{2,1},{3,19},{16,0},{17,18},{18,17},{19,3},{4,20},{5,... | collective-permute-start | bytes 776 | tf_op jit(solution)/shard_map/ppermute | solution.py:41
  4.7 1.7 %collective-permute-start.3 = (f32[1,64]{1,0:T(1,128)S(1)}, f32[1,64]{1,0:T(1,128)S(1)}, u32[]{:S(2)}, u32[]{:S(2)}) collective-permute-start(f32[1,64]{1,0:T(1,128)S(1)} %get-tuple-element.117), channel_id=1, source_target_pairs={{0,1},{1,0},{2,3},{3,2},{4,5},{5,4},{6,7},{7,6},{8,9},{9,8},{10,11... | collective-permute-start | bytes 776 | tf_op jit(solution)/shard_map/ppermute | solution.py:21
  9.5 3.5 %basis_gram.2 = (bf16[128,8192]{1,0:T(8,128)(2,1)}, f32[128,128]{1,0:T(8,128)S(1)}, f32[128,64]{1,0:T(8,128)S(1)}) custom-call(s32[1,64]{1,0:T(1,128)S(1)} %get-tuple-element.113.refs_0_.refs_11_, bf16[256,64,128]{2,1,0:T(8,128)(2,1)} %bitcast.40), custom_call_target="tpu_custom_call" | custom-call | flops 402653184 | bytes 4194304 | tf_op jit(solution)/shard_map/basis_gram/pallas_call | solution.py:657
  17.1 2.9 %all-to-all-start = ((f32[32,4,128]{2,1,0:T(4,128)}), f32[32,4,128]{2,1,0:T(4,128)S(1)}, u32[]{:S(2)}, u32[]{:S(2)}) async-start(f32[32,4,128]{2,1,0:T(4,128)} %bitcast.9), calls=%async_computation | async-start | bytes 131072 | tf_op jit(solution)/shard_map/all_to_all | solution.py:45
  19.9 1.8 %collective-permute-start.8 = (f32[1,1024]{1,0:T(1,128)S(1)}, f32[1,1024]{1,0:T(1,128)S(1)}, u32[]{:S(2)}, u32[]{:S(2)}) collective-permute-start(f32[1,1024]{1,0:T(1,128)S(1)} %get-tuple-element.133), channel_id=1, source_target_pairs={{0,1},{1,0},{2,3},{3,2},{4,5},{5,4},{6,7},{7,6},{8,9},{9,8},{10,11... | collective-permute-start | bytes 12296 | tf_op jit(solution)/shard_map/ppermute | solution.py:21
  23.8 4.4 %basis_gram.3 = (bf16[128,8192]{1,0:T(8,128)(2,1)}, f32[256,128]{1,0:T(8,128)S(1)}, f32[256,128]{1,0:T(8,128)S(1)}) custom-call(s32[1,64]{1,0:T(1,128)S(1)} %get-tuple-element.113.refs_0_.refs_11_, bf16[256,64,128]{2,1,0:T(8,128)(2,1)} %bitcast.41, bf16[128,8192]{1,0:T(8,128)(2,1)} %get-tuple-element.151.refs_2_.refs_12_.refs_4_, ...), custom_call_target="tpu_custom_call" | custom-call | flops 671088640 | bytes 4194304 | tf_op jit(solution)/shard_map/basis_gram/pallas_call | solution.py:657
  33.3 3.5 %all-to-all-start.1 = ((f32[32,4,128]{2,1,0:T(4,128)}), f32[32,4,128]{2,1,0:T(4,128)S(1)}, u32[]{:S(2)}, u32[]{:S(2)}) async-start(f32[32,4,128]{2,1,0:T(4,128)} %bitcast.11), calls=%async_computation.1 | async-start | bytes 131072 | tf_op jit(solution)/shard_map/all_to_all | solution.py:45
  46.7 2.9 %all-to-all-start.2 = ((f32[32,8,128]{2,1,0:T(8,128)}), f32[32,8,128]{2,1,0:T(8,128)S(1)}, u32[]{:S(2)}, u32[]{:S(2)}) async-start(f32[32,8,128]{2,1,0:T(8,128)} %bitcast.13), calls=%async_computation.2 | async-start | bytes 262144 | tf_op jit(solution)/shard_map/all_to_all | solution.py:45
  49.7 1.8 %collective-permute-start.15 = (f32[16,16,128]{2,1,0:T(8,128)S(1)}, f32[16,16,128]{2,1,0:T(8,128)S(1)}, u32[]{:S(2)}, u32[]{:S(2)}) collective-permute-start(f32[16,16,128]{2,1,0:T(8,128)S(1)} %get-tuple-element.148), channel_id=1, source_target_pairs={{0,16},{16,0},{1,17},{17,1},{2,18},{18,2},{3,19},{19,3},{4,20},{20... | collective-permute-start | bytes 393224 | tf_op jit(solution)/shard_map/ppermute | solution.py:21
  51.7 1.8 %collective-permute-start.19 = (f32[1,1024]{1,0:T(1,128)S(1)}, f32[1,1024]{1,0:T(1,128)S(1)}, u32[]{:S(2)}, u32[]{:S(2)}) collective-permute-start(f32[1,1024]{1,0:T(1,128)S(1)} %get-tuple-element.160), channel_id=1, source_target_pairs={{0,1},{1,0},{2,3},{3,2},{4,5},{5,4},{6,7},{7,6},{8,9},{9,8},{10,11... | collective-permute-start | bytes 12296 | tf_op jit(solution)/shard_map/ppermute | solution.py:21
  60.7 4.5 %all-to-all-start.3 = ((f32[32,8,128]{2,1,0:T(8,128)}), f32[32,8,128]{2,1,0:T(8,128)S(1)}, u32[]{:S(2)}, u32[]{:S(2)}) async-start(f32[32,8,128]{2,1,0:T(8,128)} %bitcast.15), calls=%async_computation.3 | async-start | bytes 262144 | tf_op jit(solution)/shard_map/all_to_all | solution.py:45
  65.2 1.8 %collective-permute-start.21 = (f32[16,16,128]{2,1,0:T(8,128)S(1)}, f32[16,16,128]{2,1,0:T(8,128)S(1)}, u32[]{:S(2)}, u32[]{:S(2)}) collective-permute-start(f32[16,16,128]{2,1,0:T(8,128)S(1)} %get-tuple-element.164), channel_id=1, source_target_pairs={{0,16},{16,0},{1,17},{17,1},{2,18},{18,2},{3,19},{19,3},{4,20},{20... | collective-permute-start | bytes 393224 | tf_op jit(solution)/shard_map/ppermute | solution.py:21
  67.3 1.8 %collective-permute-start.24 = (f32[1,1024]{1,0:T(1,128)S(1)}, f32[1,1024]{1,0:T(1,128)S(1)}, u32[]{:S(2)}, u32[]{:S(2)}) collective-permute-start(f32[1,1024]{1,0:T(1,128)S(1)} %get-tuple-element.171), channel_id=1, source_target_pairs={{0,1},{1,0},{2,3},{3,2},{4,5},{5,4},{6,7},{7,6},{8,9},{9,8},{10,11... | collective-permute-start | bytes 12296 | tf_op jit(solution)/shard_map/ppermute | solution.py:21
  76.2 4.5 %all-to-all-start.4 = ((f32[32,8,128]{2,1,0:T(8,128)}), f32[32,8,128]{2,1,0:T(8,128)S(1)}, u32[]{:S(2)}, u32[]{:S(2)}) async-start(f32[32,8,128]{2,1,0:T(8,128)} %bitcast.17), calls=%async_computation.4 | async-start | bytes 262144 | tf_op jit(solution)/shard_map/all_to_all | solution.py:45
  80.8 1.8 %collective-permute-start.26 = (f32[16,16,128]{2,1,0:T(8,128)S(1)}, f32[16,16,128]{2,1,0:T(8,128)S(1)}, u32[]{:S(2)}, u32[]{:S(2)}) collective-permute-start(f32[16,16,128]{2,1,0:T(8,128)S(1)} %get-tuple-element.175), channel_id=1, source_target_pairs={{0,16},{16,0},{1,17},{17,1},{2,18},{18,2},{3,19},{19,3},{4,20},{20... | collective-permute-start | bytes 393224 | tf_op jit(solution)/shard_map/ppermute | solution.py:21
  82.9 1.8 %collective-permute-start.29 = (f32[1,1024]{1,0:T(1,128)S(1)}, f32[1,1024]{1,0:T(1,128)S(1)}, u32[]{:S(2)}, u32[]{:S(2)}) collective-permute-start(f32[1,1024]{1,0:T(1,128)S(1)} %get-tuple-element.183), channel_id=1, source_target_pairs={{0,1},{1,0},{2,3},{3,2},{4,5},{5,4},{6,7},{7,6},{8,9},{9,8},{10,11... | collective-permute-start | bytes 12296 | tf_op jit(solution)/shard_map/ppermute | solution.py:21
  91.8 4.8 %all-to-all-start.5 = ((f32[32,8,128]{2,1,0:T(8,128)}), f32[32,8,128]{2,1,0:T(8,128)S(1)}, u32[]{:S(2)}, u32[]{:S(2)}) async-start(f32[32,8,128]{2,1,0:T(8,128)} %bitcast.19), calls=%async_computation.5 | async-start | bytes 262144 | tf_op jit(solution)/shard_map/all_to_all | solution.py:45
  108.2 4.7 %all-to-all-start.6 = ((f32[32,4,128]{2,1,0:T(4,128)}), f32[32,4,128]{2,1,0:T(4,128)S(1)}, u32[]{:S(2)}, u32[]{:S(2)}) async-start(f32[32,4,128]{2,1,0:T(4,128)} %bitcast.21), calls=%async_computation.6 | async-start | bytes 131072 | tf_op jit(solution)/shard_map/all_to_all | solution.py:45
  113.0 1.8 %collective-permute-start.38 = (f32[4,16,128]{2,1,0:T(8,128)S(1)}, f32[4,16,128]{2,1,0:T(8,128)S(1)}, u32[]{:S(2)}, u32[]{:S(2)}) collective-permute-start(f32[4,16,128]{2,1,0:T(8,128)S(1)} %get-tuple-element.205), channel_id=1, source_target_pairs={{0,16},{4,8},{8,4},{12,28},{16,0},{20,24},{24,20},{28,12},{1,17},{... | collective-permute-start | bytes 98312 | tf_op jit(solution)/shard_map/ppermute | solution.py:41
  120.5 4.7 %update.13 = (f32[128,128]{1,0:T(8,128)S(1)}, f32[16,8192]{1,0:T(8,128)S(1)}) custom-call(f32[10,64,128]{2,1,0:T(8,128)S(1)} %get-tuple-element.123.refs_0_, f32[16,64,128]{2,1,0:T(8,128)S(1)} %get-tuple-element.201.refs_1_, f32[16,64,128]{2,1,0:T(8,128)S(1)} %get-tuple-element.198.refs_2_.refs_0_, s32[1,1024]{1,0:T(1,128)S(1)} %get-tuple-element.111.refs_2_.refs_3_, ...), custom_call_target="tpu_custom_call" | custom-call | tf_op jit(solution)/shard_map/update/pallas_call | solution.py:778
  125.2 10.1 %all_to_all.94 = f32[32,4,128]{2,1,0:T(4,128)S(1)} all-to-all(f32[32,4,128]{2,1,0:T(4,128)S(1)} %bitcast.38), channel_id=1, replica_groups=mesh['gx'=2,'gy'=4,'gz'=4] {'gx','gy','gz'}, dimensions={0} | all-to-all | bytes 131072 | tf_op jit(solution)/shard_map/all_to_all | solution.py:45
  136.0 2.6 %all-to-all-start.8 = ((f32[32,4,128]{2,1,0:T(4,128)}), f32[32,4,128]{2,1,0:T(4,128)S(1)}, u32[]{:S(2)}, u32[]{:S(2)}) async-start(f32[32,4,128]{2,1,0:T(4,128)} %tile.2), calls=%async_computation.8 | async-start | bytes 131072 | tf_op jit(solution)/shard_map/all_to_all | solution.py:45
  140.1 6.0 %all-to-all-done.8 = f32[32,4,128]{2,1,0:T(4,128)S(1)} async-done(((f32[32,4,128]{2,1,0:T(4,128)}), f32[32,4,128]{2,1,0:T(4,128)S(1)}, u32[]{:S(2)}, u32[]{:S(2)}) %all-to-all-start.8) | async-done | bytes 65568 | tf_op jit(solution)/shard_map/all_to_all | solution.py:45
  146.1 4.8 %finish.1 = (f32[16,64,128]{2,1,0:T(8,128)}, f32[16,256]{1,0:T(8,128)}, f32[16,256]{1,0:T(8,128)}, f32[16,64]{1,0:T(8,128)}) custom-call(f32[128,128]{1,0:T(8,128)S(1)} %bitcast.35, f32[16,8192]{1,0:T(8,128)S(1)} %get-tuple-element.211.flat_ref, f32[128,128]{1,0:T(8,128)S(1)} %get-tuple-element.212.refs_0_, f32[128,128]{1,0:T(8,128)S(1)} %get-tuple-element.213.refs_1_, ...), custom_call_target="tpu_custom_call" | custom-call | tf_op jit(solution)/shard_map/finish/pallas_call | solution.py:801
  (109 shorter events, 66.1 us)
Async XLA Ops:
  1.7 11.9 %collective-permute-start.4 = (f32[1,64]{1,0:T(1,128)S(1)}, f32[1,64]{1,0:T(1,128)S(1)}, u32[]{:S(2)}, u32[]{:S(2)}) collective-permute-start(f32[1,64]{1,0:T(1,128)S(1)} %get-tuple-element.117), channel_id=1, source_target_pairs={{0,16},{1,2},{2,1},{3,19},{16,0},{17,18},{18,17},{19,3},{4,20},{5,... | collective-permute-start | bytes 776 | tf_op jit(solution)/shard_map/ppermute | solution.py:41
  4.7 8.9 %collective-permute-start.3 = (f32[1,64]{1,0:T(1,128)S(1)}, f32[1,64]{1,0:T(1,128)S(1)}, u32[]{:S(2)}, u32[]{:S(2)}) collective-permute-start(f32[1,64]{1,0:T(1,128)S(1)} %get-tuple-element.117), channel_id=1, source_target_pairs={{0,1},{1,0},{2,3},{3,2},{4,5},{5,4},{6,7},{7,6},{8,9},{9,8},{10,11... | collective-permute-start | bytes 776 | tf_op jit(solution)/shard_map/ppermute | solution.py:21
  6.4 7.3 %collective-permute-start.2 = (f32[4,128]{1,0:T(4,128)S(1)}, f32[4,128]{1,0:T(4,128)S(1)}, u32[]{:S(2)}, u32[]{:S(2)}) collective-permute-start(f32[4,128]{1,0:T(4,128)S(1)} %get-tuple-element.116), channel_id=1, source_target_pairs={{0,16},{4,8},{8,4},{12,28},{16,0},{20,24},{24,20},{28,12},{1,17},{... | collective-permute-start | bytes 6152 | tf_op jit(solution)/shard_map/ppermute | solution.py:41
  15.2 14.1 %collective-permute-start.5 = (f32[16,16,128]{2,1,0:T(8,128)S(1)}, f32[16,16,128]{2,1,0:T(8,128)S(1)}, u32[]{:S(2)}, u32[]{:S(2)}) collective-permute-start(f32[16,16,128]{2,1,0:T(8,128)S(1)} %get-tuple-element.126), channel_id=1, source_target_pairs={{0,16},{16,0},{1,17},{17,1},{2,18},{18,2},{3,19},{19,3},{4,20},{20... | collective-permute-start | bytes 393224 | tf_op jit(solution)/shard_map/ppermute | solution.py:21
  17.1 12.8 %all-to-all-start = ((f32[32,4,128]{2,1,0:T(4,128)}), f32[32,4,128]{2,1,0:T(4,128)S(1)}, u32[]{:S(2)}, u32[]{:S(2)}) async-start(f32[32,4,128]{2,1,0:T(4,128)} %bitcast.9), calls=%async_computation | async-start | bytes 131072 | tf_op jit(solution)/shard_map/all_to_all | solution.py:45
  19.9 9.9 %collective-permute-start.8 = (f32[1,1024]{1,0:T(1,128)S(1)}, f32[1,1024]{1,0:T(1,128)S(1)}, u32[]{:S(2)}, u32[]{:S(2)}) collective-permute-start(f32[1,1024]{1,0:T(1,128)S(1)} %get-tuple-element.133), channel_id=1, source_target_pairs={{0,1},{1,0},{2,3},{3,2},{4,5},{5,4},{6,7},{7,6},{8,9},{9,8},{10,11... | collective-permute-start | bytes 12296 | tf_op jit(solution)/shard_map/ppermute | solution.py:21
  21.8 8.1 %collective-permute-start.9 = (f32[1,1024]{1,0:T(1,128)S(1)}, f32[1,1024]{1,0:T(1,128)S(1)}, u32[]{:S(2)}, u32[]{:S(2)}) collective-permute-start(f32[1,1024]{1,0:T(1,128)S(1)} %get-tuple-element.134), channel_id=1, source_target_pairs={{0,16},{1,2},{2,1},{3,19},{16,0},{17,18},{18,17},{19,3},{4,20},{5,... | collective-permute-start | bytes 12296 | tf_op jit(solution)/shard_map/ppermute | solution.py:41
  23.2 6.6 %collective-permute-start.7 = (f32[4,16,128]{2,1,0:T(8,128)S(1)}, f32[4,16,128]{2,1,0:T(8,128)S(1)}, u32[]{:S(2)}, u32[]{:S(2)}) collective-permute-start(f32[4,16,128]{2,1,0:T(8,128)S(1)} %get-tuple-element.132), channel_id=1, source_target_pairs={{0,16},{4,8},{8,4},{12,28},{16,0},{20,24},{24,20},{28,12},{1,17},{... | collective-permute-start | bytes 98312 | tf_op jit(solution)/shard_map/ppermute | solution.py:41
  28.2 17.2 %collective-permute-start.16 = (f32[256,128]{1,0:T(8,128)S(1)}, f32[256,128]{1,0:T(8,128)S(1)}, u32[]{:S(2)}, u32[]{:S(2)}) collective-permute-start(f32[256,128]{1,0:T(8,128)S(1)} %get-tuple-element.155), channel_id=1, source_target_pairs={{0,4},{4,0},{8,12},{12,8},{1,5},{5,1},{9,13},{13,9},{2,6},{6,2},{1... | collective-permute-start | bytes 393224 | tf_op jit(solution)/shard_map/ppermute | solution.py:21
  31.2 9.4 %collective-permute-start.10 = (f32[16,16,128]{2,1,0:T(8,128)S(1)}, f32[16,16,128]{2,1,0:T(8,128)S(1)}, u32[]{:S(2)}, u32[]{:S(2)}) collective-permute-start(f32[16,16,128]{2,1,0:T(8,128)S(1)} %get-tuple-element.137), channel_id=1, source_target_pairs={{0,16},{16,0},{1,17},{17,1},{2,18},{18,2},{3,19},{19,3},{4,20},{20... | collective-permute-start | bytes 393224 | tf_op jit(solution)/shard_map/ppermute | solution.py:21
  33.3 10.9 %all-to-all-start.1 = ((f32[32,4,128]{2,1,0:T(4,128)}), f32[32,4,128]{2,1,0:T(4,128)S(1)}, u32[]{:S(2)}, u32[]{:S(2)}) async-start(f32[32,4,128]{2,1,0:T(4,128)} %bitcast.11), calls=%async_computation.1 | async-start | bytes 131072 | tf_op jit(solution)/shard_map/all_to_all | solution.py:45
  36.8 6.7 %collective-permute-start.12 = (f32[4,16,128]{2,1,0:T(8,128)S(1)}, f32[4,16,128]{2,1,0:T(8,128)S(1)}, u32[]{:S(2)}, u32[]{:S(2)}) collective-permute-start(f32[4,16,128]{2,1,0:T(8,128)S(1)} %get-tuple-element.143), channel_id=1, source_target_pairs={{0,16},{4,8},{8,4},{12,28},{16,0},{20,24},{24,20},{28,12},{1,17},{... | collective-permute-start | bytes 98312 | tf_op jit(solution)/shard_map/ppermute | solution.py:41
  46.7 11.4 %all-to-all-start.2 = ((f32[32,8,128]{2,1,0:T(8,128)}), f32[32,8,128]{2,1,0:T(8,128)S(1)}, u32[]{:S(2)}, u32[]{:S(2)}) async-start(f32[32,8,128]{2,1,0:T(8,128)} %bitcast.13), calls=%async_computation.2 | async-start | bytes 262144 | tf_op jit(solution)/shard_map/all_to_all | solution.py:45
  49.7 6.8 %collective-permute-start.15 = (f32[16,16,128]{2,1,0:T(8,128)S(1)}, f32[16,16,128]{2,1,0:T(8,128)S(1)}, u32[]{:S(2)}, u32[]{:S(2)}) collective-permute-start(f32[16,16,128]{2,1,0:T(8,128)S(1)} %get-tuple-element.148), channel_id=1, source_target_pairs={{0,16},{16,0},{1,17},{17,1},{2,18},{18,2},{3,19},{19,3},{4,20},{20... | collective-permute-start | bytes 393224 | tf_op jit(solution)/shard_map/ppermute | solution.py:21
  60.7 13.0 %all-to-all-start.3 = ((f32[32,8,128]{2,1,0:T(8,128)}), f32[32,8,128]{2,1,0:T(8,128)S(1)}, u32[]{:S(2)}, u32[]{:S(2)}) async-start(f32[32,8,128]{2,1,0:T(8,128)} %bitcast.15), calls=%async_computation.3 | async-start | bytes 262144 | tf_op jit(solution)/shard_map/all_to_all | solution.py:45
  65.2 6.8 %collective-permute-start.21 = (f32[16,16,128]{2,1,0:T(8,128)S(1)}, f32[16,16,128]{2,1,0:T(8,128)S(1)}, u32[]{:S(2)}, u32[]{:S(2)}) collective-permute-start(f32[16,16,128]{2,1,0:T(8,128)S(1)} %get-tuple-element.164), channel_id=1, source_target_pairs={{0,16},{16,0},{1,17},{17,1},{2,18},{18,2},{3,19},{19,3},{4,20},{20... | collective-permute-start | bytes 393224 | tf_op jit(solution)/shard_map/ppermute | solution.py:21
  76.2 13.0 %all-to-all-start.4 = ((f32[32,8,128]{2,1,0:T(8,128)}), f32[32,8,128]{2,1,0:T(8,128)S(1)}, u32[]{:S(2)}, u32[]{:S(2)}) async-start(f32[32,8,128]{2,1,0:T(8,128)} %bitcast.17), calls=%async_computation.4 | async-start | bytes 262144 | tf_op jit(solution)/shard_map/all_to_all | solution.py:45
  80.8 6.8 %collective-permute-start.26 = (f32[16,16,128]{2,1,0:T(8,128)S(1)}, f32[16,16,128]{2,1,0:T(8,128)S(1)}, u32[]{:S(2)}, u32[]{:S(2)}) collective-permute-start(f32[16,16,128]{2,1,0:T(8,128)S(1)} %get-tuple-element.175), channel_id=1, source_target_pairs={{0,16},{16,0},{1,17},{17,1},{2,18},{18,2},{3,19},{19,3},{4,20},{20... | collective-permute-start | bytes 393224 | tf_op jit(solution)/shard_map/ppermute | solution.py:21
  91.8 13.0 %all-to-all-start.5 = ((f32[32,8,128]{2,1,0:T(8,128)}), f32[32,8,128]{2,1,0:T(8,128)S(1)}, u32[]{:S(2)}, u32[]{:S(2)}) async-start(f32[32,8,128]{2,1,0:T(8,128)} %bitcast.19), calls=%async_computation.5 | async-start | bytes 262144 | tf_op jit(solution)/shard_map/all_to_all | solution.py:45
  96.6 6.6 %collective-permute-start.31 = (f32[16,16,128]{2,1,0:T(8,128)S(1)}, f32[16,16,128]{2,1,0:T(8,128)S(1)}, u32[]{:S(2)}, u32[]{:S(2)}) collective-permute-start(f32[16,16,128]{2,1,0:T(8,128)S(1)} %get-tuple-element.187), channel_id=1, source_target_pairs={{0,16},{16,0},{1,17},{17,1},{2,18},{18,2},{3,19},{19,3},{4,20},{20... | collective-permute-start | bytes 393224 | tf_op jit(solution)/shard_map/ppermute | solution.py:21
  106.2 10.6 %collective-permute-start.36 = (f32[16,16,128]{2,1,0:T(8,128)S(1)}, f32[16,16,128]{2,1,0:T(8,128)S(1)}, u32[]{:S(2)}, u32[]{:S(2)}) collective-permute-start(f32[16,16,128]{2,1,0:T(8,128)S(1)} %get-tuple-element.199), channel_id=1, source_target_pairs={{0,16},{16,0},{1,17},{17,1},{2,18},{18,2},{3,19},{19,3},{4,20},{20... | collective-permute-start | bytes 393224 | tf_op jit(solution)/shard_map/ppermute | solution.py:21
  108.2 12.2 %all-to-all-start.6 = ((f32[32,4,128]{2,1,0:T(4,128)}), f32[32,4,128]{2,1,0:T(4,128)S(1)}, u32[]{:S(2)}, u32[]{:S(2)}) async-start(f32[32,4,128]{2,1,0:T(4,128)} %bitcast.21), calls=%async_computation.6 | async-start | bytes 131072 | tf_op jit(solution)/shard_map/all_to_all | solution.py:45
  113.0 6.9 %collective-permute-start.38 = (f32[4,16,128]{2,1,0:T(8,128)S(1)}, f32[4,16,128]{2,1,0:T(8,128)S(1)}, u32[]{:S(2)}, u32[]{:S(2)}) collective-permute-start(f32[4,16,128]{2,1,0:T(8,128)S(1)} %get-tuple-element.205), channel_id=1, source_target_pairs={{0,16},{4,8},{8,4},{12,28},{16,0},{20,24},{24,20},{28,12},{1,17},{... | collective-permute-start | bytes 98312 | tf_op jit(solution)/shard_map/ppermute | solution.py:41
  136.0 10.1 %all-to-all-start.8 = ((f32[32,4,128]{2,1,0:T(4,128)}), f32[32,4,128]{2,1,0:T(4,128)S(1)}, u32[]{:S(2)}, u32[]{:S(2)}) async-start(f32[32,4,128]{2,1,0:T(4,128)} %tile.2), calls=%async_computation.8 | async-start | bytes 131072 | tf_op jit(solution)/shard_map/all_to_all | solution.py:45
  (28 other events, 102.1 us)

commit v5 on v4

--- a/solution.py
+++ b/solution.py
@@ -487,6 +487,15 @@
     found = jnp.where(mask[None], found.reshape(columns, lines, wells), 0.0)
     at += columns
     sums_out[at : at + columns, :wells] = jnp.sum(found, axis=1)
+
+
+def share_kernel(devices, parts_ref, out_ref):
+    rows = parts_ref.shape[0] // devices
+    total = parts_ref[:rows, :]
+    for i in range(1, devices):
+        total = total + parts_ref[i * rows : (i + 1) * rows, :]
+    for i in range(devices):
+        out_ref[i * rows : (i + 1) * rows, :] = total
 
 
 def exact_dot(left, right, transposed=False):
@@ -793,8 +802,15 @@
             tables[group] = table
         residual, direction, *faces = outs
 
-    mine = exchange(sums).reshape(devices, per_device, LANES).sum(axis=0)
-    sums = exchange(jnp.tile(mine, (devices, 1)))
+    sums = pl.pallas_call(
+        functools.partial(share_kernel, devices),
+        out_shape=sums_type,
+        in_specs=[vmem],
+        out_specs=vmem,
+        compiler_params=params,
+        name="share_sums",
+    )(exchange(sums))
+    sums = exchange(sums)
 
     mine = [tables[group] for group in range(groups)]
     scale = math.sqrt(full_x * full_y * full_z)

time: 152 us -> 152 us (level)
  no operation moved by 1% of the time
where the time goes in v5:
time: 152 us; the launch traced here: 151 us
  starting transfers between devices  75 us (49%)
  Pallas kernels  40.8 us (27%)
  waiting for transfers between devices  23.3 us (15%)
  blocking collectives  10.1 us (7%)
  between operations  1.82 us (1%)
    all_to_all x8, starting transfers between devices, exchange(): return lax.all_to_all(value, AXES, split_axis=0, concat_axis=0, tiled=True)  30.4 us
    ppermute x27, starting transfers between devices, swap_even(): return lax.ppermute(value, axis, pairs)  26.3 us
    ppermute x16, starting transfers between devices, swap_odd(): return lax.ppermute(value, names, pairs)  18.2 us
    pallas_call x7, Pallas kernels, local(): pl.pallas_call(body, out_shape=out_types, in_specs=in_specs, out_specs=[v...  12.4 us
    all_to_all x8, waiting for transfers between devices, exchange(): return lax.all_to_all(value, AXES, split_axis=0, concat_axis=0, tiled=True)  11.1 us
    all_to_all x1, blocking collectives, exchange(): return lax.all_to_all(value, AXES, split_axis=0, concat_axis=0, tiled=True)  10.1 us
    ppermute x27, waiting for transfers between devices, swap_even(): return lax.ppermute(value, axis, pairs)  8.96 us
    pallas_call x7, Pallas kernels, gather(): pl.pallas_call(functools.partial(gather_kernel, dims, (extra, goes, parit...  8.57 us
  transfers between devices with their start and end apart: 51, of which 21 were waited for; matrix products, arithmetic and copies ran while one was open for 0% of the time, Pallas kernels for 15%

profile of v5, /device:TPU:0, one launch (start us, length us, event | category | flops | bytes accessed | tf_op | source)
XLA Modules:
  0.0 151.1 jit_solution(16572315561020335511)
XLA Ops:
  1.7 3.0 %collective-permute-start.4 = (f32[1,64]{1,0:T(1,128)S(1)}, f32[1,64]{1,0:T(1,128)S(1)}, u32[]{:S(2)}, u32[]{:S(2)}) collective-permute-start(f32[1,64]{1,0:T(1,128)S(1)} %get-tuple-element.117), channel_id=1, source_target_pairs={{0,16},{1,2},{2,1},{3,19},{16,0},{17,18},{18,17},{19,3},{4,20},{5,... | collective-permute-start | bytes 776 | tf_op jit(solution)/shard_map/ppermute | solution.py:41
  4.7 1.7 %collective-permute-start.3 = (f32[1,64]{1,0:T(1,128)S(1)}, f32[1,64]{1,0:T(1,128)S(1)}, u32[]{:S(2)}, u32[]{:S(2)}) collective-permute-start(f32[1,64]{1,0:T(1,128)S(1)} %get-tuple-element.117), channel_id=1, source_target_pairs={{0,1},{1,0},{2,3},{3,2},{4,5},{5,4},{6,7},{7,6},{8,9},{9,8},{10,11... | collective-permute-start | bytes 776 | tf_op jit(solution)/shard_map/ppermute | solution.py:21
  9.5 3.5 %basis_gram.2 = (bf16[128,8192]{1,0:T(8,128)(2,1)}, f32[128,128]{1,0:T(8,128)S(1)}, f32[128,64]{1,0:T(8,128)S(1)}) custom-call(s32[1,64]{1,0:T(1,128)S(1)} %get-tuple-element.113.refs_0_.refs_11_, bf16[256,64,128]{2,1,0:T(8,128)(2,1)} %bitcast.43), custom_call_target="tpu_custom_call" | custom-call | flops 402653184 | bytes 4194304 | tf_op jit(solution)/shard_map/basis_gram/pallas_call | solution.py:666
  17.1 2.9 %all-to-all-start = ((f32[32,4,128]{2,1,0:T(4,128)}), f32[32,4,128]{2,1,0:T(4,128)S(1)}, u32[]{:S(2)}, u32[]{:S(2)}) async-start(f32[32,4,128]{2,1,0:T(4,128)} %bitcast.9), calls=%async_computation | async-start | bytes 131072 | tf_op jit(solution)/shard_map/all_to_all | solution.py:45
  19.9 1.8 %collective-permute-start.8 = (f32[1,1024]{1,0:T(1,128)S(1)}, f32[1,1024]{1,0:T(1,128)S(1)}, u32[]{:S(2)}, u32[]{:S(2)}) collective-permute-start(f32[1,1024]{1,0:T(1,128)S(1)} %get-tuple-element.133), channel_id=1, source_target_pairs={{0,1},{1,0},{2,3},{3,2},{4,5},{5,4},{6,7},{7,6},{8,9},{9,8},{10,11... | collective-permute-start | bytes 12296 | tf_op jit(solution)/shard_map/ppermute | solution.py:21
  23.8 4.4 %basis_gram.3 = (bf16[128,8192]{1,0:T(8,128)(2,1)}, f32[256,128]{1,0:T(8,128)S(1)}, f32[256,128]{1,0:T(8,128)S(1)}) custom-call(s32[1,64]{1,0:T(1,128)S(1)} %get-tuple-element.113.refs_0_.refs_11_, bf16[256,64,128]{2,1,0:T(8,128)(2,1)} %bitcast.44, bf16[128,8192]{1,0:T(8,128)(2,1)} %get-tuple-element.151.refs_2_.refs_12_.refs_4_, ...), custom_call_target="tpu_custom_call" | custom-call | flops 671088640 | bytes 4194304 | tf_op jit(solution)/shard_map/basis_gram/pallas_call | solution.py:666
  33.3 3.5 %all-to-all-start.1 = ((f32[32,4,128]{2,1,0:T(4,128)}), f32[32,4,128]{2,1,0:T(4,128)S(1)}, u32[]{:S(2)}, u32[]{:S(2)}) async-start(f32[32,4,128]{2,1,0:T(4,128)} %bitcast.11), calls=%async_computation.1 | async-start | bytes 131072 | tf_op jit(solution)/shard_map/all_to_all | solution.py:45
  46.7 2.9 %all-to-all-start.2 = ((f32[32,8,128]{2,1,0:T(8,128)}), f32[32,8,128]{2,1,0:T(8,128)S(1)}, u32[]{:S(2)}, u32[]{:S(2)}) async-start(f32[32,8,128]{2,1,0:T(8,128)} %bitcast.13), calls=%async_computation.2 | async-start | bytes 262144 | tf_op jit(solution)/shard_map/all_to_all | solution.py:45
  49.7 1.8 %collective-permute-start.15 = (f32[16,16,128]{2,1,0:T(8,128)S(1)}, f32[16,16,128]{2,1,0:T(8,128)S(1)}, u32[]{:S(2)}, u32[]{:S(2)}) collective-permute-start(f32[16,16,128]{2,1,0:T(8,128)S(1)} %get-tuple-element.148), channel_id=1, source_target_pairs={{0,16},{16,0},{1,17},{17,1},{2,18},{18,2},{3,19},{19,3},{4,20},{20... | collective-permute-start | bytes 393224 | tf_op jit(solution)/shard_map/ppermute | solution.py:21
  51.7 1.8 %collective-permute-start.19 = (f32[1,1024]{1,0:T(1,128)S(1)}, f32[1,1024]{1,0:T(1,128)S(1)}, u32[]{:S(2)}, u32[]{:S(2)}) collective-permute-start(f32[1,1024]{1,0:T(1,128)S(1)} %get-tuple-element.160), channel_id=1, source_target_pairs={{0,1},{1,0},{2,3},{3,2},{4,5},{5,4},{6,7},{7,6},{8,9},{9,8},{10,11... | collective-permute-start | bytes 12296 | tf_op jit(solution)/shard_map/ppermute | solution.py:21
  60.7 4.5 %all-to-all-start.3 = ((f32[32,8,128]{2,1,0:T(8,128)}), f32[32,8,128]{2,1,0:T(8,128)S(1)}, u32[]{:S(2)}, u32[]{:S(2)}) async-start(f32[32,8,128]{2,1,0:T(8,128)} %bitcast.15), calls=%async_computation.3 | async-start | bytes 262144 | tf_op jit(solution)/shard_map/all_to_all | solution.py:45
  65.2 1.8 %collective-permute-start.21 = (f32[16,16,128]{2,1,0:T(8,128)S(1)}, f32[16,16,128]{2,1,0:T(8,128)S(1)}, u32[]{:S(2)}, u32[]{:S(2)}) collective-permute-start(f32[16,16,128]{2,1,0:T(8,128)S(1)} %get-tuple-element.164), channel_id=1, source_target_pairs={{0,16},{16,0},{1,17},{17,1},{2,18},{18,2},{3,19},{19,3},{4,20},{20... | collective-permute-start | bytes 393224 | tf_op jit(solution)/shard_map/ppermute | solution.py:21
  67.3 1.8 %collective-permute-start.24 = (f32[1,1024]{1,0:T(1,128)S(1)}, f32[1,1024]{1,0:T(1,128)S(1)}, u32[]{:S(2)}, u32[]{:S(2)}) collective-permute-start(f32[1,1024]{1,0:T(1,128)S(1)} %get-tuple-element.171), channel_id=1, source_target_pairs={{0,1},{1,0},{2,3},{3,2},{4,5},{5,4},{6,7},{7,6},{8,9},{9,8},{10,11... | collective-permute-start | bytes 12296 | tf_op jit(solution)/shard_map/ppermute | solution.py:21
  76.2 4.5 %all-to-all-start.4 = ((f32[32,8,128]{2,1,0:T(8,128)}), f32[32,8,128]{2,1,0:T(8,128)S(1)}, u32[]{:S(2)}, u32[]{:S(2)}) async-start(f32[32,8,128]{2,1,0:T(8,128)} %bitcast.17), calls=%async_computation.4 | async-start | bytes 262144 | tf_op jit(solution)/shard_map/all_to_all | solution.py:45
  80.8 1.8 %collective-permute-start.26 = (f32[16,16,128]{2,1,0:T(8,128)S(1)}, f32[16,16,128]{2,1,0:T(8,128)S(1)}, u32[]{:S(2)}, u32[]{:S(2)}) collective-permute-start(f32[16,16,128]{2,1,0:T(8,128)S(1)} %get-tuple-element.175), channel_id=1, source_target_pairs={{0,16},{16,0},{1,17},{17,1},{2,18},{18,2},{3,19},{19,3},{4,20},{20... | collective-permute-start | bytes 393224 | tf_op jit(solution)/shard_map/ppermute | solution.py:21
  82.9 1.8 %collective-permute-start.29 = (f32[1,1024]{1,0:T(1,128)S(1)}, f32[1,1024]{1,0:T(1,128)S(1)}, u32[]{:S(2)}, u32[]{:S(2)}) collective-permute-start(f32[1,1024]{1,0:T(1,128)S(1)} %get-tuple-element.183), channel_id=1, source_target_pairs={{0,1},{1,0},{2,3},{3,2},{4,5},{5,4},{6,7},{7,6},{8,9},{9,8},{10,11... | collective-permute-start | bytes 12296 | tf_op jit(solution)/shard_map/ppermute | solution.py:21
  91.8 4.8 %all-to-all-start.5 = ((f32[32,8,128]{2,1,0:T(8,128)}), f32[32,8,128]{2,1,0:T(8,128)S(1)}, u32[]{:S(2)}, u32[]{:S(2)}) async-start(f32[32,8,128]{2,1,0:T(8,128)} %bitcast.19), calls=%async_computation.5 | async-start | bytes 262144 | tf_op jit(solution)/shard_map/all_to_all | solution.py:45
  108.2 4.7 %all-to-all-start.6 = ((f32[32,4,128]{2,1,0:T(4,128)}), f32[32,4,128]{2,1,0:T(4,128)S(1)}, u32[]{:S(2)}, u32[]{:S(2)}) async-start(f32[32,4,128]{2,1,0:T(4,128)} %bitcast.21), calls=%async_computation.6 | async-start | bytes 131072 | tf_op jit(solution)/shard_map/all_to_all | solution.py:45
  113.0 1.8 %collective-permute-start.38 = (f32[4,16,128]{2,1,0:T(8,128)S(1)}, f32[4,16,128]{2,1,0:T(8,128)S(1)}, u32[]{:S(2)}, u32[]{:S(2)}) collective-permute-start(f32[4,16,128]{2,1,0:T(8,128)S(1)} %get-tuple-element.205), channel_id=1, source_target_pairs={{0,16},{4,8},{8,4},{12,28},{16,0},{20,24},{24,20},{28,12},{1,17},{... | collective-permute-start | bytes 98312 | tf_op jit(solution)/shard_map/ppermute | solution.py:41
  120.5 4.7 %update.13 = (f32[128,128]{1,0:T(8,128)S(1)}, f32[16,8192]{1,0:T(8,128)S(1)}) custom-call(f32[10,64,128]{2,1,0:T(8,128)S(1)} %get-tuple-element.123.refs_0_, f32[16,64,128]{2,1,0:T(8,128)S(1)} %get-tuple-element.201.refs_1_, f32[16,64,128]{2,1,0:T(8,128)S(1)} %get-tuple-element.198.refs_2_.refs_0_, s32[1,1024]{1,0:T(1,128)S(1)} %get-tuple-element.111.refs_2_.refs_3_, ...), custom_call_target="tpu_custom_call" | custom-call | tf_op jit(solution)/shard_map/update/pallas_call | solution.py:787
  125.2 10.1 %all_to_all.99 = f32[32,4,128]{2,1,0:T(4,128)S(1)} all-to-all(f32[32,4,128]{2,1,0:T(4,128)S(1)} %bitcast.41), channel_id=1, replica_groups=mesh['gx'=2,'gy'=4,'gz'=4] {'gx','gy','gz'}, dimensions={0} | all-to-all | bytes 131072 | tf_op jit(solution)/shard_map/all_to_all | solution.py:45
  136.0 2.6 %all-to-all-start.8 = ((f32[32,4,128]{2,1,0:T(4,128)}), f32[32,4,128]{2,1,0:T(4,128)S(1)}, u32[]{:S(2)}, u32[]{:S(2)}) async-start(f32[32,4,128]{2,1,0:T(4,128)} %bitcast.25), calls=%async_computation.8 | async-start | bytes 131072 | tf_op jit(solution)/shard_map/all_to_all | solution.py:45
  140.0 6.0 %all-to-all-done.8 = f32[32,4,128]{2,1,0:T(4,128)S(1)} async-done(((f32[32,4,128]{2,1,0:T(4,128)}), f32[32,4,128]{2,1,0:T(4,128)S(1)}, u32[]{:S(2)}, u32[]{:S(2)}) %all-to-all-start.8) | async-done | bytes 65568 | tf_op jit(solution)/shard_map/all_to_all | solution.py:45
  146.1 4.8 %finish.1 = (f32[16,64,128]{2,1,0:T(8,128)}, f32[16,256]{1,0:T(8,128)}, f32[16,256]{1,0:T(8,128)}, f32[16,64]{1,0:T(8,128)}) custom-call(f32[128,128]{1,0:T(8,128)S(1)} %bitcast.37, f32[16,8192]{1,0:T(8,128)S(1)} %get-tuple-element.211.flat_ref, f32[128,128]{1,0:T(8,128)S(1)} %get-tuple-element.212.refs_0_, f32[128,128]{1,0:T(8,128)S(1)} %get-tuple-element.213.refs_1_, ...), custom_call_target="tpu_custom_call" | custom-call | tf_op jit(solution)/shard_map/finish/pallas_call | solution.py:817
  (108 shorter events, 66.1 us)
Async XLA Ops:
  1.7 11.9 %collective-permute-start.4 = (f32[1,64]{1,0:T(1,128)S(1)}, f32[1,64]{1,0:T(1,128)S(1)}, u32[]{:S(2)}, u32[]{:S(2)}) collective-permute-start(f32[1,64]{1,0:T(1,128)S(1)} %get-tuple-element.117), channel_id=1, source_target_pairs={{0,16},{1,2},{2,1},{3,19},{16,0},{17,18},{18,17},{19,3},{4,20},{5,... | collective-permute-start | bytes 776 | tf_op jit(solution)/shard_map/ppermute | solution.py:41
  4.7 8.9 %collective-permute-start.3 = (f32[1,64]{1,0:T(1,128)S(1)}, f32[1,64]{1,0:T(1,128)S(1)}, u32[]{:S(2)}, u32[]{:S(2)}) collective-permute-start(f32[1,64]{1,0:T(1,128)S(1)} %get-tuple-element.117), channel_id=1, source_target_pairs={{0,1},{1,0},{2,3},{3,2},{4,5},{5,4},{6,7},{7,6},{8,9},{9,8},{10,11... | collective-permute-start | bytes 776 | tf_op jit(solution)/shard_map/ppermute | solution.py:21
  6.4 7.3 %collective-permute-start.2 = (f32[4,128]{1,0:T(4,128)S(1)}, f32[4,128]{1,0:T(4,128)S(1)}, u32[]{:S(2)}, u32[]{:S(2)}) collective-permute-start(f32[4,128]{1,0:T(4,128)S(1)} %get-tuple-element.116), channel_id=1, source_target_pairs={{0,16},{4,8},{8,4},{12,28},{16,0},{20,24},{24,20},{28,12},{1,17},{... | collective-permute-start | bytes 6152 | tf_op jit(solution)/shard_map/ppermute | solution.py:41
  15.2 14.1 %collective-permute-start.5 = (f32[16,16,128]{2,1,0:T(8,128)S(1)}, f32[16,16,128]{2,1,0:T(8,128)S(1)}, u32[]{:S(2)}, u32[]{:S(2)}) collective-permute-start(f32[16,16,128]{2,1,0:T(8,128)S(1)} %get-tuple-element.126), channel_id=1, source_target_pairs={{0,16},{16,0},{1,17},{17,1},{2,18},{18,2},{3,19},{19,3},{4,20},{20... | collective-permute-start | bytes 393224 | tf_op jit(solution)/shard_map/ppermute | solution.py:21
  17.1 12.8 %all-to-all-start = ((f32[32,4,128]{2,1,0:T(4,128)}), f32[32,4,128]{2,1,0:T(4,128)S(1)}, u32[]{:S(2)}, u32[]{:S(2)}) async-start(f32[32,4,128]{2,1,0:T(4,128)} %bitcast.9), calls=%async_computation | async-start | bytes 131072 | tf_op jit(solution)/shard_map/all_to_all | solution.py:45
  19.9 9.9 %collective-permute-start.8 = (f32[1,1024]{1,0:T(1,128)S(1)}, f32[1,1024]{1,0:T(1,128)S(1)}, u32[]{:S(2)}, u32[]{:S(2)}) collective-permute-start(f32[1,1024]{1,0:T(1,128)S(1)} %get-tuple-element.133), channel_id=1, source_target_pairs={{0,1},{1,0},{2,3},{3,2},{4,5},{5,4},{6,7},{7,6},{8,9},{9,8},{10,11... | collective-permute-start | bytes 12296 | tf_op jit(solution)/shard_map/ppermute | solution.py:21
  21.8 8.1 %collective-permute-start.9 = (f32[1,1024]{1,0:T(1,128)S(1)}, f32[1,1024]{1,0:T(1,128)S(1)}, u32[]{:S(2)}, u32[]{:S(2)}) collective-permute-start(f32[1,1024]{1,0:T(1,128)S(1)} %get-tuple-element.134), channel_id=1, source_target_pairs={{0,16},{1,2},{2,1},{3,19},{16,0},{17,18},{18,17},{19,3},{4,20},{5,... | collective-permute-start | bytes 12296 | tf_op jit(solution)/shard_map/ppermute | solution.py:41
  23.2 6.6 %collective-permute-start.7 = (f32[4,16,128]{2,1,0:T(8,128)S(1)}, f32[4,16,128]{2,1,0:T(8,128)S(1)}, u32[]{:S(2)}, u32[]{:S(2)}) collective-permute-start(f32[4,16,128]{2,1,0:T(8,128)S(1)} %get-tuple-element.132), channel_id=1, source_target_pairs={{0,16},{4,8},{8,4},{12,28},{16,0},{20,24},{24,20},{28,12},{1,17},{... | collective-permute-start | bytes 98312 | tf_op jit(solution)/shard_map/ppermute | solution.py:41
  28.2 17.2 %collective-permute-start.16 = (f32[256,128]{1,0:T(8,128)S(1)}, f32[256,128]{1,0:T(8,128)S(1)}, u32[]{:S(2)}, u32[]{:S(2)}) collective-permute-start(f32[256,128]{1,0:T(8,128)S(1)} %get-tuple-element.155), channel_id=1, source_target_pairs={{0,4},{4,0},{8,12},{12,8},{1,5},{5,1},{9,13},{13,9},{2,6},{6,2},{1... | collective-permute-start | bytes 393224 | tf_op jit(solution)/shard_map/ppermute | solution.py:21
  31.2 9.4 %collective-permute-start.10 = (f32[16,16,128]{2,1,0:T(8,128)S(1)}, f32[16,16,128]{2,1,0:T(8,128)S(1)}, u32[]{:S(2)}, u32[]{:S(2)}) collective-permute-start(f32[16,16,128]{2,1,0:T(8,128)S(1)} %get-tuple-element.137), channel_id=1, source_target_pairs={{0,16},{16,0},{1,17},{17,1},{2,18},{18,2},{3,19},{19,3},{4,20},{20... | collective-permute-start | bytes 393224 | tf_op jit(solution)/shard_map/ppermute | solution.py:21
  33.3 10.9 %all-to-all-start.1 = ((f32[32,4,128]{2,1,0:T(4,128)}), f32[32,4,128]{2,1,0:T(4,128)S(1)}, u32[]{:S(2)}, u32[]{:S(2)}) async-start(f32[32,4,128]{2,1,0:T(4,128)} %bitcast.11), calls=%async_computation.1 | async-start | bytes 131072 | tf_op jit(solution)/shard_map/all_to_all | solution.py:45
  36.8 6.7 %collective-permute-start.12 = (f32[4,16,128]{2,1,0:T(8,128)S(1)}, f32[4,16,128]{2,1,0:T(8,128)S(1)}, u32[]{:S(2)}, u32[]{:S(2)}) collective-permute-start(f32[4,16,128]{2,1,0:T(8,128)S(1)} %get-tuple-element.143), channel_id=1, source_target_pairs={{0,16},{4,8},{8,4},{12,28},{16,0},{20,24},{24,20},{28,12},{1,17},{... | collective-permute-start | bytes 98312 | tf_op jit(solution)/shard_map/ppermute | solution.py:41
  46.7 11.4 %all-to-all-start.2 = ((f32[32,8,128]{2,1,0:T(8,128)}), f32[32,8,128]{2,1,0:T(8,128)S(1)}, u32[]{:S(2)}, u32[]{:S(2)}) async-start(f32[32,8,128]{2,1,0:T(8,128)} %bitcast.13), calls=%async_computation.2 | async-start | bytes 262144 | tf_op jit(solution)/shard_map/all_to_all | solution.py:45
  49.7 6.8 %collective-permute-start.15 = (f32[16,16,128]{2,1,0:T(8,128)S(1)}, f32[16,16,128]{2,1,0:T(8,128)S(1)}, u32[]{:S(2)}, u32[]{:S(2)}) collective-permute-start(f32[16,16,128]{2,1,0:T(8,128)S(1)} %get-tuple-element.148), channel_id=1, source_target_pairs={{0,16},{16,0},{1,17},{17,1},{2,18},{18,2},{3,19},{19,3},{4,20},{20... | collective-permute-start | bytes 393224 | tf_op jit(solution)/shard_map/ppermute | solution.py:21
  60.7 13.0 %all-to-all-start.3 = ((f32[32,8,128]{2,1,0:T(8,128)}), f32[32,8,128]{2,1,0:T(8,128)S(1)}, u32[]{:S(2)}, u32[]{:S(2)}) async-start(f32[32,8,128]{2,1,0:T(8,128)} %bitcast.15), calls=%async_computation.3 | async-start | bytes 262144 | tf_op jit(solution)/shard_map/all_to_all | solution.py:45
  65.2 6.8 %collective-permute-start.21 = (f32[16,16,128]{2,1,0:T(8,128)S(1)}, f32[16,16,128]{2,1,0:T(8,128)S(1)}, u32[]{:S(2)}, u32[]{:S(2)}) collective-permute-start(f32[16,16,128]{2,1,0:T(8,128)S(1)} %get-tuple-element.164), channel_id=1, source_target_pairs={{0,16},{16,0},{1,17},{17,1},{2,18},{18,2},{3,19},{19,3},{4,20},{20... | collective-permute-start | bytes 393224 | tf_op jit(solution)/shard_map/ppermute | solution.py:21
  76.2 13.0 %all-to-all-start.4 = ((f32[32,8,128]{2,1,0:T(8,128)}), f32[32,8,128]{2,1,0:T(8,128)S(1)}, u32[]{:S(2)}, u32[]{:S(2)}) async-start(f32[32,8,128]{2,1,0:T(8,128)} %bitcast.17), calls=%async_computation.4 | async-start | bytes 262144 | tf_op jit(solution)/shard_map/all_to_all | solution.py:45
  80.8 6.8 %collective-permute-start.26 = (f32[16,16,128]{2,1,0:T(8,128)S(1)}, f32[16,16,128]{2,1,0:T(8,128)S(1)}, u32[]{:S(2)}, u32[]{:S(2)}) collective-permute-start(f32[16,16,128]{2,1,0:T(8,128)S(1)} %get-tuple-element.175), channel_id=1, source_target_pairs={{0,16},{16,0},{1,17},{17,1},{2,18},{18,2},{3,19},{19,3},{4,20},{20... | collective-permute-start | bytes 393224 | tf_op jit(solution)/shard_map/ppermute | solution.py:21
  91.8 13.0 %all-to-all-start.5 = ((f32[32,8,128]{2,1,0:T(8,128)}), f32[32,8,128]{2,1,0:T(8,128)S(1)}, u32[]{:S(2)}, u32[]{:S(2)}) async-start(f32[32,8,128]{2,1,0:T(8,128)} %bitcast.19), calls=%async_computation.5 | async-start | bytes 262144 | tf_op jit(solution)/shard_map/all_to_all | solution.py:45
  96.6 6.6 %collective-permute-start.31 = (f32[16,16,128]{2,1,0:T(8,128)S(1)}, f32[16,16,128]{2,1,0:T(8,128)S(1)}, u32[]{:S(2)}, u32[]{:S(2)}) collective-permute-start(f32[16,16,128]{2,1,0:T(8,128)S(1)} %get-tuple-element.187), channel_id=1, source_target_pairs={{0,16},{16,0},{1,17},{17,1},{2,18},{18,2},{3,19},{19,3},{4,20},{20... | collective-permute-start | bytes 393224 | tf_op jit(solution)/shard_map/ppermute | solution.py:21
  106.2 10.6 %collective-permute-start.36 = (f32[16,16,128]{2,1,0:T(8,128)S(1)}, f32[16,16,128]{2,1,0:T(8,128)S(1)}, u32[]{:S(2)}, u32[]{:S(2)}) collective-permute-start(f32[16,16,128]{2,1,0:T(8,128)S(1)} %get-tuple-element.199), channel_id=1, source_target_pairs={{0,16},{16,0},{1,17},{17,1},{2,18},{18,2},{3,19},{19,3},{4,20},{20... | collective-permute-start | bytes 393224 | tf_op jit(solution)/shard_map/ppermute | solution.py:21
  108.2 12.2 %all-to-all-start.6 = ((f32[32,4,128]{2,1,0:T(4,128)}), f32[32,4,128]{2,1,0:T(4,128)S(1)}, u32[]{:S(2)}, u32[]{:S(2)}) async-start(f32[32,4,128]{2,1,0:T(4,128)} %bitcast.21), calls=%async_computation.6 | async-start | bytes 131072 | tf_op jit(solution)/shard_map/all_to_all | solution.py:45
  113.0 6.9 %collective-permute-start.38 = (f32[4,16,128]{2,1,0:T(8,128)S(1)}, f32[4,16,128]{2,1,0:T(8,128)S(1)}, u32[]{:S(2)}, u32[]{:S(2)}) collective-permute-start(f32[4,16,128]{2,1,0:T(8,128)S(1)} %get-tuple-element.205), channel_id=1, source_target_pairs={{0,16},{4,8},{8,4},{12,28},{16,0},{20,24},{24,20},{28,12},{1,17},{... | collective-permute-start | bytes 98312 | tf_op jit(solution)/shard_map/ppermute | solution.py:41
  136.0 10.1 %all-to-all-start.8 = ((f32[32,4,128]{2,1,0:T(4,128)}), f32[32,4,128]{2,1,0:T(4,128)S(1)}, u32[]{:S(2)}, u32[]{:S(2)}) async-start(f32[32,4,128]{2,1,0:T(4,128)} %bitcast.25), calls=%async_computation.8 | async-start | bytes 131072 | tf_op jit(solution)/shard_map/all_to_all | solution.py:45
  (28 other events, 102.1 us)
